TPU v7x, 512 devices: a whole 4x8x8 slice. The times are simulated.
512 devices in a mesh: section: 16 (over y_lo, x, core), dp: 32 (over y_hi, z).
Axes of the slice: x: 4, y: 8 (y_hi: 4, y_lo: 2; y = y_hi * 2 + y_lo), z: 8, core: 2. Of those that a mesh axis runs over, the one named last changes fastest.
Arguments:
- inputs: bfloat16 [4, 1024, 2560], P(None, 'dp'), may hold values from -6 to 6
- cotangent: bfloat16 [4, 1024, 2560], P(None, 'dp'), may hold values from -4.2 to 4.2
- weight: bfloat16 [16, 2560, 2560], P('section', 'dp'), may hold values from -1 to 1
- gain: float32 [16, 2560], P('section'), may hold values from 0.1 to 1.9
- momentum: float32 [16, 32, 2560], P('section', 'dp'), may hold values from -6 to 6
- prev_grads: float32 [16, 32, 32, 2560], P('section', 'dp'), may hold values from -6 to 6
Outputs:
- input_grads: bfloat16 [16, 4, 1024, 2560], P('section', None, 'dp')
- gain_grads: float32 [16, 32, 2560], P('section', 'dp')
- new_momentum: float32 [16, 32, 2560], P('section', 'dp')
All inputs are finite; a program needn't handle non-finite values.
Results may differ from a plain program's by a relative error of at most 0.015.
Values may be sent and summed in bfloat16 or wider, within the bound.
No kernel may reach another device: no remote copies, remote signals or barrier semaphores. Data moves between devices by JAX's collectives and lax.ppermute only.
A program may use at most 64 MiB of HBM per device.

v0:
```python
import jax
import jax.numpy as jnp
from jax import lax
from jax.sharding import PartitionSpec as P


def shifted(array, axis, by):
    length = lax.axis_size(axis)
    pairs = [(i, i + by) for i in range(length) if 0 <= i + by < length]
    return lax.ppermute(array, axis, pairs)


def normalize(acts):
    values = acts.astype(jnp.float32)
    center = values - jnp.mean(values, axis=-1, keepdims=True)
    variance = jnp.mean(center * center, axis=-1, keepdims=True)
    inverse = 1.0 / jnp.sqrt(variance + 1e-05)
    return (center * inverse, inverse)


def per_device(inputs, cotangent, weight, gain, momentum, prev_grads):
    sections = lax.axis_size("section")
    section_index = lax.axis_index("section")
    batches = inputs.shape[0]
    rows = inputs.shape[1]
    width = inputs.shape[2]
    gain_row = gain[0]
    splits = 1
    count = batches * splits
    height = rows // splits
    ticks = sections + count - 1
    forward_weight = lax.all_gather(weight[0], "dp", axis=0, tiled=True)

    def forward_run(block):
        normed, inverse = normalize(block)
        scaled_in = (normed * gain_row).astype(jnp.bfloat16)
        projected = jnp.dot(scaled_in, forward_weight, preferred_element_type=jnp.float32)
        return (block.astype(jnp.float32) + projected).astype(jnp.bfloat16)

    def forward_skip(block):
        return jnp.zeros_like(block)

    def forward_tick(tick, carry):
        received, stash = carry
        position = tick - section_index
        active = jnp.logical_and(position >= 0, position < count)
        slot = jnp.clip(position, 0, count - 1)
        fresh = lax.dynamic_index_in_dim(inputs, slot, 0, keepdims=False)
        block = jnp.where(section_index == 0, fresh, received)
        output = lax.cond(active, forward_run, forward_skip, block)
        previous = lax.dynamic_index_in_dim(stash, slot, 0, keepdims=False)
        stash = lax.dynamic_update_index_in_dim(stash, jnp.where(active, block, previous), slot, 0)
        received = shifted(output, "section", 1)
        return (received, stash)

    empty = jnp.zeros((height, width), jnp.bfloat16)
    start_stash = jnp.zeros((count, height, width), jnp.bfloat16)
    unused, stash = lax.fori_loop(0, ticks, forward_tick, (empty, start_stash))

    def backward_run(operands):
        incoming, saved = operands
        normed, inverse = normalize(saved)
        back_proj = lax.dot_general(
            incoming, forward_weight, (((1,), (1,)), ((), ())), preferred_element_type=jnp.float32
        )
        scaled = back_proj * gain_row
        mean_one = jnp.mean(scaled, axis=-1, keepdims=True)
        mean_two = jnp.mean(scaled * normed, axis=-1, keepdims=True)
        norm_grad = inverse * (scaled - mean_one - normed * mean_two)
        outgoing = (incoming.astype(jnp.float32) + norm_grad).astype(jnp.bfloat16)
        return (outgoing, jnp.sum(back_proj * normed, axis=0))

    def backward_skip(operands):
        return (jnp.zeros_like(operands[0]), jnp.zeros((width,), jnp.float32))

    def backward_tick(tick, carry):
        received, collected, gain_total = carry
        position = tick - (sections - 1 - section_index)
        active = jnp.logical_and(position >= 0, position < count)
        slot = jnp.clip(position, 0, count - 1)
        fresh = lax.dynamic_index_in_dim(cotangent, slot, 0, keepdims=False)
        incoming = jnp.where(section_index == sections - 1, fresh, received)
        saved = lax.dynamic_index_in_dim(stash, slot, 0, keepdims=False)
        outgoing, gain_part = lax.cond(active, backward_run, backward_skip, (incoming, saved))
        previous = lax.dynamic_index_in_dim(collected, slot, 0, keepdims=False)
        collected = lax.dynamic_update_index_in_dim(
            collected, jnp.where(active, outgoing, previous), slot, 0
        )
        received = shifted(outgoing, "section", -1)
        return (received, collected, gain_total + gain_part)

    start_grads = jnp.zeros((count, height, width), jnp.bfloat16)
    start_gain = jnp.zeros((width,), jnp.float32)
    unused, collected, gain_total = lax.fori_loop(
        0, ticks, backward_tick, (empty, start_grads, start_gain)
    )
    input_grads = collected.reshape(1, batches, rows, width)
    gain_grads = gain_total.reshape(1, 1, width)
    local_bucket = prev_grads[0, 0]
    owned = momentum.shape[1]
    whole = lax.psum(local_bucket.astype(jnp.bfloat16), "dp").astype(jnp.float32)
    summed = lax.dynamic_slice_in_dim(whole, lax.axis_index("dp") * owned, owned, 0)
    new_momentum = 0.9 * momentum + (summed / lax.axis_size("dp"))[None]
    return (input_grads, gain_grads, new_momentum)


def solution(mesh):
    in_specs = (
        P(None, "dp", None),
        P(None, "dp", None),
        P("section", "dp", None),
        P("section", None),
        P("section", "dp", None),
        P("section", "dp", None, None),
    )
    out_specs = (P("section", None, "dp", None), P("section", "dp", None), P("section", "dp", None))
    return jax.shard_map(
        per_device, mesh=mesh, in_specs=in_specs, out_specs=out_specs, check_vma=False
    )
```

profile of v0, /device:TPU:1, one launch (start us, length us, event | category | flops | bytes accessed | tf_op | source)
XLA Modules:
  0.0 1061.2 jit_solution(4656035352061871559)
XLA Ops:
  9.7 285.7 %all-reduce.2.cloned.1.call-done = bf16[32,2560]{1,0:T(8,128)(2,1)} async-done(((bf16[32,2560]{1,0:T(8,128)(2,1)}), bf16[32,2560]{1,0:T(8,128)(2,1)}) %all-reduce.2.cloned.1.call-update) | async-done | bytes 163856 | tf_op jit(solution)/shard_map/psum | solution.py:101
  296.8 198.1 %all-gather.3.cloned.1.call-done = bf16[1,2560,2560]{2,1,0:T(8,128)(2,1)} async-done(((bf16[1,80,2560]{2,1,0:T(8,128)(2,1)}), bf16[1,2560,2560]{2,1,0:T(8,128)(2,1)}) %all-gather.3.cloned.1.call-update) | async-done | bytes 13107216 | tf_op jit(solution)/shard_map/all_gather | solution.py:32
  495.0 221.6 %while.36 = (s32[]{:T(128)}, bf16[32,2560]{1,0:T(8,128)(2,1)S(1)}, bf16[4,32,2560]{2,1,0:T(8,128)(2,1)S(1)}, s32[]{:T(128)}, pred[]{:T(512)}, /*index=5*/bf16[4,...) while((s32[]{:T(128)}, bf16[32,2560]{1,0:T(8,128)(2,1)S(1)}, ...), condition=%wide.region_5.6_spmd, body=%wide.region_0.5_spmd.sunk | while | flops 420741152 | bytes 15596937 | solution.py:58
  500.2 7.4 collective-permute-done
  508.7 8.3 conditional.5
  509.8 7.1 fusion
  522.2 8.3 conditional.5
  523.3 7.1 fusion
  538.1 8.3 conditional.5
  539.3 7.1 fusion
  554.1 8.3 conditional.5
  555.2 7.1 fusion
  570.1 12.6 %collective-permute-start = (bf16[32,2560]{1,0:T(8,128)(2,1)S(1)}, bf16[32,2560]{1,0:T(8,128)(2,1)S(1)}, u32[]{:S(2)}, u32[]{:S(2)}) collective-permute-start(bf16[32,2560]{1,0:T(8,128)(2,1)S(1)} %get-tuple-element.741), channel_id=1, source_target_pairs={{0,32},{32,64},{64,96},{96,128},{128,160},{160,192},{192,224},{224... | collective-permute-start | bytes 491528 | tf_op jit(solution)/shard_map/while/body/eval_jaxpr/ppermute | solution.py:10
  610.3 10.2 collective-permute-start
  648.1 10.2 collective-permute-start
  669.3 7.3 collective-permute-start
  689.8 14.7 %collective-permute-start = (bf16[32,2560]{1,0:T(8,128)(2,1)S(1)}, bf16[32,2560]{1,0:T(8,128)(2,1)S(1)}, u32[]{:S(2)}, u32[]{:S(2)}) collective-permute-start(bf16[32,2560]{1,0:T(8,128)(2,1)S(1)} %get-tuple-element.741), channel_id=1, source_target_pairs={{0,32},{32,64},{64,96},{96,128},{128,160},{160,192},{192,224},{224... | collective-permute-start | bytes 491528 | tf_op jit(solution)/shard_map/while/body/eval_jaxpr/ppermute | solution.py:10
  716.7 336.8 %while.37 = (s32[]{:T(128)}, bf16[32,2560]{1,0:T(8,128)(2,1)S(1)}, bf16[4,32,2560]{2,1,0:T(8,128)(2,1)S(1)}, f32[2560]{0:T(1024)S(1)}, s32[]{:T(128)}, /*index=5...) while((s32[]{:T(128)}, bf16[32,2560]{1,0:T(8,128)(2,1)S(1)}, ...), condition=%wide.region_14.15_spmd.clone, body=%wide.region_6.14_spmd.clone.sunk | while | flops 421808672 | bytes 16800728 | solution.py:94
  718.8 7.5 collective-permute-done.1
  737.0 7.5 collective-permute-done.1
  755.2 7.5 collective-permute-done.1
  773.4 7.5 collective-permute-done.1
  835.6 135.2 %collective-permute-done.1 = bf16[32,2560]{1,0:T(8,128)(2,1)S(1)} collective-permute-done((bf16[32,2560]{1,0:T(8,128)(2,1)S(1)}, bf16[32,2560]{1,0:T(8,128)(2,1)S(1)}, u32[]{:S(2)}, u32[]{:S(2)}) %collective-permute-start.1) | collective-permute-done | bytes 163872 | tf_op jit(solution)/shard_map/while/body/eval_jaxpr/ppermute | solution.py:10
  970.8 10.0 conditional.6
  971.9 8.8 fusion.21
  989.6 10.0 conditional.6
  990.7 8.8 fusion.21
  1008.4 10.0 conditional.6
  1009.5 8.8 fusion.21
  1027.2 10.0 conditional.6
  1028.3 8.8 fusion.21
  1043.9 8.6 collective-permute-start.1
  (298 shorter events, 262.5 us)
Async XLA Ops:
  7.2 288.2 %all-reduce.2.cloned.1.call-start = ((), (), s32[]{:S(2)}) async-start(), calls=%async_computation | async-start | bytes 327680 | tf_op jit(solution)/shard_map/psum | solution.py:101
  8.9 486.0 %all-gather.3.cloned.1.call-start = ((), (), s32[]{:S(2)}) async-start(), calls=%async_computation.1 | async-start | bytes 13516800 | tf_op jit(solution)/shard_map/all_gather | solution.py:32
  496.2 11.5 %collective-permute-start = (bf16[32,2560]{1,0:T(8,128)(2,1)S(1)}, bf16[32,2560]{1,0:T(8,128)(2,1)S(1)}, u32[]{:S(2)}, u32[]{:S(2)}) collective-permute-start(bf16[32,2560]{1,0:T(8,128)(2,1)S(1)} %get-tuple-element.741), channel_id=1, source_target_pairs={{0,32},{32,64},{64,96},{96,128},{128,160},{160,192},{192,224},{224... | collective-permute-start | bytes 491528 | tf_op jit(solution)/shard_map/while/body/eval_jaxpr/ppermute | solution.py:10
  546.4 6.6 collective-permute-start
  570.1 14.9 %collective-permute-start = (bf16[32,2560]{1,0:T(8,128)(2,1)S(1)}, bf16[32,2560]{1,0:T(8,128)(2,1)S(1)}, u32[]{:S(2)}, u32[]{:S(2)}) collective-permute-start(bf16[32,2560]{1,0:T(8,128)(2,1)S(1)} %get-tuple-element.741), channel_id=1, source_target_pairs={{0,32},{32,64},{64,96},{96,128},{128,160},{160,192},{192,224},{224... | collective-permute-start | bytes 491528 | tf_op jit(solution)/shard_map/while/body/eval_jaxpr/ppermute | solution.py:10
  593.7 7.8 collective-permute-start
  610.3 12.4 %collective-permute-start = (bf16[32,2560]{1,0:T(8,128)(2,1)S(1)}, bf16[32,2560]{1,0:T(8,128)(2,1)S(1)}, u32[]{:S(2)}, u32[]{:S(2)}) collective-permute-start(bf16[32,2560]{1,0:T(8,128)(2,1)S(1)} %get-tuple-element.741), channel_id=1, source_target_pairs={{0,32},{32,64},{64,96},{96,128},{128,160},{160,192},{192,224},{224... | collective-permute-start | bytes 491528 | tf_op jit(solution)/shard_map/while/body/eval_jaxpr/ppermute | solution.py:10
  631.5 7.8 collective-permute-start
  648.1 12.4 %collective-permute-start = (bf16[32,2560]{1,0:T(8,128)(2,1)S(1)}, bf16[32,2560]{1,0:T(8,128)(2,1)S(1)}, u32[]{:S(2)}, u32[]{:S(2)}) collective-permute-start(bf16[32,2560]{1,0:T(8,128)(2,1)S(1)} %get-tuple-element.741), channel_id=1, source_target_pairs={{0,32},{32,64},{64,96},{96,128},{128,160},{160,192},{192,224},{224... | collective-permute-start | bytes 491528 | tf_op jit(solution)/shard_map/while/body/eval_jaxpr/ppermute | solution.py:10
  661.6 6.6 collective-permute-start
  669.3 9.6 collective-permute-start
  680.0 8.7 collective-permute-start
  689.8 17.0 %collective-permute-start = (bf16[32,2560]{1,0:T(8,128)(2,1)S(1)}, bf16[32,2560]{1,0:T(8,128)(2,1)S(1)}, u32[]{:S(2)}, u32[]{:S(2)}) collective-permute-start(bf16[32,2560]{1,0:T(8,128)(2,1)S(1)} %get-tuple-element.741), channel_id=1, source_target_pairs={{0,32},{32,64},{64,96},{96,128},{128,160},{160,192},{192,224},{224... | collective-permute-start | bytes 491528 | tf_op jit(solution)/shard_map/while/body/eval_jaxpr/ppermute | solution.py:10
  707.9 8.7 collective-permute-start
  716.8 9.5 collective-permute-start.1
  726.3 8.6 collective-permute-start.1
  735.0 9.5 collective-permute-start.1
  744.5 8.6 collective-permute-start.1
  753.1 9.5 collective-permute-start.1
  762.7 8.6 collective-permute-start.1
  771.3 9.5 collective-permute-start.1
  780.9 8.7 collective-permute-start.1
  789.6 8.7 collective-permute-start.1
  798.4 8.7 collective-permute-start.1
  807.2 8.7 collective-permute-start.1
  816.0 8.7 collective-permute-start.1
  824.8 8.7 collective-permute-start.1
  833.6 137.2 %collective-permute-start.1 = (bf16[32,2560]{1,0:T(8,128)(2,1)S(1)}, bf16[32,2560]{1,0:T(8,128)(2,1)S(1)}, u32[]{:S(2)}, u32[]{:S(2)}) collective-permute-start(bf16[32,2560]{1,0:T(8,128)(2,1)S(1)} %get-tuple-element.657), channel_id=1, source_target_pairs={{32,0},{64,32},{96,64},{128,96},{160,128},{192,160},{224,192},{256... | collective-permute-start | bytes 491528 | tf_op jit(solution)/shard_map/while/body/eval_jaxpr/ppermute | solution.py:10
  980.8 8.8 collective-permute-start.1
  999.6 8.8 collective-permute-start.1
  1018.5 8.8 collective-permute-start.1
  1043.9 9.6 collective-permute-start.1
  (10 other events, 273.2 us)
Sparse Core Ops, SparseCore 0:
  11.5 283.8 all-reduce.1
  299.0 195.8 all-gather.2
where the time goes:
time: 1060 us
  waiting for transfers between devices  783 us (74%)
  starting transfers between devices  164 us (15%)
  matrix products  63.6 us (6%)
  other arithmetic  32.8 us (3%)
  between operations  14.1 us (1%)
    ppermute x38, waiting for transfers between devices, shifted(): return lax.ppermute(array, axis, pairs)  299 us
    psum x1, waiting for transfers between devices, per_device(): lax.psum(local_bucket.astype(jnp.bfloat16), 'dp').astype(jnp.float32)  286 us
    all_gather x1, waiting for transfers between devices, per_device(): forward_weight = lax.all_gather(weight[0], 'dp', axis=0, tiled=True)  198 us
    ppermute x38, starting transfers between devices, shifted(): return lax.ppermute(array, axis, pairs)  163 us
    dot_general x4, matrix products, backward_run(): lax.dot_general(incoming, forward_weight, (((1,), (1,)), ((), ())), prefe...  35 us
    dot_general x4, matrix products, forward_run(): jnp.dot(scaled_in, forward_weight, preferred_element_type=jnp.float32)  28.6 us
  transfers between devices with their start and end apart: 40, of which 40 were waited for; matrix products, arithmetic and copies ran while one was open for 0% of the time, Pallas kernels for 0%

commit v1 on v0

v1 whole, which is shorter than its diff:
```python
import functools

import jax
import jax.numpy as jnp
from jax import lax
from jax.experimental import pallas as pl
from jax.experimental.pallas import tpu as pltpu
from jax.sharding import PartitionSpec as P

VMEM = pl.BlockSpec(memory_space=pltpu.VMEM)
BF16 = jnp.bfloat16
F32 = jnp.float32
LIMIT = 20 << 20


def normalize(acts):
    values = acts.astype(F32)
    center = values - jnp.mean(values, axis=-1, keepdims=True)
    variance = jnp.mean(center * center, axis=-1, keepdims=True)
    inverse = 1.0 / jnp.sqrt(variance + 1e-05)
    return center * inverse, inverse


def prepare_kernel(step, source, weight_ref, turned_ref, sems):
    width = source.shape[0]
    count = width // step

    def piece(i):
        here = pl.ds(i * step, step)
        return pltpu.make_async_copy(source.at[here, :], weight_ref.at[here, :], sems.at[i])

    for i in range(count):
        piece(i).start()
    for i in range(count):
        piece(i).wait()

        def turn(j, _):
            across = pl.ds(pl.multiple_of(j * step, step), step)
            turned_ref[across, i * step : (i + 1) * step] = weight_ref[i * step : (i + 1) * step, across].T

        lax.fori_loop(0, count, turn, None)


def prepare(whole):
    step = 256
    return pl.pallas_call(
        functools.partial(prepare_kernel, step),
        out_shape=[pltpu.VMEM(whole.shape, whole.dtype)] * 2,
        in_specs=[pl.BlockSpec(memory_space=pltpu.HBM)],
        out_specs=[VMEM] * 2,
        scratch_shapes=[pltpu.SemaphoreType.DMA((whole.shape[0] // step,))],
        compiler_params=pltpu.CompilerParams(vmem_limit_bytes=LIMIT),
        name="prepare_weight",
    )(whole)


def forward_kernel(tile, x_ref, gain_ref, weight_ref, y_ref, scaled):
    normed, _ = normalize(x_ref[...])
    scaled[...] = (normed * gain_ref[...]).astype(BF16)

    def column(i, _):
        here = pl.ds(pl.multiple_of(i * tile, tile), tile)
        projected = jnp.dot(scaled[...], weight_ref[:, here], preferred_element_type=F32)
        y_ref[:, here] = (x_ref[:, here].astype(F32) + projected).astype(BF16)

    lax.fori_loop(0, x_ref.shape[1] // tile, column, None)


def forward(x, gain, weight):
    rows, width = x.shape
    return pl.pallas_call(
        functools.partial(forward_kernel, width // 2),
        out_shape=jax.ShapeDtypeStruct(x.shape, BF16),
        in_specs=[VMEM] * 3,
        out_specs=VMEM,
        scratch_shapes=[pltpu.VMEM((rows, width), BF16)],
        compiler_params=pltpu.CompilerParams(vmem_limit_bytes=LIMIT),
        name="forward",
    )(x, gain, pltpu.with_memory_space_constraint(weight, pltpu.VMEM))


def backward_kernel(tile, grad_ref, x_ref, gain_ref, total_ref, weight_ref, out_ref, new_total_ref, back):
    def column(i, _):
        here = pl.ds(pl.multiple_of(i * tile, tile), tile)
        back[:, here] = jnp.dot(grad_ref[...], weight_ref[:, here], preferred_element_type=F32)

    lax.fori_loop(0, x_ref.shape[1] // tile, column, None)
    normed, inverse = normalize(x_ref[...])
    back_proj = back[...]
    scaled = back_proj * gain_ref[...]
    mean_one = jnp.mean(scaled, axis=-1, keepdims=True)
    mean_two = jnp.mean(scaled * normed, axis=-1, keepdims=True)
    norm_grad = inverse * (scaled - mean_one - normed * mean_two)
    out_ref[...] = (grad_ref[...].astype(F32) + norm_grad).astype(BF16)
    new_total_ref[...] = total_ref[...] + jnp.sum(back_proj * normed, axis=0, keepdims=True)


def backward(grad, x, gain, total, weight):
    rows, width = x.shape
    return pl.pallas_call(
        functools.partial(backward_kernel, width // 2),
        out_shape=(jax.ShapeDtypeStruct(x.shape, BF16), jax.ShapeDtypeStruct(total.shape, F32)),
        in_specs=[VMEM] * 5,
        out_specs=[VMEM] * 2,
        scratch_shapes=[pltpu.VMEM((rows, width), F32)],
        compiler_params=pltpu.CompilerParams(vmem_limit_bytes=LIMIT),
        name="backward",
    )(grad, x, gain, total, pltpu.with_memory_space_constraint(weight, pltpu.VMEM))


def per_device(inputs, cotangent, weight, gain, momentum, prev_grads):
    sections = lax.axis_size("section")
    section = lax.axis_index("section")
    batches, rows, width = inputs.shape

    whole = lax.all_gather(weight[0], "dp", axis=0, tiled=True)

    bucket = prev_grads[0, 0].astype(BF16)
    pieces = lax.all_to_all(bucket, "dp", 0, 0, tiled=True).astype(F32)
    summed = jnp.sum(pieces, axis=0, keepdims=True)
    new_momentum = 0.9 * momentum + (summed / lax.axis_size("dp"))[None]

    resident, turned = prepare(whole)

    parts = range(batches)
    up = [[(s, s + 1) for s in range(h, sections - 1, 2)] for h in range(2)]
    down = [[(s, s - 1) for s in range(sections - 1 - h, 0, -2)] for h in range(2)]

    def forward_pair(j, carry):
        received, stash = carry
        for h in range(2):
            s = 2 * j + h
            mine = section == s
            runs = jnp.logical_and(mine, section < sections - 1)
            sent = []
            for m in parts:
                y = lax.cond(runs, lambda x: forward(x, gain, resident), lambda x: x, received[m])
                sent.append(lax.ppermute(y, "section", up[h]))
            stash = [jnp.where(mine, received[m], stash[m]) for m in parts]
            received = sent
        return received, stash

    fresh = [inputs[m] for m in parts]
    received, stash = lax.fori_loop(0, sections // 2, forward_pair, (fresh, fresh))

    def backward_pair(j, carry):
        incoming, collected, total = carry
        for h in range(2):
            s = sections - 1 - 2 * j - h
            sent = []
            kept = []
            for m in parts:
                out, total = lax.cond(
                    section == s,
                    lambda grad, x, old, total: tuple(backward(grad, x, gain, total, turned)),
                    lambda grad, x, old, total: (old, total),
                    incoming[m],
                    stash[m],
                    collected[m],
                    total,
                )
                kept.append(out)
                sent.append(lax.ppermute(out, "section", down[h]))
            incoming, collected = sent, kept
        return incoming, collected, total

    start = ([cotangent[m] for m in parts], [jnp.zeros((rows, width), BF16) for m in parts], jnp.zeros((1, width), F32))
    incoming, collected, total = lax.fori_loop(0, sections // 2, backward_pair, start)
    input_grads = jnp.stack(collected)[None]
    return input_grads, total[None], new_momentum


def solution(mesh):
    in_specs = (
        P(None, "dp", None),
        P(None, "dp", None),
        P("section", "dp", None),
        P("section", None),
        P("section", "dp", None),
        P("section", "dp", None, None),
    )
    out_specs = (P("section", None, "dp", None), P("section", "dp", None), P("section", "dp", None))
    return jax.shard_map(per_device, mesh=mesh, in_specs=in_specs, out_specs=out_specs, check_vma=False)
```

time: 1060 us -> 1070 us (level)
  starting transfers between devices: 164 us -> 329 us
  waiting for transfers between devices: 783 us -> 619 us
  matrix products: 63.6 us -> 0 us
  local copies, waits for them, and re-layouts: 2.06 us -> 58.5 us
  Pallas kernels: 0 us -> 34.4 us
  other arithmetic: 32.8 us -> 6.44 us
    psum x1 -> x0, waiting for transfers between devices: 286 us -> none  [per_device(): lax.psum(local_bucket.astype(jnp.bfloat16), 'dp').astype(jnp.float32)]
    ppermute x38 -> x128, waiting for transfers between devices: 299 us -> 450 us  [the longest x64 422 us: backward_pair(): sent.append(lax.ppermute(out, 'section', down[h]))]
    ppermute x38 -> x128, starting transfers between devices: 163 us -> 312 us  [the longest x64 229 us: forward_pair(): sent.append(lax.ppermute(y, 'section', up[h]))]
    dot_general x8 -> x0, matrix products: 63.6 us -> none  [the longest x4 35 us: backward_run(): lax.dot_general(incoming, forward_weight, (((1,), (1,)), ((), ())), prefe...]
    cond x0 -> x80, local copies, waits for them, and re-layouts: none -> 38.6 us
    all_gather x1, waiting for transfers between devices: 198 us -> 160 us  [per_device(): whole = lax.all_gather(weight[0], 'dp', axis=0, tiled=True)]
    pallas_call x0 -> x9, Pallas kernels: none -> 34.4 us  [the longest x4 13.3 us: backward(): pl.pallas_call(functools.partial(backward_kernel, width // 2), out_shape=...]
    dynamic_update_slice x38 -> x0, other arithmetic: 20.1 us -> none  [the longest x19 19.2 us: forward_tick(): lax.dynamic_update_index_in_dim(stash, jnp.where(active, block, previous)...]
  transfers between devices with their start and end apart: 40 -> 130, of which waited for: 40 -> 58; matrix products, arithmetic and copies ran while one was open for 0% -> 1% of each run, Pallas kernels for 0% -> 2%
where the time goes in v1:
time: 1070 us
  waiting for transfers between devices  619 us (58%)
  starting transfers between devices  329 us (31%)
  local copies, waits for them, and re-layouts  58.5 us (5%)
  Pallas kernels  34.4 us (3%)
  between operations  14.2 us (1%)
    ppermute x64, waiting for transfers between devices, backward_pair(): sent.append(lax.ppermute(out, 'section', down[h]))  422 us
    ppermute x64, starting transfers between devices, forward_pair(): sent.append(lax.ppermute(y, 'section', up[h]))  229 us
    all_gather x1, waiting for transfers between devices, per_device(): whole = lax.all_gather(weight[0], 'dp', axis=0, tiled=True)  160 us
    ppermute x64, starting transfers between devices, backward_pair(): sent.append(lax.ppermute(out, 'section', down[h]))  82.8 us
    cond x80, local copies, waits for them, and re-layouts  38.6 us
    ppermute x64, waiting for transfers between devices, forward_pair(): sent.append(lax.ppermute(y, 'section', up[h]))  28.5 us
  transfers between devices with their start and end apart: 130, of which 58 were waited for; matrix products, arithmetic and copies ran while one was open for 1% of the time, Pallas kernels for 2%

profile of v1, /device:TPU:1, one launch (start us, length us, event | category | flops | bytes accessed | tf_op | source)
XLA Modules:
  0.0 1067.3 jit_solution(14530839185027559490)
XLA Ops:
  10.8 16.5 %all-to-all-start = ((bf16[32,2,1280]{2,1,0:T(2,128)(2,1)}), bf16[32,2,1280]{2,1,0:T(2,128)(2,1)S(1)}, u32[]{:S(2)}, u32[]{:S(2)}) async-start(bf16[32,2,1280]{2,1,0:T(2,128)(2,1)} %reshape.32), calls=%async_computation | async-start | bytes 327680 | tf_op jit(solution)/shard_map/all_to_all | solution.py:119
  30.6 8.4 all-to-all-done
  40.8 160.1 %all-gather.3.cloned.1.call-done = bf16[1,2560,2560]{2,1,0:T(8,128)(2,1)} async-done(((bf16[1,80,2560]{2,1,0:T(8,128)(2,1)}), bf16[1,2560,2560]{2,1,0:T(8,128)(2,1)}) %all-gather.3.cloned.1.call-update) | async-done | bytes 13107216 | tf_op jit(solution)/shard_map/all_gather | solution.py:116
  200.9 10.2 prepare_weight.1
  211.1 4.7 copy-done
  215.8 4.8 copy-done.9
  220.6 294.5 %while.73 = (s32[]{:T(128)}, bf16[32,2560]{1,0:T(8,128)(2,1)S(1)}, bf16[32,2560]{1,0:T(8,128)(2,1)S(1)}, bf16[32,2560]{1,0:T(8,128)(2,1)S(1)}, bf16[32,2560]{1,0...) while((s32[]{:T(128)}, bf16[32,2560]{1,0:T(8,128)(2,1)S(1)}, ...), condition=%wide.region_17.0_spmd, body=%wide.region_0.17_spmd.sunk | while | flops 655370 | bytes 428606400 | solution.py:144
  226.1 5.3 collective-permute-done.2
  231.4 7.5 conditional.35
  231.4 4.7 copy-done.14
  240.2 7.5 conditional.37
  240.2 4.7 copy-done.15
  249.0 7.5 conditional.39
  249.0 4.7 copy-done.16
  257.8 7.5 conditional.33
  257.8 4.7 copy-done.17
  274.3 34.2 %collective-permute-start.3 = (bf16[32,2560]{1,0:T(8,128)(2,1)S(1)}, bf16[32,2560]{1,0:T(8,128)(2,1)S(1)}, u32[]{:S(2)}, u32[]{:S(2)}) collective-permute-start(bf16[32,2560]{1,0:T(8,128)(2,1)S(1)} %get-tuple-element.1570), channel_id=1, source_target_pairs={{32,64},{96,128},{160,192},{224,256},{288,320},{352,384},{416,448}... | collective-permute-start | bytes 491528 | tf_op jit(solution)/shard_map/while/body/eval_jaxpr/ppermute | solution.py:138
  321.5 5.5 collective-permute-start.3
  339.9 34.2 %collective-permute-start.3 = (bf16[32,2560]{1,0:T(8,128)(2,1)S(1)}, bf16[32,2560]{1,0:T(8,128)(2,1)S(1)}, u32[]{:S(2)}, u32[]{:S(2)}) collective-permute-start(bf16[32,2560]{1,0:T(8,128)(2,1)S(1)} %get-tuple-element.1570), channel_id=1, source_target_pairs={{32,64},{96,128},{160,192},{224,256},{288,320},{352,384},{416,448}... | collective-permute-start | bytes 491528 | tf_op jit(solution)/shard_map/while/body/eval_jaxpr/ppermute | solution.py:138
  387.1 5.5 collective-permute-start.3
  405.6 34.2 %collective-permute-start.3 = (bf16[32,2560]{1,0:T(8,128)(2,1)S(1)}, bf16[32,2560]{1,0:T(8,128)(2,1)S(1)}, u32[]{:S(2)}, u32[]{:S(2)}) collective-permute-start(bf16[32,2560]{1,0:T(8,128)(2,1)S(1)} %get-tuple-element.1570), channel_id=1, source_target_pairs={{32,64},{96,128},{160,192},{224,256},{288,320},{352,384},{416,448}... | collective-permute-start | bytes 491528 | tf_op jit(solution)/shard_map/while/body/eval_jaxpr/ppermute | solution.py:138
  452.8 5.5 collective-permute-start.3
  471.3 36.3 %collective-permute-start.3 = (bf16[32,2560]{1,0:T(8,128)(2,1)S(1)}, bf16[32,2560]{1,0:T(8,128)(2,1)S(1)}, u32[]{:S(2)}, u32[]{:S(2)}) collective-permute-start(bf16[32,2560]{1,0:T(8,128)(2,1)S(1)} %get-tuple-element.1570), channel_id=1, source_target_pairs={{32,64},{96,128},{160,192},{224,256},{288,320},{352,384},{416,448}... | collective-permute-start | bytes 491528 | tf_op jit(solution)/shard_map/while/body/eval_jaxpr/ppermute | solution.py:138
  515.2 544.3 %while.74 = (s32[]{:T(128)}, bf16[32,2560]{1,0:T(8,128)(2,1)}, bf16[32,2560]{1,0:T(8,128)(2,1)S(1)}, bf16[32,2560]{1,0:T(8,128)(2,1)}, bf16[32,2560]{1,0:T(8,128...) while((s32[]{:T(128)}, bf16[32,2560]{1,0:T(8,128)(2,1)}, ...), condition=%wide.region_35.0_spmd, body=%wide.region_18.35_spmd.sunk | while | flops 9 | bytes 426149152 | solution.py:168
  547.3 29.5 %collective-permute-done.15 = bf16[32,2560]{1,0:T(8,128)(2,1)S(1)} collective-permute-done((bf16[32,2560]{1,0:T(8,128)(2,1)S(1)}, bf16[32,2560]{1,0:T(8,128)(2,1)S(1)}, u32[]{:S(2)}, u32[]{:S(2)}) %collective-permute-start.15) | collective-permute-done | bytes 163872 | tf_op jit(solution)/shard_map/while/body/eval_jaxpr/ppermute | solution.py:163
  614.6 29.5 %collective-permute-done.15 = bf16[32,2560]{1,0:T(8,128)(2,1)S(1)} collective-permute-done((bf16[32,2560]{1,0:T(8,128)(2,1)S(1)}, bf16[32,2560]{1,0:T(8,128)(2,1)S(1)}, u32[]{:S(2)}, u32[]{:S(2)}) %collective-permute-start.15) | collective-permute-done | bytes 163872 | tf_op jit(solution)/shard_map/while/body/eval_jaxpr/ppermute | solution.py:163
  682.5 28.9 %collective-permute-done.15 = bf16[32,2560]{1,0:T(8,128)(2,1)S(1)} collective-permute-done((bf16[32,2560]{1,0:T(8,128)(2,1)S(1)}, bf16[32,2560]{1,0:T(8,128)(2,1)S(1)}, u32[]{:S(2)}, u32[]{:S(2)}) %collective-permute-start.15) | collective-permute-done | bytes 163872 | tf_op jit(solution)/shard_map/while/body/eval_jaxpr/ppermute | solution.py:163
  728.8 273.6 %collective-permute-done.15 = bf16[32,2560]{1,0:T(8,128)(2,1)S(1)} collective-permute-done((bf16[32,2560]{1,0:T(8,128)(2,1)S(1)}, bf16[32,2560]{1,0:T(8,128)(2,1)S(1)}, u32[]{:S(2)}, u32[]{:S(2)}) %collective-permute-start.15) | collective-permute-done | bytes 163872 | tf_op jit(solution)/shard_map/while/body/eval_jaxpr/ppermute | solution.py:163
  1008.4 8.5 conditional.40
  1018.2 7.6 conditional.41
  1027.2 8.6 conditional.42
  1037.0 7.6 conditional.43
  (576 shorter events, 304.2 us)
Async XLA Ops:
  7.2 193.7 %all-gather.3.cloned.1.call-start = ((), (), s32[]{:S(2)}) async-start(), calls=%async_computation.1 | async-start | bytes 13516800 | tf_op jit(solution)/shard_map/all_gather | solution.py:116
  270.2 38.3 %collective-permute-start.4 = (bf16[32,2560]{1,0:T(8,128)(2,1)S(1)}, bf16[32,2560]{1,0:T(8,128)(2,1)S(1)}, u32[]{:S(2)}, u32[]{:S(2)}) collective-permute-start(bf16[32,2560]{1,0:T(8,128)(2,1)S(1)} %get-tuple-element.1571), channel_id=1, source_target_pairs={{0,32},{64,96},{128,160},{192,224},{256,288},{320,352},{384,416},{... | collective-permute-start | bytes 491528 | tf_op jit(solution)/shard_map/while/body/eval_jaxpr/ppermute | solution.py:138
  271.6 38.3 %collective-permute-start.6 = (bf16[32,2560]{1,0:T(8,128)(2,1)S(1)}, bf16[32,2560]{1,0:T(8,128)(2,1)S(1)}, u32[]{:S(2)}, u32[]{:S(2)}) collective-permute-start(bf16[32,2560]{1,0:T(8,128)(2,1)S(1)} %get-tuple-element.1573), channel_id=1, source_target_pairs={{0,32},{64,96},{128,160},{192,224},{256,288},{320,352},{384,416},{... | collective-permute-start | bytes 491528 | tf_op jit(solution)/shard_map/while/body/eval_jaxpr/ppermute | solution.py:138
  272.9 38.3 %collective-permute-start = (bf16[32,2560]{1,0:T(8,128)(2,1)S(1)}, bf16[32,2560]{1,0:T(8,128)(2,1)S(1)}, u32[]{:S(2)}, u32[]{:S(2)}) collective-permute-start(bf16[32,2560]{1,0:T(8,128)(2,1)S(1)} %get-tuple-element.1567), channel_id=1, source_target_pairs={{0,32},{64,96},{128,160},{192,224},{256,288},{320,352},{384,416},{... | collective-permute-start | bytes 491528 | tf_op jit(solution)/shard_map/while/body/eval_jaxpr/ppermute | solution.py:138
  274.3 38.6 %collective-permute-start.3 = (bf16[32,2560]{1,0:T(8,128)(2,1)S(1)}, bf16[32,2560]{1,0:T(8,128)(2,1)S(1)}, u32[]{:S(2)}, u32[]{:S(2)}) collective-permute-start(bf16[32,2560]{1,0:T(8,128)(2,1)S(1)} %get-tuple-element.1570), channel_id=1, source_target_pairs={{32,64},{96,128},{160,192},{224,256},{288,320},{352,384},{416,448}... | collective-permute-start | bytes 491528 | tf_op jit(solution)/shard_map/while/body/eval_jaxpr/ppermute | solution.py:138
  335.9 38.3 %collective-permute-start.4 = (bf16[32,2560]{1,0:T(8,128)(2,1)S(1)}, bf16[32,2560]{1,0:T(8,128)(2,1)S(1)}, u32[]{:S(2)}, u32[]{:S(2)}) collective-permute-start(bf16[32,2560]{1,0:T(8,128)(2,1)S(1)} %get-tuple-element.1571), channel_id=1, source_target_pairs={{0,32},{64,96},{128,160},{192,224},{256,288},{320,352},{384,416},{... | collective-permute-start | bytes 491528 | tf_op jit(solution)/shard_map/while/body/eval_jaxpr/ppermute | solution.py:138
  337.2 38.3 %collective-permute-start.6 = (bf16[32,2560]{1,0:T(8,128)(2,1)S(1)}, bf16[32,2560]{1,0:T(8,128)(2,1)S(1)}, u32[]{:S(2)}, u32[]{:S(2)}) collective-permute-start(bf16[32,2560]{1,0:T(8,128)(2,1)S(1)} %get-tuple-element.1573), channel_id=1, source_target_pairs={{0,32},{64,96},{128,160},{192,224},{256,288},{320,352},{384,416},{... | collective-permute-start | bytes 491528 | tf_op jit(solution)/shard_map/while/body/eval_jaxpr/ppermute | solution.py:138
  338.6 38.3 %collective-permute-start = (bf16[32,2560]{1,0:T(8,128)(2,1)S(1)}, bf16[32,2560]{1,0:T(8,128)(2,1)S(1)}, u32[]{:S(2)}, u32[]{:S(2)}) collective-permute-start(bf16[32,2560]{1,0:T(8,128)(2,1)S(1)} %get-tuple-element.1567), channel_id=1, source_target_pairs={{0,32},{64,96},{128,160},{192,224},{256,288},{320,352},{384,416},{... | collective-permute-start | bytes 491528 | tf_op jit(solution)/shard_map/while/body/eval_jaxpr/ppermute | solution.py:138
  339.9 38.6 %collective-permute-start.3 = (bf16[32,2560]{1,0:T(8,128)(2,1)S(1)}, bf16[32,2560]{1,0:T(8,128)(2,1)S(1)}, u32[]{:S(2)}, u32[]{:S(2)}) collective-permute-start(bf16[32,2560]{1,0:T(8,128)(2,1)S(1)} %get-tuple-element.1570), channel_id=1, source_target_pairs={{32,64},{96,128},{160,192},{224,256},{288,320},{352,384},{416,448}... | collective-permute-start | bytes 491528 | tf_op jit(solution)/shard_map/while/body/eval_jaxpr/ppermute | solution.py:138
  401.6 38.3 %collective-permute-start.4 = (bf16[32,2560]{1,0:T(8,128)(2,1)S(1)}, bf16[32,2560]{1,0:T(8,128)(2,1)S(1)}, u32[]{:S(2)}, u32[]{:S(2)}) collective-permute-start(bf16[32,2560]{1,0:T(8,128)(2,1)S(1)} %get-tuple-element.1571), channel_id=1, source_target_pairs={{0,32},{64,96},{128,160},{192,224},{256,288},{320,352},{384,416},{... | collective-permute-start | bytes 491528 | tf_op jit(solution)/shard_map/while/body/eval_jaxpr/ppermute | solution.py:138
  402.9 38.3 %collective-permute-start.6 = (bf16[32,2560]{1,0:T(8,128)(2,1)S(1)}, bf16[32,2560]{1,0:T(8,128)(2,1)S(1)}, u32[]{:S(2)}, u32[]{:S(2)}) collective-permute-start(bf16[32,2560]{1,0:T(8,128)(2,1)S(1)} %get-tuple-element.1573), channel_id=1, source_target_pairs={{0,32},{64,96},{128,160},{192,224},{256,288},{320,352},{384,416},{... | collective-permute-start | bytes 491528 | tf_op jit(solution)/shard_map/while/body/eval_jaxpr/ppermute | solution.py:138
  404.2 38.3 %collective-permute-start = (bf16[32,2560]{1,0:T(8,128)(2,1)S(1)}, bf16[32,2560]{1,0:T(8,128)(2,1)S(1)}, u32[]{:S(2)}, u32[]{:S(2)}) collective-permute-start(bf16[32,2560]{1,0:T(8,128)(2,1)S(1)} %get-tuple-element.1567), channel_id=1, source_target_pairs={{0,32},{64,96},{128,160},{192,224},{256,288},{320,352},{384,416},{... | collective-permute-start | bytes 491528 | tf_op jit(solution)/shard_map/while/body/eval_jaxpr/ppermute | solution.py:138
  405.6 38.6 %collective-permute-start.3 = (bf16[32,2560]{1,0:T(8,128)(2,1)S(1)}, bf16[32,2560]{1,0:T(8,128)(2,1)S(1)}, u32[]{:S(2)}, u32[]{:S(2)}) collective-permute-start(bf16[32,2560]{1,0:T(8,128)(2,1)S(1)} %get-tuple-element.1570), channel_id=1, source_target_pairs={{32,64},{96,128},{160,192},{224,256},{288,320},{352,384},{416,448}... | collective-permute-start | bytes 491528 | tf_op jit(solution)/shard_map/while/body/eval_jaxpr/ppermute | solution.py:138
  467.2 40.4 %collective-permute-start.4 = (bf16[32,2560]{1,0:T(8,128)(2,1)S(1)}, bf16[32,2560]{1,0:T(8,128)(2,1)S(1)}, u32[]{:S(2)}, u32[]{:S(2)}) collective-permute-start(bf16[32,2560]{1,0:T(8,128)(2,1)S(1)} %get-tuple-element.1571), channel_id=1, source_target_pairs={{0,32},{64,96},{128,160},{192,224},{256,288},{320,352},{384,416},{... | collective-permute-start | bytes 491528 | tf_op jit(solution)/shard_map/while/body/eval_jaxpr/ppermute | solution.py:138
  468.6 40.4 %collective-permute-start.6 = (bf16[32,2560]{1,0:T(8,128)(2,1)S(1)}, bf16[32,2560]{1,0:T(8,128)(2,1)S(1)}, u32[]{:S(2)}, u32[]{:S(2)}) collective-permute-start(bf16[32,2560]{1,0:T(8,128)(2,1)S(1)} %get-tuple-element.1573), channel_id=1, source_target_pairs={{0,32},{64,96},{128,160},{192,224},{256,288},{320,352},{384,416},{... | collective-permute-start | bytes 491528 | tf_op jit(solution)/shard_map/while/body/eval_jaxpr/ppermute | solution.py:138
  469.9 40.4 %collective-permute-start = (bf16[32,2560]{1,0:T(8,128)(2,1)S(1)}, bf16[32,2560]{1,0:T(8,128)(2,1)S(1)}, u32[]{:S(2)}, u32[]{:S(2)}) collective-permute-start(bf16[32,2560]{1,0:T(8,128)(2,1)S(1)} %get-tuple-element.1567), channel_id=1, source_target_pairs={{0,32},{64,96},{128,160},{192,224},{256,288},{320,352},{384,416},{... | collective-permute-start | bytes 491528 | tf_op jit(solution)/shard_map/while/body/eval_jaxpr/ppermute | solution.py:138
  471.3 40.7 %collective-permute-start.3 = (bf16[32,2560]{1,0:T(8,128)(2,1)S(1)}, bf16[32,2560]{1,0:T(8,128)(2,1)S(1)}, u32[]{:S(2)}, u32[]{:S(2)}) collective-permute-start(bf16[32,2560]{1,0:T(8,128)(2,1)S(1)} %get-tuple-element.1570), channel_id=1, source_target_pairs={{32,64},{96,128},{160,192},{224,256},{288,320},{352,384},{416,448}... | collective-permute-start | bytes 491528 | tf_op jit(solution)/shard_map/while/body/eval_jaxpr/ppermute | solution.py:138
  542.1 34.7 %collective-permute-start.15 = (bf16[32,2560]{1,0:T(8,128)(2,1)S(1)}, bf16[32,2560]{1,0:T(8,128)(2,1)S(1)}, u32[]{:S(2)}, u32[]{:S(2)}) collective-permute-start(bf16[32,2560]{1,0:T(8,128)(2,1)S(1)} %get-tuple-element.1554), channel_id=1, source_target_pairs={{448,416},{384,352},{320,288},{256,224},{192,160},{128,96},{64,32}... | collective-permute-start | bytes 491528 | tf_op jit(solution)/shard_map/while/body/eval_jaxpr/ppermute | solution.py:163
  543.4 35.2 %collective-permute-start.13 = (bf16[32,2560]{1,0:T(8,128)(2,1)S(1)}, bf16[32,2560]{1,0:T(8,128)(2,1)S(1)}, u32[]{:S(2)}, u32[]{:S(2)}) collective-permute-start(bf16[32,2560]{1,0:T(8,128)(2,1)S(1)} %get-tuple-element.1553), channel_id=1, source_target_pairs={{448,416},{384,352},{320,288},{256,224},{192,160},{128,96},{64,32}... | collective-permute-start | bytes 491528 | tf_op jit(solution)/shard_map/while/body/eval_jaxpr/ppermute | solution.py:163
  544.7 35.7 %collective-permute-start.11 = (bf16[32,2560]{1,0:T(8,128)(2,1)S(1)}, bf16[32,2560]{1,0:T(8,128)(2,1)S(1)}, u32[]{:S(2)}, u32[]{:S(2)}) collective-permute-start(bf16[32,2560]{1,0:T(8,128)(2,1)S(1)} %get-tuple-element.1552), channel_id=1, source_target_pairs={{448,416},{384,352},{320,288},{256,224},{192,160},{128,96},{64,32}... | collective-permute-start | bytes 491528 | tf_op jit(solution)/shard_map/while/body/eval_jaxpr/ppermute | solution.py:163
  546.0 36.1 %collective-permute-start.9 = (bf16[32,2560]{1,0:T(8,128)(2,1)S(1)}, bf16[32,2560]{1,0:T(8,128)(2,1)S(1)}, u32[]{:S(2)}, u32[]{:S(2)}) collective-permute-start(bf16[32,2560]{1,0:T(8,128)(2,1)S(1)} %get-tuple-element.1551), channel_id=1, source_target_pairs={{448,416},{384,352},{320,288},{256,224},{192,160},{128,96},{64,32}... | collective-permute-start | bytes 491528 | tf_op jit(solution)/shard_map/while/body/eval_jaxpr/ppermute | solution.py:163
  609.4 34.7 %collective-permute-start.15 = (bf16[32,2560]{1,0:T(8,128)(2,1)S(1)}, bf16[32,2560]{1,0:T(8,128)(2,1)S(1)}, u32[]{:S(2)}, u32[]{:S(2)}) collective-permute-start(bf16[32,2560]{1,0:T(8,128)(2,1)S(1)} %get-tuple-element.1554), channel_id=1, source_target_pairs={{448,416},{384,352},{320,288},{256,224},{192,160},{128,96},{64,32}... | collective-permute-start | bytes 491528 | tf_op jit(solution)/shard_map/while/body/eval_jaxpr/ppermute | solution.py:163
  610.7 35.2 %collective-permute-start.13 = (bf16[32,2560]{1,0:T(8,128)(2,1)S(1)}, bf16[32,2560]{1,0:T(8,128)(2,1)S(1)}, u32[]{:S(2)}, u32[]{:S(2)}) collective-permute-start(bf16[32,2560]{1,0:T(8,128)(2,1)S(1)} %get-tuple-element.1553), channel_id=1, source_target_pairs={{448,416},{384,352},{320,288},{256,224},{192,160},{128,96},{64,32}... | collective-permute-start | bytes 491528 | tf_op jit(solution)/shard_map/while/body/eval_jaxpr/ppermute | solution.py:163
  612.0 35.6 %collective-permute-start.11 = (bf16[32,2560]{1,0:T(8,128)(2,1)S(1)}, bf16[32,2560]{1,0:T(8,128)(2,1)S(1)}, u32[]{:S(2)}, u32[]{:S(2)}) collective-permute-start(bf16[32,2560]{1,0:T(8,128)(2,1)S(1)} %get-tuple-element.1552), channel_id=1, source_target_pairs={{448,416},{384,352},{320,288},{256,224},{192,160},{128,96},{64,32}... | collective-permute-start | bytes 491528 | tf_op jit(solution)/shard_map/while/body/eval_jaxpr/ppermute | solution.py:163
  613.3 36.1 %collective-permute-start.9 = (bf16[32,2560]{1,0:T(8,128)(2,1)S(1)}, bf16[32,2560]{1,0:T(8,128)(2,1)S(1)}, u32[]{:S(2)}, u32[]{:S(2)}) collective-permute-start(bf16[32,2560]{1,0:T(8,128)(2,1)S(1)} %get-tuple-element.1551), channel_id=1, source_target_pairs={{448,416},{384,352},{320,288},{256,224},{192,160},{128,96},{64,32}... | collective-permute-start | bytes 491528 | tf_op jit(solution)/shard_map/while/body/eval_jaxpr/ppermute | solution.py:163
  678.6 34.6 %collective-permute-start.13 = (bf16[32,2560]{1,0:T(8,128)(2,1)S(1)}, bf16[32,2560]{1,0:T(8,128)(2,1)S(1)}, u32[]{:S(2)}, u32[]{:S(2)}) collective-permute-start(bf16[32,2560]{1,0:T(8,128)(2,1)S(1)} %get-tuple-element.1553), channel_id=1, source_target_pairs={{448,416},{384,352},{320,288},{256,224},{192,160},{128,96},{64,32}... | collective-permute-start | bytes 491528 | tf_op jit(solution)/shard_map/while/body/eval_jaxpr/ppermute | solution.py:163
  679.9 35.0 %collective-permute-start.11 = (bf16[32,2560]{1,0:T(8,128)(2,1)S(1)}, bf16[32,2560]{1,0:T(8,128)(2,1)S(1)}, u32[]{:S(2)}, u32[]{:S(2)}) collective-permute-start(bf16[32,2560]{1,0:T(8,128)(2,1)S(1)} %get-tuple-element.1552), channel_id=1, source_target_pairs={{448,416},{384,352},{320,288},{256,224},{192,160},{128,96},{64,32}... | collective-permute-start | bytes 491528 | tf_op jit(solution)/shard_map/while/body/eval_jaxpr/ppermute | solution.py:163
  681.2 35.5 %collective-permute-start.9 = (bf16[32,2560]{1,0:T(8,128)(2,1)S(1)}, bf16[32,2560]{1,0:T(8,128)(2,1)S(1)}, u32[]{:S(2)}, u32[]{:S(2)}) collective-permute-start(bf16[32,2560]{1,0:T(8,128)(2,1)S(1)} %get-tuple-element.1551), channel_id=1, source_target_pairs={{448,416},{384,352},{320,288},{256,224},{192,160},{128,96},{64,32}... | collective-permute-start | bytes 491528 | tf_op jit(solution)/shard_map/while/body/eval_jaxpr/ppermute | solution.py:163
  723.6 278.8 %collective-permute-start.15 = (bf16[32,2560]{1,0:T(8,128)(2,1)S(1)}, bf16[32,2560]{1,0:T(8,128)(2,1)S(1)}, u32[]{:S(2)}, u32[]{:S(2)}) collective-permute-start(bf16[32,2560]{1,0:T(8,128)(2,1)S(1)} %get-tuple-element.1554), channel_id=1, source_target_pairs={{448,416},{384,352},{320,288},{256,224},{192,160},{128,96},{64,32}... | collective-permute-start | bytes 491528 | tf_op jit(solution)/shard_map/while/body/eval_jaxpr/ppermute | solution.py:163
  724.9 279.3 %collective-permute-start.13 = (bf16[32,2560]{1,0:T(8,128)(2,1)S(1)}, bf16[32,2560]{1,0:T(8,128)(2,1)S(1)}, u32[]{:S(2)}, u32[]{:S(2)}) collective-permute-start(bf16[32,2560]{1,0:T(8,128)(2,1)S(1)} %get-tuple-element.1553), channel_id=1, source_target_pairs={{448,416},{384,352},{320,288},{256,224},{192,160},{128,96},{64,32}... | collective-permute-start | bytes 491528 | tf_op jit(solution)/shard_map/while/body/eval_jaxpr/ppermute | solution.py:163
  726.2 279.8 %collective-permute-start.11 = (bf16[32,2560]{1,0:T(8,128)(2,1)S(1)}, bf16[32,2560]{1,0:T(8,128)(2,1)S(1)}, u32[]{:S(2)}, u32[]{:S(2)}) collective-permute-start(bf16[32,2560]{1,0:T(8,128)(2,1)S(1)} %get-tuple-element.1552), channel_id=1, source_target_pairs={{448,416},{384,352},{320,288},{256,224},{192,160},{128,96},{64,32}... | collective-permute-start | bytes 491528 | tf_op jit(solution)/shard_map/while/body/eval_jaxpr/ppermute | solution.py:163
  727.5 280.2 %collective-permute-start.9 = (bf16[32,2560]{1,0:T(8,128)(2,1)S(1)}, bf16[32,2560]{1,0:T(8,128)(2,1)S(1)}, u32[]{:S(2)}, u32[]{:S(2)}) collective-permute-start(bf16[32,2560]{1,0:T(8,128)(2,1)S(1)} %get-tuple-element.1551), channel_id=1, source_target_pairs={{448,416},{384,352},{320,288},{256,224},{192,160},{128,96},{64,32}... | collective-permute-start | bytes 491528 | tf_op jit(solution)/shard_map/while/body/eval_jaxpr/ppermute | solution.py:163
  (128 other events, 1642.0 us)
Sparse Core Ops, SparseCore 0:
  11.2 189.6 all-gather.2

commit v2 on v1

v2 whole, which is shorter than its diff:
```python
import functools

import jax
import jax.numpy as jnp
from jax import lax
from jax.experimental import pallas as pl
from jax.experimental.pallas import tpu as pltpu
from jax.sharding import PartitionSpec as P

VMEM = pl.BlockSpec(memory_space=pltpu.VMEM)
SMEM = pl.BlockSpec(memory_space=pltpu.SMEM)
HBM = pl.BlockSpec(memory_space=pltpu.HBM)
BF16 = jnp.bfloat16
F32 = jnp.float32
LIMIT = 2 << 20


def held(array):
    return pltpu.with_memory_space_constraint(array, pltpu.VMEM)


def place_kernel(step, source, *rest):
    weights, turned, sems = rest[-3:]
    slot = 0 if len(rest) == 3 else 1
    width = source.shape[0]
    count = width // step

    def piece(i):
        here = pl.ds(i * step, step)
        return pltpu.make_async_copy(source.at[here, :], weights.at[slot, here, :], sems.at[i])

    for i in range(count):
        piece(i).start()
    for i in range(count):
        piece(i).wait()
        rows = slice(i * step, (i + 1) * step)

        def turn(j, _):
            across = pl.ds(pl.multiple_of(j * step, step), step)
            turned[slot, across, rows] = weights[slot, rows, across].T

        lax.fori_loop(0, count, turn, None)


def place(whole, buffers):
    step = 256
    return pl.pallas_call(
        functools.partial(place_kernel, step),
        out_shape=[pltpu.VMEM((2,) + whole.shape, BF16)] * 2,
        in_specs=[HBM] + [VMEM] * len(buffers),
        out_specs=[VMEM] * 2,
        input_output_aliases={1 + i: i for i in range(len(buffers))},
        scratch_shapes=[pltpu.SemaphoreType.DMA((whole.shape[0] // step,))],
        compiler_params=pltpu.CompilerParams(vmem_limit_bytes=LIMIT),
        name="place_weight",
    )(whole, *[held(b) for b in buffers])


def normalize(acts):
    values = acts.astype(F32)
    center = values - jnp.mean(values, axis=-1, keepdims=True)
    variance = jnp.mean(center * center, axis=-1, keepdims=True)
    inverse = 1.0 / jnp.sqrt(variance + 1e-05)
    return center * inverse, inverse


def project(x, gain, weight_ref, into, scaled):
    normed, _ = normalize(x)
    scaled[...] = (normed * gain).astype(BF16)
    width = weight_ref.shape[1]
    tile = width // 2
    for i in range(0, width, tile):
        here = slice(i, i + tile)
        product = jnp.dot(scaled[...], weight_ref[:, here], preferred_element_type=F32)
        into[:, here] = (x[:, here].astype(F32) + product).astype(BF16)


def pull_back(grad, x, gain, turned_ref, into, total, back):
    width = turned_ref.shape[1]
    tile = width // 2
    for i in range(0, width, tile):
        here = slice(i, i + tile)
        back[:, here] = jnp.dot(grad, turned_ref[:, here], preferred_element_type=F32)
    normed, inverse = normalize(x)
    back_proj = back[...]
    scaled = back_proj * gain
    mean_one = jnp.mean(scaled, axis=-1, keepdims=True)
    mean_two = jnp.mean(scaled * normed, axis=-1, keepdims=True)
    norm_grad = inverse * (scaled - mean_one - normed * mean_two)
    into[...] = (grad.astype(F32) + norm_grad).astype(BF16)
    total[...] = total[...] + jnp.sum(back_proj * normed, axis=0, keepdims=True)


def forward_kernel(tick, stages, state, fresh, received, gains, weights, _, *rest):
    sent, stash, scaled = rest[-3:]
    stage, core = state[0], state[1]
    part = tick - stage

    @pl.when((part >= 0) & (part < stash.shape[0]) & (stage < stages - 1))
    def _():
        x = jnp.where(stage == 0, fresh[...], received[...])
        stash[part, 0] = x
        project(x, gains[0:1, :], weights.at[core], stash.at[part, 1], scaled)
        project(stash[part, 1], gains[1:2, :], weights.at[1 - core], sent, scaled)


def forward(tick, stages, parts, state, fresh, received, gains, weights, turned, stash):
    operands = [state, fresh, received, gains, held(weights), held(turned)] + [held(b) for b in stash]
    return pl.pallas_call(
        functools.partial(forward_kernel, tick, stages),
        out_shape=[
            jax.ShapeDtypeStruct(fresh.shape, BF16),
            pltpu.VMEM((parts, 2) + fresh.shape, BF16),
        ],
        in_specs=[SMEM] + [VMEM] * (len(operands) - 1),
        out_specs=[VMEM] * 2,
        input_output_aliases={6: 1} if stash else {},
        scratch_shapes=[pltpu.VMEM(fresh.shape, BF16)],
        compiler_params=pltpu.CompilerParams(vmem_limit_bytes=LIMIT),
        name="forward",
    )(*operands)


def turn_kernel(part, stages, state, fresh, received, gains, weights, turned, *rest):
    sent, collected, totals, scaled, middle, back = rest[-6:]
    stage, core = state[0], state[1]
    if part == 0:
        totals[...] = jnp.zeros_like(totals)

    @pl.when(stage == stages - 1)
    def _():
        x = received[...]
        project(x, gains[0:1, :], weights.at[core], middle, scaled)
        pull_back(fresh[...], middle[...], gains[1:2, :], turned.at[1 - core], collected.at[part, 1], totals.at[1], back)
        pull_back(collected[part, 1], x, gains[0:1, :], turned.at[core], sent, totals.at[0], back)
        collected[part, 0] = sent[...]


def backward_kernel(tick, stages, state, received, leaving, stash, gains, turned, _, __, sent, collected, totals, back):
    stage, core = state[0], state[1]
    part = tick - (2 * stages - 2 - stage)
    active = (part >= 0) & (part < stash.shape[0]) & (stage < stages - 1)

    @pl.when(active)
    def _():
        pull_back(received[...], stash[part, 1], gains[1:2, :], turned.at[1 - core], collected.at[part, 1], totals.at[1], back)
        pull_back(collected[part, 1], stash[part, 0], gains[0:1, :], turned.at[core], sent, totals.at[0], back)
        collected[part, 0] = sent[...]

    @pl.when(stage == stages - 1)
    def _():
        sent[...] = leaving[...]


def backward(kernel, parts, operands, kept, scratch, name):
    rows, width = operands[1].shape
    count = len(operands)
    return pl.pallas_call(
        kernel,
        out_shape=[
            jax.ShapeDtypeStruct((rows, width), BF16),
            pltpu.VMEM((parts, 2, rows, width), BF16),
            pltpu.VMEM((2, 1, width), F32),
        ],
        in_specs=[SMEM] + [VMEM] * (count + len(kept) - 1),
        out_specs=[VMEM] * 3,
        input_output_aliases={count + i: 1 + i for i in range(len(kept))},
        scratch_shapes=scratch + [pltpu.VMEM((rows, width), F32)],
        compiler_params=pltpu.CompilerParams(vmem_limit_bytes=LIMIT),
        name=name,
    )(*operands, *[held(b) for b in kept])


def per_device(inputs, cotangent, weight, gain, momentum, prev_grads):
    sections = lax.axis_size("section")
    section = lax.axis_index("section")
    stages = sections // 2
    stage, core = section // 2, lax.rem(section, 2)
    batches, rows, width = inputs.shape
    parts = batches // 2
    siblings = [(i, i ^ 1) for i in range(sections)]

    def swap(array):
        return lax.ppermute(array, "section", siblings)

    def ordered(own, other, axis):
        return jnp.where(
            core == 0, jnp.concatenate([own, other], axis), jnp.concatenate([other, own], axis)
        )

    whole = lax.all_gather(weight[0], "dp", axis=0, tiled=True)

    bucket = prev_grads[0, 0].astype(BF16)
    pieces = lax.all_to_all(bucket, "dp", 0, 0, tiled=True).astype(F32)
    summed = jnp.sum(pieces, axis=0, keepdims=True)
    new_momentum = 0.9 * momentum + (summed / lax.axis_size("dp"))[None]

    gains = ordered(gain, swap(gain), 0)
    state = jnp.stack([stage, core]).astype(jnp.int32)
    fresh = lax.dynamic_slice_in_dim(inputs, core * parts, parts, 0)
    target = lax.dynamic_slice_in_dim(cotangent, core * parts, parts, 0)
    fresh = [fresh[m] for m in range(parts)]
    target = [target[m] for m in range(parts)]
    whole, new_momentum, gains, state, fresh, target = lax.optimization_barrier(
        (whole, new_momentum, gains, state, fresh, target)
    )
    received = fresh[0]
    incoming = target[0]
    weights, turned = place(whole, [])
    weights, turned = place(swap(whole), [weights, turned])

    def hops(tick, ahead):
        pairs = []
        for k in range(stages):
            to = k + 1 if ahead else k - 1
            part = tick - k if ahead else tick - (2 * stages - 2 - k)
            if 0 <= to < stages and 0 <= part < parts:
                pairs += [(2 * k + c, 2 * to + c) for c in range(2)]
        return pairs

    stash, kept = [], []
    for tick in range(2 * stages - 2 + parts):
        arrived, returned = received, incoming
        if tick < stages + parts - 2:
            sent, *stash = forward(
                tick, stages, parts, state, fresh[min(tick, parts - 1)], arrived, gains, weights, turned, stash
            )
            received = lax.ppermute(sent, "section", hops(tick, True))
        leaving = incoming
        m = tick - (stages - 1)
        if 0 <= m < parts:
            leaving, *kept = backward(
                functools.partial(turn_kernel, m, stages),
                parts,
                [state, target[m], arrived, gains, held(weights), held(turned)],
                kept,
                [pltpu.VMEM((rows, width), BF16)] * 2,
                "turn",
            )
        if tick >= stages:
            leaving, *kept = backward(
                functools.partial(backward_kernel, tick, stages),
                parts,
                [state, returned, leaving, held(stash[0]), gains, held(turned)],
                kept,
                [],
                "backward",
            )
        pairs = hops(tick, False)
        if pairs:
            incoming = lax.ppermute(leaving, "section", pairs)
    collected, totals = kept

    own = lax.dynamic_index_in_dim(collected, core, 1, keepdims=False)
    other = lax.dynamic_index_in_dim(collected, 1 - core, 1, keepdims=False)
    input_grads = ordered(own, swap(other), 0)[None]
    own_total = lax.dynamic_index_in_dim(totals, core, 0, keepdims=False)
    other_total = lax.dynamic_index_in_dim(totals, 1 - core, 0, keepdims=False)
    gain_grads = (own_total + swap(other_total))[None]
    return input_grads, gain_grads, new_momentum


def solution(mesh):
    in_specs = (
        P(None, "dp", None),
        P(None, "dp", None),
        P("section", "dp", None),
        P("section", None),
        P("section", "dp", None),
        P("section", "dp", None, None),
    )
    out_specs = (P("section", None, "dp", None), P("section", "dp", None), P("section", "dp", None))
    return jax.shard_map(per_device, mesh=mesh, in_specs=in_specs, out_specs=out_specs, check_vma=False)
```

time: 1070 us -> 467 us (0.44)
  waiting for transfers between devices: 619 us -> 302 us
  starting transfers between devices: 329 us -> 55.1 us
  local copies, waits for them, and re-layouts: 58.5 us -> 19.5 us
  Pallas kernels: 34.4 us -> 62 us
    ppermute x128 -> x20, waiting for transfers between devices: 450 us -> 135 us  [the longest x8 118 us: per_device(): incoming = lax.ppermute(leaving, 'section', pairs)]
    ppermute x128 -> x20, starting transfers between devices: 312 us -> 44.8 us  [the longest x4 28.7 us: swap(): return lax.ppermute(array, 'section', siblings)]
    cond x80 -> x0, local copies, waits for them, and re-layouts: 38.6 us -> none
    pallas_call x9 -> x20, Pallas kernels: 34.4 us -> 62 us  [the longest x10 23.3 us: backward(): pl.pallas_call(kernel, out_shape=[jax.ShapeDtypeStruct((rows, width), BF1...]
  transfers between devices with their start and end apart: 130 -> 22, of which waited for: 58 -> 8; matrix products, arithmetic and copies ran while one was open for 1% -> 2% of each run, Pallas kernels for 2% -> 3%
where the time goes in v2:
time: 467 us; the launch traced here: 460 us
  waiting for transfers between devices  302 us (65%)
  Pallas kernels  62 us (13%)
  starting transfers between devices  55.1 us (12%)
  local copies, waits for them, and re-layouts  19.5 us (4%)
  between operations  15 us (3%)
  other arithmetic  5.77 us (1%)
    all_gather x1, waiting for transfers between devices, per_device(): whole = lax.all_gather(weight[0], 'dp', axis=0, tiled=True)  157 us
    ppermute x8, waiting for transfers between devices, per_device(): incoming = lax.ppermute(leaving, 'section', pairs)  118 us
    ppermute x4, starting transfers between devices, swap(): return lax.ppermute(array, 'section', siblings)  28.7 us
    pallas_call x10, Pallas kernels, backward(): pl.pallas_call(kernel, out_shape=[jax.ShapeDtypeStruct((rows, width), BF1...  23.3 us
    pallas_call x2, Pallas kernels, place(): pl.pallas_call(functools.partial(place_kernel, step), out_shape=[pltpu.VM...  20.4 us
    pallas_call x8, Pallas kernels, forward(): pl.pallas_call(functools.partial(forward_kernel, tick, stages), out_shape...  18.3 us
    unnamed x8, local copies, waits for them, and re-layouts  17.7 us
    ppermute x4, waiting for transfers between devices, swap(): return lax.ppermute(array, 'section', siblings)  10.6 us
  transfers between devices with their start and end apart: 22, of which 8 were waited for; matrix products, arithmetic and copies ran while one was open for 2% of the time, Pallas kernels for 3%

profile of v2, /device:TPU:1, one launch (start us, length us, event | category | flops | bytes accessed | tf_op | source)
XLA Modules:
  0.0 459.6 jit_solution(8537144745297563876)
XLA Ops:
  7.9 8.8 %collective-permute-start = (f32[1,2560]{1,0:T(1,128)}, f32[1,2560]{1,0:T(1,128)S(1)}, u32[]{:S(2)}, u32[]{:S(2)}) collective-permute-start(f32[1,2560]{1,0:T(1,128)} %param.9), channel_id=1, source_target_pairs={{0,32},{32,0},{64,96},{96,64},{128,160},{160,128},{192,224},{224,1... | collective-permute-start | bytes 30728 | tf_op jit(solution)/shard_map/ppermute | solution.py:184
  16.7 1.0 convert_bitcast_fusion
  19.6 10.3 %all-to-all-start = ((bf16[32,2,1280]{2,1,0:T(2,128)(2,1)}), bf16[32,2,1280]{2,1,0:T(2,128)(2,1)S(1)}, u32[]{:S(2)}, u32[]{:S(2)}) async-start(bf16[32,2,1280]{2,1,0:T(2,128)(2,1)} %reshape.89), calls=%async_computation | async-start | bytes 327680 | tf_op jit(solution)/shard_map/all_to_all | solution.py:194
  29.9 1.2 dynamic-slice_bitcast_fusion.2
  32.1 9.6 %all-to-all-done = bf16[32,2,1280]{2,1,0:T(2,128)(2,1)S(1)} async-done(((bf16[32,2,1280]{2,1,0:T(2,128)(2,1)}), bf16[32,2,1280]{2,1,0:T(2,128)(2,1)S(1)}, u32[]{:S(2)}, u32[]{:S(2)}) %all-to-all-start) | async-done | bytes 163872 | tf_op jit(solution)/shard_map/all_to_all | solution.py:194
  42.1 1.3 reshape_add_fusion
  43.4 156.9 %all-gather.3.cloned.1.call-done = bf16[1,2560,2560]{2,1,0:T(8,128)(2,1)} async-done(((bf16[1,80,2560]{2,1,0:T(8,128)(2,1)}), bf16[1,2560,2560]{2,1,0:T(8,128)(2,1)}) %all-gather.3.cloned.1.call-update) | async-done | bytes 13107216 | tf_op jit(solution)/shard_map/all_gather | solution.py:191
  200.4 3.0 collective-permute-start.1
  203.3 10.2 %place_weight.2 = (bf16[2,2560,2560]{2,1,0:T(8,128)(2,1)S(1)}, bf16[2,2560,2560]{2,1,0:T(8,128)(2,1)S(1)}) custom-call(bf16[2560,2560]{1,0:T(8,128)(2,1)} %bitcast.27), custom_call_target="tpu_custom_call" | custom-call | tf_op jit(solution)/shard_map/place_weight/pallas_call | solution.py:47
  213.6 9.6 %collective-permute-done.1.source = bf16[2560,2560]{1,0:T(8,128)(2,1)} collective-permute-done((bf16[2560,2560]{1,0:T(8,128)(2,1)}, bf16[2560,2560]{1,0:T(8,128)(2,1)}, u32[]{:S(2)}, u32[]{:S(2)}) %collective-permute-start.1) | collective-permute-done | bytes 13107232 | tf_op jit(solution)/shard_map/ppermute | solution.py:184
  223.2 10.2 %place_weight.3 = (bf16[2,2560,2560]{2,1,0:T(8,128)(2,1)S(1)}, bf16[2,2560,2560]{2,1,0:T(8,128)(2,1)S(1)}) custom-call(bf16[2560,2560]{1,0:T(8,128)(2,1)} %collective-permute-done.1.source, bf16[2,2560,2560]{2,1,0:T(8,128)(2,1)S(1)} %get-tuple-element.66.rest_0_, ...), custom_call_target="tpu_custom_call", output_to_operand_aliasing={{0}: (1, {}), {1}: (2, {})} | custom-call | tf_op jit(solution)/shard_map/place_weight/pallas_call | solution.py:47
  233.4 5.6 %forward.8 = (bf16[32,2560]{1,0:T(8,128)(2,1)S(1)}, bf16[2,2,32,2560]{3,2,1,0:T(8,128)(2,1)S(1)}) custom-call(s32[2]{0:T(128)S(1)} %pad_add_fusion.state, bf16[32,2560]{1,0:T(8,128)(2,1)S(1)} %get-tuple-element.63.fresh.received, bf16[32,2560]{1,0:T(8,128)(2,1)S(1)} %get-tuple-element.63.fresh.received, f32[2,2560]{1,0:T(2,128)S(1)} %maximum_select_fusion.1.gains, ...), custom_call_target="tpu_custom_call" | custom-call | tf_op jit(solution)/shard_map/forward/pallas_call | solution.py:109
  239.1 1.3 collective-permute-start.2
  240.4 3.5 collective-permute-done.2.received
  243.9 5.6 %forward.9 = (bf16[32,2560]{1,0:T(8,128)(2,1)S(1)}, bf16[2,2,32,2560]{3,2,1,0:T(8,128)(2,1)S(1)}) custom-call(s32[2]{0:T(128)S(1)} %pad_add_fusion.state, bf16[32,2560]{1,0:T(8,128)(2,1)S(1)} %get-tuple-element.62.fresh, bf16[32,2560]{1,0:T(8,128)(2,1)S(1)} %collective-permute-done.2.received, ...), custom_call_target="tpu_custom_call", output_to_operand_aliasing={{1}: (6, {})} | custom-call | tf_op jit(solution)/shard_map/forward/pallas_call | solution.py:109
  249.5 4.1 collective-permute-start.3
  253.7 2.6 collective-permute-done.3.received
  260.2 4.0 forward.13
  267.4 3.8 turn.2
  272.5 8.4 %copy-done.1 = bf16[2,2560,2560]{2,1,0:T(8,128)(2,1)S(1)} copy-done((bf16[2,2560,2560]{2,1,0:T(8,128)(2,1)S(1)}, bf16[2,2560,2560]{2,1,0:T(8,128)(2,1)}, u32[]{:S(2)}) %copy-start.1) | copy-done | bytes 26214424
  286.2 4.3 backward.12
  291.7 1.3 collective-permute-start.16
  293.0 111.8 %collective-permute-done.16.received.leaving = bf16[32,2560]{1,0:T(8,128)(2,1)S(1)} collective-permute-done((bf16[32,2560]{1,0:T(8,128)(2,1)S(1)}, bf16[32,2560]{1,0:T(8,128)(2,1)S(1)}, u32[]{:S(2)}, u32[]{:S(2)}) %collective-permute-start.16) | collective-permute-done | bytes 163872 | tf_op jit(solution)/shard_map/ppermute | solution.py:251
  404.8 5.5 %backward.14 = (bf16[32,2560]{1,0:T(8,128)(2,1)S(1)}, bf16[2,2,32,2560]{3,2,1,0:T(8,128)(2,1)S(1)}, f32[2,1,2560]{2,1,0:T(1,128)S(1)}) custom-call(s32[2]{0:T(128)S(1)} %pad_add_fusion.state, bf16[32,2560]{1,0:T(8,128)(2,1)S(1)} %collective-permute-done.16.received.leaving, ...), custom_call_target="tpu_custom_call", output_to_operand_aliasing={{1}: (6, {}), {2}: (7, {})} | custom-call | tf_op jit(solution)/shard_map/backward/pallas_call | solution.py:158
  410.3 1.3 collective-permute-start.17
  411.6 6.5 %collective-permute-done.17.received.leaving = bf16[32,2560]{1,0:T(8,128)(2,1)S(1)} collective-permute-done((bf16[32,2560]{1,0:T(8,128)(2,1)S(1)}, bf16[32,2560]{1,0:T(8,128)(2,1)S(1)}, u32[]{:S(2)}, u32[]{:S(2)}) %collective-permute-start.17) | collective-permute-done | bytes 163872 | tf_op jit(solution)/shard_map/ppermute | solution.py:251
  418.1 8.5 %copy-done.2 = bf16[2,2560,2560]{2,1,0:T(8,128)(2,1)S(1)} copy-done((bf16[2,2560,2560]{2,1,0:T(8,128)(2,1)S(1)}, bf16[2,2560,2560]{2,1,0:T(8,128)(2,1)}, u32[]{:S(2)}) %copy-start.2) | copy-done | bytes 26214424
  426.6 6.2 %backward.15 = (bf16[32,2560]{1,0:T(8,128)(2,1)}, bf16[2,2,32,2560]{3,2,1,0:T(8,128)(2,1)S(1)}, f32[2,1,2560]{2,1,0:T(1,128)S(1)}) custom-call(s32[2]{0:T(128)S(1)} %pad_add_fusion.state, bf16[32,2560]{1,0:T(8,128)(2,1)S(1)} %collective-permute-done.17.received.leaving, ...), custom_call_target="tpu_custom_call", output_to_operand_aliasing={{1}: (6, {}), {2}: (7, {})} | custom-call | tf_op jit(solution)/shard_map/backward/pallas_call | solution.py:158
  432.7 15.0 %collective-permute-start.19 = (f32[1,2560]{1,0:T(1,128)S(1)}, f32[1,2560]{1,0:T(1,128)S(1)}, u32[]{:S(2)}, u32[]{:S(2)}) collective-permute-start(f32[1,2560]{1,0:T(1,128)S(1)} %dynamic-slice_bitcast_fusion.6), channel_id=1, source_target_pairs={{0,32},{32,0},{64,96},{96,64},{128,160},{160,128},{192,224},{224,1... | collective-permute-start | bytes 30728 | tf_op jit(solution)/shard_map/ppermute | solution.py:184
  447.8 1.9 collective-permute-start.18
  450.4 1.0 collective-permute-done.18
  451.3 0.9 maximum_select_fusion
  (54 shorter events, 19.3 us)
Async XLA Ops:
  7.2 193.2 %all-gather.3.cloned.1.call-start = ((), (), s32[]{:S(2)}) async-start(), calls=%async_computation.1 | async-start | bytes 13516800 | tf_op jit(solution)/shard_map/all_gather | solution.py:191
  7.9 23.3 %collective-permute-start = (f32[1,2560]{1,0:T(1,128)}, f32[1,2560]{1,0:T(1,128)S(1)}, u32[]{:S(2)}, u32[]{:S(2)}) collective-permute-start(f32[1,2560]{1,0:T(1,128)} %param.9), channel_id=1, source_target_pairs={{0,32},{32,0},{64,96},{96,64},{128,160},{160,128},{192,224},{224,1... | collective-permute-start | bytes 30728 | tf_op jit(solution)/shard_map/ppermute | solution.py:184
  19.6 22.0 %all-to-all-start = ((bf16[32,2,1280]{2,1,0:T(2,128)(2,1)}), bf16[32,2,1280]{2,1,0:T(2,128)(2,1)S(1)}, u32[]{:S(2)}, u32[]{:S(2)}) async-start(bf16[32,2,1280]{2,1,0:T(2,128)(2,1)} %reshape.89), calls=%async_computation | async-start | bytes 327680 | tf_op jit(solution)/shard_map/all_to_all | solution.py:194
  200.4 22.8 %collective-permute-start.1 = (bf16[2560,2560]{1,0:T(8,128)(2,1)}, bf16[2560,2560]{1,0:T(8,128)(2,1)}, u32[]{:S(2)}, u32[]{:S(2)}) collective-permute-start(bf16[2560,2560]{1,0:T(8,128)(2,1)} %bitcast.26), channel_id=1, source_target_pairs={{0,32},{32,0},{64,96},{96,64},{128,160},{160,128},{192,224},{224,1... | collective-permute-start | bytes 39321608 | tf_op jit(solution)/shard_map/ppermute | solution.py:184
  233.4 38.5 %copy-start = (bf16[2,2560,2560]{2,1,0:T(8,128)(2,1)}, bf16[2,2560,2560]{2,1,0:T(8,128)(2,1)S(1)}, u32[]{:S(2)}) copy-start(bf16[2,2560,2560]{2,1,0:T(8,128)(2,1)S(1)} %get-tuple-element.69._.turned) | copy-start | bytes 78643200
  239.1 4.8 %collective-permute-start.2 = (bf16[32,2560]{1,0:T(8,128)(2,1)S(1)}, bf16[32,2560]{1,0:T(8,128)(2,1)S(1)}, u32[]{:S(2)}, u32[]{:S(2)}) collective-permute-start(bf16[32,2560]{1,0:T(8,128)(2,1)S(1)} %get-tuple-element.70), channel_id=1, source_target_pairs={{0,64},{32,96},{1,65},{33,97},{2,66},{34,98},{3,67},{35,99},{4,68}... | collective-permute-start | bytes 491528 | tf_op jit(solution)/shard_map/ppermute | solution.py:228
  249.5 6.7 %collective-permute-start.3 = (bf16[32,2560]{1,0:T(8,128)(2,1)S(1)}, bf16[32,2560]{1,0:T(8,128)(2,1)S(1)}, u32[]{:S(2)}, u32[]{:S(2)}) collective-permute-start(bf16[32,2560]{1,0:T(8,128)(2,1)S(1)} %get-tuple-element.72), channel_id=1, source_target_pairs={{0,64},{32,96},{64,128},{96,160},{1,65},{33,97},{65,129},{97,161},... | collective-permute-start | bytes 491528 | tf_op jit(solution)/shard_map/ppermute | solution.py:228
  257.0 0.7 collective-permute-start.4
  258.3 0.7 collective-permute-start.5
  259.5 0.7 collective-permute-start.6
  264.2 0.7 collective-permute-start.7
  265.5 0.7 collective-permute-start.8
  266.7 5.2 %collective-permute-start.10 = (bf16[32,2560]{1,0:T(8,128)(2,1)S(1)}, bf16[32,2560]{1,0:T(8,128)(2,1)S(1)}, u32[]{:S(2)}, u32[]{:S(2)}) collective-permute-start(bf16[32,2560]{1,0:T(8,128)(2,1)S(1)} %get-tuple-element.86), channel_id=1, source_target_pairs={{384,448},{416,480},{385,449},{417,481},{386,450},{418,482},{387,4... | collective-permute-start | bytes 491528 | tf_op jit(solution)/shard_map/ppermute | solution.py:228
  271.2 1.3 collective-permute-start.9
  272.5 8.5 %copy-start.1 = (bf16[2,2560,2560]{2,1,0:T(8,128)(2,1)S(1)}, bf16[2,2560,2560]{2,1,0:T(8,128)(2,1)}, u32[]{:S(2)}) copy-start(bf16[2,2560,2560]{2,1,0:T(8,128)(2,1)} %copy-done) | copy-start | bytes 78643200
  281.7 0.7 collective-permute-start.11
  283.0 0.7 collective-permute-start.12
  284.2 0.7 collective-permute-start.13
  285.5 0.7 collective-permute-start.14
  290.4 0.7 collective-permute-start.15
  291.7 113.1 %collective-permute-start.16 = (bf16[32,2560]{1,0:T(8,128)(2,1)S(1)}, bf16[32,2560]{1,0:T(8,128)(2,1)S(1)}, u32[]{:S(2)}, u32[]{:S(2)}) collective-permute-start(bf16[32,2560]{1,0:T(8,128)(2,1)S(1)} %get-tuple-element.108), channel_id=1, source_target_pairs={{64,0},{96,32},{128,64},{160,96},{65,1},{97,33},{129,65},{161,97},... | collective-permute-start | bytes 491528 | tf_op jit(solution)/shard_map/ppermute | solution.py:251
  410.3 7.8 %collective-permute-start.17 = (bf16[32,2560]{1,0:T(8,128)(2,1)S(1)}, bf16[32,2560]{1,0:T(8,128)(2,1)S(1)}, u32[]{:S(2)}, u32[]{:S(2)}) collective-permute-start(bf16[32,2560]{1,0:T(8,128)(2,1)S(1)} %get-tuple-element.111), channel_id=1, source_target_pairs={{64,0},{96,32},{65,1},{97,33},{66,2},{98,34},{67,3},{99,35},{68,4}... | collective-permute-start | bytes 491528 | tf_op jit(solution)/shard_map/ppermute | solution.py:251
  418.1 8.5 %copy-start.2 = (bf16[2,2560,2560]{2,1,0:T(8,128)(2,1)S(1)}, bf16[2,2560,2560]{2,1,0:T(8,128)(2,1)}, u32[]{:S(2)}) copy-start(bf16[2,2560,2560]{2,1,0:T(8,128)(2,1)} %copy-done) | copy-start | bytes 78643200
  432.7 17.0 %collective-permute-start.19 = (f32[1,2560]{1,0:T(1,128)S(1)}, f32[1,2560]{1,0:T(1,128)S(1)}, u32[]{:S(2)}, u32[]{:S(2)}) collective-permute-start(f32[1,2560]{1,0:T(1,128)S(1)} %dynamic-slice_bitcast_fusion.6), channel_id=1, source_target_pairs={{0,32},{32,0},{64,96},{96,64},{128,160},{160,128},{192,224},{224,1... | collective-permute-start | bytes 30728 | tf_op jit(solution)/shard_map/ppermute | solution.py:184
  447.8 3.5 collective-permute-start.18
Sparse Core Ops, SparseCore 0:
  11.2 189.1 all-gather.2

commit v3 on v2

v3 whole, which is shorter than its diff:
```python
import functools

import jax
import jax.numpy as jnp
from jax import lax
from jax.experimental import pallas as pl
from jax.experimental.pallas import tpu as pltpu
from jax.sharding import PartitionSpec as P

VMEM = pl.BlockSpec(memory_space=pltpu.VMEM)
SMEM = pl.BlockSpec(memory_space=pltpu.SMEM)
HBM = pl.BlockSpec(memory_space=pltpu.HBM)
BF16 = jnp.bfloat16
F32 = jnp.float32
LIMIT = 2 << 20


def held(array):
    return pltpu.with_memory_space_constraint(array, pltpu.VMEM)


def assemble_kernel(*refs):
    *pieces, out, stage, arrived, left = refs
    count = len(pieces) // 2
    copies = []
    for i in range(2):
        at = 0
        for piece in pieces[i * count : (i + 1) * count]:
            rows, columns = piece.shape
            here = (pl.ds(at, rows), pl.ds(i * columns, columns))
            n = len(copies)
            copies.append(
                (
                    pltpu.make_async_copy(piece, stage.at[here], arrived.at[n]),
                    pltpu.make_async_copy(stage.at[here], out.at[here], left.at[n]),
                )
            )
            at += rows
    for into, _ in copies:
        into.start()
    for into, onward in copies:
        into.wait()
        onward.start()
    for _, onward in copies:
        onward.wait()


def assemble(lefts, rights):
    pieces = [pltpu.with_memory_space_constraint(piece, pltpu.HBM) for piece in lefts + rights]
    shape = (sum(piece.shape[0] for piece in lefts), 2 * lefts[0].shape[1])
    return pl.pallas_call(
        assemble_kernel,
        out_shape=pltpu.HBM(shape, BF16),
        in_specs=[HBM] * len(pieces),
        out_specs=HBM,
        scratch_shapes=[pltpu.VMEM(shape, BF16)] + [pltpu.SemaphoreType.DMA((len(pieces),))] * 2,
        compiler_params=pltpu.CompilerParams(vmem_limit_bytes=16 << 20),
        name="assemble",
    )(*pieces)


def place_kernel(layouts, state, *rest):
    weights, sems = rest[-3], rest[-1]
    row, col = state[2], state[3]
    height = weights.shape[1] // 32
    copies = []
    for source, (slot, shifts) in zip(rest, layouts):
        for i, shift in enumerate(shifts):
            for j, across in enumerate((0, -1, 1, -2)):
                replica = lax.rem(row + across + 4, 4) * 8 + lax.rem(col + shift + 8, 8)
                into = weights.at[slot, pl.ds(pl.multiple_of(replica * height, 16), height), :]
                at = (i * 4 + j) * height
                copies.append(pltpu.make_async_copy(source.at[at : at + height, :], into, sems.at[len(copies)]))
    for copy in copies:
        copy.start()
    for copy in copies:
        copy.wait()


def place(state, layouts, pieces, buffers):
    width = pieces[0].shape[1]
    pieces = [pltpu.with_memory_space_constraint(piece, pltpu.HBM) for piece in pieces]
    copies = 4 * sum(len(shifts) for _, shifts in layouts)
    return pl.pallas_call(
        functools.partial(place_kernel, layouts),
        out_shape=[pltpu.VMEM((2, width, width), BF16)] * 2,
        in_specs=[SMEM] + [HBM] * len(pieces) + [VMEM] * len(buffers),
        out_specs=[VMEM] * 2,
        input_output_aliases={1 + len(pieces) + i: i for i in range(len(buffers))},
        scratch_shapes=[pltpu.SemaphoreType.DMA((copies,))],
        compiler_params=pltpu.CompilerParams(vmem_limit_bytes=LIMIT),
        name="place_weight",
    )(state, *pieces, *[held(b) for b in buffers])


def pack_kernel(collected, totals, packed):
    parts, rows = collected.shape[1:3]
    for m in range(parts):
        packed[m * rows : (m + 1) * rows, :] = collected[1, m]
    total = totals[1]
    head = total.astype(BF16).astype(F32)
    row = lax.broadcasted_iota(jnp.int32, (16, total.shape[1]), 0)
    tail = jnp.where(row == 0, head, jnp.where(row == 1, total - head, 0.0))
    packed[parts * rows :, :] = tail.astype(BF16)


def pack(collected, totals):
    _, parts, rows, width = collected.shape
    return pl.pallas_call(
        pack_kernel,
        out_shape=jax.ShapeDtypeStruct((parts * rows + 16, width), BF16),
        in_specs=[VMEM] * 2,
        out_specs=VMEM,
        compiler_params=pltpu.CompilerParams(vmem_limit_bytes=LIMIT),
        name="pack",
    )(held(collected), held(totals))


def transpose_kernel(early, state, weights, _, turned):
    step = 256
    count = weights.shape[1] // step

    @pl.when((state[0] <= 1) == early)
    def _():
        def turn(i, _):
            rows = pl.ds(pl.multiple_of(i * step, step), step)
            for slot in range(2):
                for j in range(0, count * step, step):
                    turned[slot, j : j + step, rows] = weights[slot, rows, j : j + step].T

        lax.fori_loop(0, count, turn, None)


def transpose(early, state, weights, turned):
    return pl.pallas_call(
        functools.partial(transpose_kernel, early),
        out_shape=pltpu.VMEM(weights.shape, BF16),
        in_specs=[SMEM] + [VMEM] * 2,
        out_specs=VMEM,
        input_output_aliases={2: 0},
        compiler_params=pltpu.CompilerParams(vmem_limit_bytes=LIMIT),
        name="transpose_weight",
    )(state, held(weights), held(turned))


def normalize(acts):
    values = acts.astype(F32)
    center = values - jnp.mean(values, axis=-1, keepdims=True)
    variance = jnp.mean(center * center, axis=-1, keepdims=True)
    inverse = 1.0 / jnp.sqrt(variance + 1e-05)
    return center * inverse, inverse


def project(x, gain, weight_ref, into, scaled):
    normed, _ = normalize(x)
    scaled[...] = (normed * gain).astype(BF16)
    width = weight_ref.shape[1]
    tile = width // 2
    for i in range(0, width, tile):
        here = slice(i, i + tile)
        product = jnp.dot(scaled[...], weight_ref[:, here], preferred_element_type=F32)
        into[:, here] = (x[:, here].astype(F32) + product).astype(BF16)


def pull_back(grad, x, gain, turned_ref, into, total, back):
    width = turned_ref.shape[1]
    tile = width // 2
    for i in range(0, width, tile):
        here = slice(i, i + tile)
        back[:, here] = jnp.dot(grad, turned_ref[:, here], preferred_element_type=F32)
    normed, inverse = normalize(x)
    back_proj = back[...]
    scaled = back_proj * gain
    mean_one = jnp.mean(scaled, axis=-1, keepdims=True)
    mean_two = jnp.mean(scaled * normed, axis=-1, keepdims=True)
    norm_grad = inverse * (scaled - mean_one - normed * mean_two)
    into[...] = (grad.astype(F32) + norm_grad).astype(BF16)
    total[...] = total[...] + jnp.sum(back_proj * normed, axis=0, keepdims=True)


def forward_kernel(k, part, state, arrived, gains, weights, *rest):
    sent, stash, scaled = rest[-3:]
    core = state[1]

    @pl.when(state[0] == k)
    def _():
        x = arrived[...]
        stash[part, 0] = x
        project(x, gains[0:1, :], weights.at[core], stash.at[part, 1], scaled)
        project(stash[part, 1], gains[1:2, :], weights.at[1 - core], sent, scaled)


def forward(k, part, parts, state, arrived, gains, weights, turned, stash):
    operands = [state, arrived, gains, held(weights), held(turned)] + [held(b) for b in stash]
    return pl.pallas_call(
        functools.partial(forward_kernel, k, part),
        out_shape=[
            jax.ShapeDtypeStruct(arrived.shape, BF16),
            pltpu.VMEM((parts, 2) + arrived.shape, BF16),
        ],
        in_specs=[SMEM] + [VMEM] * (len(operands) - 1),
        out_specs=[VMEM] * 2,
        input_output_aliases={5: 1} if stash else {},
        scratch_shapes=[pltpu.VMEM(arrived.shape, BF16)],
        compiler_params=pltpu.CompilerParams(vmem_limit_bytes=LIMIT),
        name="forward",
    )(*operands)


def turn_kernel(part, stages, state, fresh, received, gains, weights, turned, *rest):
    sent, collected, totals, scaled, middle, back = rest[-6:]
    stage, core = state[0], state[1]
    if part == 0:
        totals[...] = jnp.zeros_like(totals)

    @pl.when(stage == stages - 1)
    def _():
        x = received[...]
        project(x, gains[0:1, :], weights.at[core], middle, scaled)
        pull_back(
            fresh[...], middle[...], gains[1:2, :], turned.at[1 - core], collected.at[1 - core, part], totals.at[1 - core], back
        )
        pull_back(collected[1 - core, part], x, gains[0:1, :], turned.at[core], sent, totals.at[core], back)
        collected[core, part] = sent[...]


def backward_kernel(k, part, state, received, stash, gains, turned, *rest):
    sent, collected, totals, back = rest[-4:]
    core = state[1]

    @pl.when(state[0] == k)
    def _():
        pull_back(
            received[...], stash[part, 1], gains[1:2, :], turned.at[1 - core], collected.at[1 - core, part], totals.at[1 - core], back
        )
        pull_back(collected[1 - core, part], stash[part, 0], gains[0:1, :], turned.at[core], sent, totals.at[core], back)
        collected[core, part] = sent[...]


def backward(kernel, parts, operands, kept, scratch, name):
    rows, width = operands[1].shape
    count = len(operands)
    return pl.pallas_call(
        kernel,
        out_shape=[
            jax.ShapeDtypeStruct((rows, width), BF16),
            pltpu.VMEM((2, parts, rows, width), BF16),
            pltpu.VMEM((2, 1, width), F32),
        ],
        in_specs=[SMEM] + [VMEM] * (count + len(kept) - 1),
        out_specs=[VMEM] * 3,
        input_output_aliases={count + i: 1 + i for i in range(len(kept))},
        scratch_shapes=scratch + [pltpu.VMEM((rows, width), F32)],
        compiler_params=pltpu.CompilerParams(vmem_limit_bytes=LIMIT),
        name=name,
    )(*operands, *[held(b) for b in kept])


def per_device(inputs, cotangent, weight, gain, momentum, prev_grads):
    sections = lax.axis_size("section")
    section = lax.axis_index("section")
    stages = sections // 2
    stage, core = section // 2, lax.rem(section, 2)
    batches, rows, width = inputs.shape
    parts = batches // 2
    siblings = [(i, i ^ 1) for i in range(sections)]

    def swap(array):
        return lax.ppermute(array, "section", siblings)

    def ordered(own, other):
        return jnp.where(core == 0, jnp.concatenate([own, other], 0), jnp.concatenate([other, own], 0))

    def unpacked(block):
        return block[0:1].astype(F32) + block[1:2].astype(F32)

    def over(array, rows, columns):
        pairs = [
            (y * 8 + z, ((y + rows) % 4) * 8 + (z + columns) % 8) for y in range(4) for z in range(8)
        ]
        return lax.ppermute(array, "dp", pairs)

    def first_block(shard):
        above, below = over(shard, 1, 0), over(shard, -1, 0)
        return jnp.concatenate([shard, above, below, over(above, 1, 0)], 0)

    bucket = prev_grads[0, 0].astype(BF16)
    pieces = lax.all_to_all(bucket, "dp", 0, 0, tiled=True).astype(F32)
    summed = jnp.sum(pieces, axis=0, keepdims=True)
    new_momentum = 0.9 * momentum + (summed / lax.axis_size("dp"))[None]

    half = width // 2
    shards = [weight[0, :, :half], weight[0, :, half:]]
    shards[1], new_momentum = lax.optimization_barrier((shards[1], new_momentum))
    blocks = [first_block(shard) for shard in shards]
    rings = [[(block, block)] for block in blocks]
    for step in range(3):
        for ring in rings:
            right, left = ring[-1]
            ring.append(lax.optimization_barrier((over(right, 0, 1), over(left, 0, -1))))
    ends = [over(rings[0][3][0], 0, 1), over(rings[1][3][1], 0, -1)]
    inner = [[ring[0][0], *ring[1], *ring[2]] for ring in rings]
    inner, rings[0][3], rings[1][3] = lax.optimization_barrier((inner, rings[0][3], rings[1][3]))
    inner = assemble(*inner)
    inner_other = swap(inner)

    outer = assemble(*[[*ring[3], end] for ring, end in zip(rings, ends)])
    outer_other = swap(outer)

    gains = ordered(gain, swap(gain))
    replica = lax.axis_index("dp")
    state = jnp.stack([stage, core, replica // 8, lax.rem(replica, 8)]).astype(jnp.int32)
    fresh = lax.dynamic_slice_in_dim(inputs, core * parts, parts, 0)
    target = lax.dynamic_slice_in_dim(cotangent, core * parts, parts, 0)
    fresh = [fresh[m] for m in range(parts)]
    target = [target[m] for m in range(parts)]
    gains, state, fresh, target, outer = lax.optimization_barrier((gains, state, fresh, target, outer))
    near, far = (0, -1, 1, -2, 2), (-3, 3, 4)
    buffers = place(state, ((0, near), (0, far), (1, near)), [inner, outer, inner_other], [])
    weights, turned = place(state, ((1, far),), [outer_other], buffers)
    turned = transpose(False, state, weights, turned)

    def hop(array, k, to, after):
        if after is not None:
            array, after = lax.optimization_barrier((array, after))
        return lax.ppermute(array, "section", [(2 * k + c, 2 * to + c) for c in range(2)])

    arrived = fresh
    stash, kept = [], []
    for k in range(stages - 1):
        landed = []
        for m in range(parts):
            sent, *stash = forward(k, m, parts, state, arrived[m], gains, weights, turned, stash)
            landed.append(hop(sent, k, k + 1, landed[-1] if landed else None))
        arrived = landed
        if k == 3:
            turned = transpose(True, state, weights, turned)
    for k in range(stages - 1, -1, -1):
        landed = []
        for m in range(parts):
            if k == stages - 1:
                kernel, scratch = functools.partial(turn_kernel, m, stages), [pltpu.VMEM((rows, width), BF16)] * 2
                operands = [state, target[m], arrived[m], gains, held(weights), held(turned)]
            else:
                kernel, scratch = functools.partial(backward_kernel, k, m), []
                operands = [state, arrived[m], held(stash[0]), gains, held(turned), held(weights)]
            leaving, *kept = backward(kernel, parts, operands, kept, scratch, "turn" if scratch else "backward")
            if k > 0:
                landed.append(hop(leaving, k, k - 1, landed[-1] if landed else None))
        arrived = landed
    collected, totals = kept

    other = swap(pack(collected, totals))
    input_grads = ordered(collected[0], other[: parts * rows].reshape(parts, rows, width))[None]
    gain_grads = (totals[0] + unpacked(other[parts * rows :]))[None]

    return input_grads, gain_grads, new_momentum


def solution(mesh):
    in_specs = (
        P(None, "dp", None),
        P(None, "dp", None),
        P("section", "dp", None),
        P("section", None),
        P("section", "dp", None),
        P("section", "dp", None, None),
    )
    out_specs = (P("section", None, "dp", None), P("section", "dp", None), P("section", "dp", None))
    return jax.shard_map(per_device, mesh=mesh, in_specs=in_specs, out_specs=out_specs, check_vma=False)
```

time: 467 us -> 431 us (0.923)
  waiting for transfers between devices: 302 us -> 184 us
  starting transfers between devices: 55.1 us -> 138 us
  Pallas kernels: 62 us -> 90.5 us
  local copies, waits for them, and re-layouts: 19.5 us -> 3.57 us
  between operations: 15 us -> 2.09 us
    all_gather x1 -> x0, waiting for transfers between devices: 157 us -> none  [per_device(): whole = lax.all_gather(weight[0], 'dp', axis=0, tiled=True)]
    ppermute x16 -> x48, starting transfers between devices: 16.1 us -> 88.1 us  [the longest x20 64 us: over(): return lax.ppermute(array, 'dp', pairs)]
    ppermute x16 -> x48, waiting for transfers between devices: 124 us -> 177 us  [the longest x28 91.5 us: hop(): lax.ppermute(array, 'section', [(2 * k + c, 2 * to + c) for c in range(2)])]
    pallas_call x10 -> x21, Pallas kernels: 38.7 us -> 55.4 us  [the longest x14 24.6 us: forward(): pl.pallas_call(functools.partial(forward_kernel, k, part), out_shape=[jax...]
    unnamed x8 -> x43, local copies, waits for them, and re-layouts: 17.7 us -> 1.89 us
    pallas_call x10 -> x16, Pallas kernels: 23.3 us -> 35.1 us  [backward(): pl.pallas_call(kernel, out_shape=[jax.ShapeDtypeStruct((rows, width), BF1...]
    all_to_all x1, waiting for transfers between devices: 9.6 us -> 0.01 us  [per_device(): pieces = lax.all_to_all(bucket, 'dp', 0, 0, tiled=True).astype(F32)]
    all_to_all x1, starting transfers between devices: 10.3 us -> 16.5 us  [per_device(): pieces = lax.all_to_all(bucket, 'dp', 0, 0, tiled=True).astype(F32)]
  transfers between devices with their start and end apart: 22 -> 53, of which waited for: 8 -> 15; matrix products, arithmetic and copies ran while one was open for 2% -> 1% of each run, Pallas kernels for 3% -> 16%
where the time goes in v3:
time: 431 us; the launch traced here: 423 us
  waiting for transfers between devices  184 us (43%)
  starting transfers between devices  138 us (32%)
  Pallas kernels  90.5 us (21%)
  other arithmetic  5.03 us (1%)
    ppermute x28, waiting for transfers between devices, hop(): lax.ppermute(array, 'section', [(2 * k + c, 2 * to + c) for c in range(2)])  91.5 us
    ppermute x20, waiting for transfers between devices, over(): return lax.ppermute(array, 'dp', pairs)  85.8 us
    ppermute x20, starting transfers between devices, over(): return lax.ppermute(array, 'dp', pairs)  64 us
    pallas_call x16, Pallas kernels, backward(): pl.pallas_call(kernel, out_shape=[jax.ShapeDtypeStruct((rows, width), BF1...  35.1 us
    ppermute x4, starting transfers between devices, swap(): return lax.ppermute(array, 'section', siblings)  33.1 us
    pallas_call x14, Pallas kernels, forward(): pl.pallas_call(functools.partial(forward_kernel, k, part), out_shape=[jax...  24.6 us
    ppermute x28, starting transfers between devices, hop(): lax.ppermute(array, 'section', [(2 * k + c, 2 * to + c) for c in range(2)])  24.1 us
    all_to_all x1, starting transfers between devices, per_device(): pieces = lax.all_to_all(bucket, 'dp', 0, 0, tiled=True).astype(F32)  16.5 us
  transfers between devices with their start and end apart: 53, of which 15 were waited for; matrix products, arithmetic and copies ran while one was open for 1% of the time, Pallas kernels for 16%

profile of v3, /device:TPU:1, one launch (start us, length us, event | category | flops | bytes accessed | tf_op | source)
XLA Modules:
  0.0 423.2 jit_solution(3911843486816243510)
XLA Ops:
  3.5 16.5 %all-to-all-start = ((bf16[32,2,1280]{2,1,0:T(2,128)(2,1)}), bf16[32,2,1280]{2,1,0:T(2,128)(2,1)S(1)}, u32[]{:S(2)}, u32[]{:S(2)}) async-start(bf16[32,2,1280]{2,1,0:T(2,128)(2,1)} %reshape.85), calls=%async_computation | async-start | bytes 327680 | tf_op jit(solution)/shard_map/all_to_all | solution.py:288
  28.5 4.6 %collective-permute-done.1 = bf16[80,1280]{1,0:T(8,128)(2,1)S(1)} collective-permute-done((bf16[80,1280]{1,0:T(8,128)(2,1)S(1)}, bf16[80,1280]{1,0:T(8,128)(2,1)S(1)}, u32[]{:S(2)}, u32[]{:S(2)}) %collective-permute-start.1) | collective-permute-done | bytes 204832 | tf_op jit(solution)/shard_map/ppermute | solution.py:281
  36.8 5.5 %collective-permute-start.9 = (bf16[80,1280]{1,0:T(8,128)(2,1)S(1)}, bf16[80,1280]{1,0:T(8,128)(2,1)S(1)}, u32[]{:S(2)}, u32[]{:S(2)}) collective-permute-start(bf16[80,1280]{1,0:T(8,128)(2,1)S(1)} %get-tuple-element.134), channel_id=1, source_target_pairs={{0,24},{1,25},{2,26},{3,27},{4,28},{5,29},{6,30},{7,31},{8,0},{9,1... | collective-permute-start | bytes 614408 | tf_op jit(solution)/shard_map/ppermute | solution.py:281
  55.6 6.2 %collective-permute-done.10 = bf16[80,1280]{1,0:T(8,128)(2,1)S(1)} collective-permute-done((bf16[80,1280]{1,0:T(8,128)(2,1)S(1)}, bf16[80,1280]{1,0:T(8,128)(2,1)S(1)}, u32[]{:S(2)}, u32[]{:S(2)}) %collective-permute-start.10) | collective-permute-done | bytes 204832 | tf_op jit(solution)/shard_map/ppermute | solution.py:281
  61.8 4.3 %collective-permute-start.12 = (bf16[320,1280]{1,0:T(8,128)(2,1)S(1)}, bf16[320,1280]{1,0:T(8,128)(2,1)S(1)}, u32[]{:S(2)}, u32[]{:S(2)}) collective-permute-start(bf16[320,1280]{1,0:T(8,128)(2,1)S(1)} %constant_dynamic-update-slice_fusion.refs_5_), channel_id=1, source_target_pairs={{0,7},{1,0},{2,1},{3,2},{4,3},{5,4},{6,5},{7,6},{8,15},{9,8},{10,9... | collective-permute-start | bytes 2457608 | tf_op jit(solution)/shard_map/ppermute | solution.py:281
  70.1 4.4 %collective-permute-start.7 = (bf16[320,1280]{1,0:T(8,128)(2,1)S(1)}, bf16[320,1280]{1,0:T(8,128)(2,1)S(1)}, u32[]{:S(2)}, u32[]{:S(2)}) collective-permute-start(bf16[320,1280]{1,0:T(8,128)(2,1)S(1)} %collective-permute-done.5.refs_2_), channel_id=1, source_target_pairs={{0,7},{1,0},{2,1},{3,2},{4,3},{5,4},{6,5},{7,6},{8,15},{9,8},{10,9... | collective-permute-start | bytes 2457608 | tf_op jit(solution)/shard_map/ppermute | solution.py:281
  75.4 5.0 %collective-permute-done.11.refs_6_ = bf16[320,1280]{1,0:T(8,128)(2,1)S(1)} collective-permute-done((bf16[320,1280]{1,0:T(8,128)(2,1)S(1)}, bf16[320,1280]{1,0:T(8,128)(2,1)S(1)}, u32[]{:S(2)}, u32[]{:S(2)}) %collective-permute-start.11) | collective-permute-done | bytes 819232 | tf_op jit(solution)/shard_map/ppermute | solution.py:281
  82.3 4.6 %collective-permute-start.14 = (bf16[320,1280]{1,0:T(8,128)(2,1)S(1)}, bf16[320,1280]{1,0:T(8,128)(2,1)S(1)}, u32[]{:S(2)}, u32[]{:S(2)}) collective-permute-start(bf16[320,1280]{1,0:T(8,128)(2,1)S(1)} %collective-permute-done.12.refs_7_), channel_id=1, source_target_pairs={{0,7},{1,0},{2,1},{3,2},{4,3},{5,4},{6,5},{7,6},{8,15},{9,8},{10,9... | collective-permute-start | bytes 2457608 | tf_op jit(solution)/shard_map/ppermute | solution.py:281
  86.9 9.8 %collective-permute-done.6.refs_3_ = bf16[320,1280]{1,0:T(8,128)(2,1)S(1)} collective-permute-done((bf16[320,1280]{1,0:T(8,128)(2,1)S(1)}, bf16[320,1280]{1,0:T(8,128)(2,1)S(1)}, u32[]{:S(2)}, u32[]{:S(2)}) %collective-permute-start.6) | collective-permute-done | bytes 819232 | tf_op jit(solution)/shard_map/ppermute | solution.py:281
  98.6 4.6 %collective-permute-start.16 = (bf16[320,1280]{1,0:T(8,128)(2,1)S(1)}, bf16[320,1280]{1,0:T(8,128)(2,1)S(1)}, u32[]{:S(2)}, u32[]{:S(2)}) collective-permute-start(bf16[320,1280]{1,0:T(8,128)(2,1)S(1)} %collective-permute-done.7.refs_4_), channel_id=1, source_target_pairs={{0,7},{1,0},{2,1},{3,2},{4,3},{5,4},{6,5},{7,6},{8,15},{9,8},{10,9... | collective-permute-start | bytes 2457608 | tf_op jit(solution)/shard_map/ppermute | solution.py:281
  103.2 11.0 %collective-permute-done.13.refs_8_ = bf16[320,1280]{1,0:T(8,128)(2,1)S(1)} collective-permute-done((bf16[320,1280]{1,0:T(8,128)(2,1)S(1)}, bf16[320,1280]{1,0:T(8,128)(2,1)S(1)}, u32[]{:S(2)}, u32[]{:S(2)}) %collective-permute-start.13) | collective-permute-done | bytes 819232 | tf_op jit(solution)/shard_map/ppermute | solution.py:281
  116.2 4.6 %collective-permute-start.18 = (bf16[320,1280]{1,0:T(8,128)(2,1)S(1)}, bf16[320,1280]{1,0:T(8,128)(2,1)S(1)}, u32[]{:S(2)}, u32[]{:S(2)}) collective-permute-start(bf16[320,1280]{1,0:T(8,128)(2,1)S(1)} %collective-permute-done.14.refs_9_), channel_id=1, source_target_pairs={{0,7},{1,0},{2,1},{3,2},{4,3},{5,4},{6,5},{7,6},{8,15},{9,8},{10,9... | collective-permute-start | bytes 2457608 | tf_op jit(solution)/shard_map/ppermute | solution.py:281
  120.7 11.0 %collective-permute-done.15.refs_0_ = bf16[320,1280]{1,0:T(8,128)(2,1)S(1)} collective-permute-done((bf16[320,1280]{1,0:T(8,128)(2,1)S(1)}, bf16[320,1280]{1,0:T(8,128)(2,1)S(1)}, u32[]{:S(2)}, u32[]{:S(2)}) %collective-permute-start.15) | collective-permute-done | bytes 819232 | tf_op jit(solution)/shard_map/ppermute | solution.py:281
  131.8 17.5 %collective-permute-done.17.refs_3_ = bf16[320,1280]{1,0:T(8,128)(2,1)S(1)} collective-permute-done((bf16[320,1280]{1,0:T(8,128)(2,1)S(1)}, bf16[320,1280]{1,0:T(8,128)(2,1)S(1)}, u32[]{:S(2)}, u32[]{:S(2)}) %collective-permute-start.17) | collective-permute-done | bytes 819232 | tf_op jit(solution)/shard_map/ppermute | solution.py:281
  149.5 7.1 %assemble.3.rest_0_ = bf16[1600,2560]{1,0:T(8,128)(2,1)} custom-call(bf16[320,1280]{1,0:T(8,128)(2,1)} %copy-done, bf16[320,1280]{1,0:T(8,128)(2,1)} %copy-done.9, bf16[320,1280]{1,0:T(8,128)(2,1)} %copy-done.8, bf16[320,1280]{1,0:T(8,128)(2,1)} %copy-done.12, bf16[320,1280]{1,0:T(8,128)(2,1)} %copy-done.13, bf16[320,1280]{1,0:T(8,128)(2,1)} %copy-done.1, ...), custom_call_target="tpu_custom_call" | custom-call | tf_op jit(solution)/shard_map/assemble/pallas_call | solution.py:51
  156.6 12.8 %collective-permute-start.22 = (bf16[1600,2560]{1,0:T(8,128)(2,1)}, bf16[1600,2560]{1,0:T(8,128)(2,1)}, u32[]{:S(2)}, u32[]{:S(2)}) collective-permute-start(bf16[1600,2560]{1,0:T(8,128)(2,1)} %assemble.3.rest_0_), channel_id=1, source_target_pairs={{0,32},{32,0},{64,96},{96,64},{128,160},{160,128},{192,224},{224,1... | collective-permute-start | bytes 24576008 | tf_op jit(solution)/shard_map/ppermute | solution.py:269
  171.3 4.6 %collective-permute-start.20 = (bf16[320,1280]{1,0:T(8,128)(2,1)S(1)}, bf16[320,1280]{1,0:T(8,128)(2,1)S(1)}, u32[]{:S(2)}, u32[]{:S(2)}) collective-permute-start(bf16[320,1280]{1,0:T(8,128)(2,1)S(1)} %collective-permute-done.18.refs_4_), channel_id=1, source_target_pairs={{0,7},{1,0},{2,1},{3,2},{4,3},{5,4},{6,5},{7,6},{8,15},{9,8},{10,9... | collective-permute-start | bytes 2457608 | tf_op jit(solution)/shard_map/ppermute | solution.py:281
  175.9 16.4 %collective-permute-done.19.refs_2_ = bf16[320,1280]{1,0:T(8,128)(2,1)S(1)} collective-permute-done((bf16[320,1280]{1,0:T(8,128)(2,1)S(1)}, bf16[320,1280]{1,0:T(8,128)(2,1)S(1)}, u32[]{:S(2)}, u32[]{:S(2)}) %collective-permute-start.19) | collective-permute-done | bytes 819232 | tf_op jit(solution)/shard_map/ppermute | solution.py:281
  194.2 4.2 assemble.2.rest_1_
  203.6 5.7 %collective-permute-done = f32[1,2560]{1,0:T(1,128)S(1)} collective-permute-done((f32[1,2560]{1,0:T(1,128)S(1)}, f32[1,2560]{1,0:T(1,128)S(1)}, u32[]{:S(2)}, u32[]{:S(2)}) %collective-permute-start) | collective-permute-done | bytes 10272 | tf_op jit(solution)/shard_map/ppermute | solution.py:269
  209.3 8.1 %place_weight.2 = (bf16[2,2560,2560]{2,1,0:T(8,128)(2,1)S(1)}, bf16[2,2560,2560]{2,1,0:T(8,128)(2,1)S(1)}) custom-call(s32[4]{0:T(128)S(1)} %pad_add_fusion.state, bf16[1600,2560]{1,0:T(8,128)(2,1)} %assemble.3.rest_0_, bf16[960,2560]{1,0:T(8,128)(2,1)} %assemble.2.rest_1_, bf16[1600,2560]{1,0:T(8,128)(2,1)} %collective-permute-done.22.rest_2_), custom_call_target="tpu_custom_call" | custom-call | tf_op jit(solution)/shard_map/place_weight/pallas_call | solution.py:84
  221.0 5.7 %forward.14 = (bf16[32,2560]{1,0:T(8,128)(2,1)S(1)}, bf16[2,2,32,2560]{3,2,1,0:T(8,128)(2,1)S(1)}) custom-call(s32[4]{0:T(128)S(1)} %pad_add_fusion.state, bf16[32,2560]{1,0:T(8,128)(2,1)S(1)} %get-tuple-element.166.arrived, f32[2,2560]{1,0:T(2,128)S(1)} %maximum_select_fusion.1.gains, bf16[2,2560,2560]{2,1,0:T(8,128)(2,1)S(1)} %get-tuple-element.164.weights.rest_0_, ...), custom_call_target="tpu_custom_call" | custom-call | tf_op jit(solution)/shard_map/forward/pallas_call | solution.py:195
  228.0 5.8 %forward.15 = (bf16[32,2560]{1,0:T(8,128)(2,1)S(1)}, bf16[2,2,32,2560]{3,2,1,0:T(8,128)(2,1)S(1)}) custom-call(s32[4]{0:T(128)S(1)} %pad_add_fusion.state, bf16[32,2560]{1,0:T(8,128)(2,1)S(1)} %get-tuple-element.149.arrived, f32[2,2560]{1,0:T(2,128)S(1)} %maximum_select_fusion.1.gains, ...), custom_call_target="tpu_custom_call", output_to_operand_aliasing={{1}: (5, {})} | custom-call | tf_op jit(solution)/shard_map/forward/pallas_call | solution.py:195
  243.4 4.4 %forward.21 = (bf16[32,2560]{1,0:T(8,128)(2,1)S(1)}, bf16[2,2,32,2560]{3,2,1,0:T(8,128)(2,1)S(1)}) custom-call(s32[4]{0:T(128)S(1)} %pad_add_fusion.state, bf16[32,2560]{1,0:T(8,128)(2,1)S(1)} %collective-permute-done.28.arrived, f32[2,2560]{1,0:T(2,128)S(1)} %maximum_select_fusion.1.gains, ...), custom_call_target="tpu_custom_call", output_to_operand_aliasing={{1}: (5, {})} | custom-call | tf_op jit(solution)/shard_map/forward/pallas_call | solution.py:195
  247.7 7.8 %transpose_weight.3.rest_0_.turned = bf16[2,2560,2560]{2,1,0:T(8,128)(2,1)S(1)} custom-call(s32[4]{0:T(128)S(1)} %pad_add_fusion.state, bf16[2,2560,2560]{2,1,0:T(8,128)(2,1)S(1)} %get-tuple-element.164.weights.rest_0_, bf16[2,2560,2560]{2,1,0:T(8,128)(2,1)S(1)} %transpose_weight.2.rest_0_._), custom_call_target="tpu_custom_call", output_to_operand_aliasing={{}: (2, {})} | custom-call | tf_op jit(solution)/shard_map/transpose_weight/pallas_call | solution.py:135
  267.5 6.1 %turn.3 = (bf16[32,2560]{1,0:T(8,128)(2,1)S(1)}, bf16[2,2,32,2560]{3,2,1,0:T(8,128)(2,1)S(1)}, f32[2,1,2560]{2,1,0:T(1,128)S(1)}) custom-call(s32[4]{0:T(128)S(1)} %pad_add_fusion.state, bf16[32,2560]{1,0:T(8,128)(2,1)S(1)} %get-tuple-element.148.fresh, ...), custom_call_target="tpu_custom_call", output_to_operand_aliasing={{1}: (6, {}), {2}: (7, {})} | custom-call | tf_op jit(solution)/shard_map/turn/pallas_call | solution.py:243
  276.7 5.3 %backward.16 = (bf16[32,2560]{1,0:T(8,128)(2,1)S(1)}, bf16[2,2,32,2560]{3,2,1,0:T(8,128)(2,1)S(1)}, f32[2,1,2560]{2,1,0:T(1,128)S(1)}) custom-call(s32[4]{0:T(128)S(1)} %pad_add_fusion.state, bf16[32,2560]{1,0:T(8,128)(2,1)S(1)} %collective-permute-done.39.received, ...), custom_call_target="tpu_custom_call", output_to_operand_aliasing={{1}: (6, {}), {2}: (7, {})} | custom-call | tf_op jit(solution)/shard_map/backward/pallas_call | solution.py:243
  292.6 5.0 %backward.23 = (bf16[32,2560]{1,0:T(8,128)(2,1)S(1)}, bf16[2,2,32,2560]{3,2,1,0:T(8,128)(2,1)S(1)}, f32[2,1,2560]{2,1,0:T(1,128)S(1)}) custom-call(s32[4]{0:T(128)S(1)} %pad_add_fusion.state, bf16[32,2560]{1,0:T(8,128)(2,1)S(1)} %collective-permute-done.46.received, ...), custom_call_target="tpu_custom_call", output_to_operand_aliasing={{1}: (6, {}), {2}: (7, {})} | custom-call | tf_op jit(solution)/shard_map/backward/pallas_call | solution.py:243
  300.7 90.1 %collective-permute-done.49.received = bf16[32,2560]{1,0:T(8,128)(2,1)S(1)} collective-permute-done((bf16[32,2560]{1,0:T(8,128)(2,1)S(1)}, bf16[32,2560]{1,0:T(8,128)(2,1)S(1)}, u32[]{:S(2)}, u32[]{:S(2)}) %collective-permute-start.49) | collective-permute-done | bytes 163872 | tf_op jit(solution)/shard_map/ppermute | solution.py:326
  392.1 6.2 %backward.26 = (bf16[32,2560]{1,0:T(8,128)(2,1)}, bf16[2,2,32,2560]{3,2,1,0:T(8,128)(2,1)S(1)}, f32[2,1,2560]{2,1,0:T(1,128)S(1)}) custom-call(s32[4]{0:T(128)S(1)} %pad_add_fusion.state, bf16[32,2560]{1,0:T(8,128)(2,1)S(1)} %collective-permute-done.49.received, ...), custom_call_target="tpu_custom_call", output_to_operand_aliasing={{1}: (6, {}), {2}: (7, {})} | custom-call | tf_op jit(solution)/shard_map/backward/pallas_call | solution.py:243
  398.3 6.4 %backward.27 = (bf16[32,2560]{1,0:T(8,128)(2,1)}, bf16[2,2,32,2560]{3,2,1,0:T(8,128)(2,1)S(1)}, f32[2,1,2560]{2,1,0:T(1,128)S(1)}) custom-call(s32[4]{0:T(128)S(1)} %pad_add_fusion.state, bf16[32,2560]{1,0:T(8,128)(2,1)S(1)} %collective-permute-done.50.received, ...), custom_call_target="tpu_custom_call", output_to_operand_aliasing={{1}: (6, {}), {2}: (7, {})} | custom-call | tf_op jit(solution)/shard_map/backward/pallas_call | solution.py:243
  404.8 15.4 %collective-permute-start.51 = (bf16[80,2560]{1,0:T(8,128)(2,1)S(1)}, bf16[80,2560]{1,0:T(8,128)(2,1)S(1)}, u32[]{:S(2)}, u32[]{:S(2)}) collective-permute-start(bf16[80,2560]{1,0:T(8,128)(2,1)S(1)} %pack.1), channel_id=1, source_target_pairs={{0,32},{32,0},{64,96},{96,64},{128,160},{160,128},{192,224},{224,1... | collective-permute-start | bytes 1228808 | tf_op jit(solution)/shard_map/ppermute | solution.py:269
  (170 shorter events, 94.5 us)
Async XLA Ops:
  3.5 31.5 %all-to-all-start = ((bf16[32,2,1280]{2,1,0:T(2,128)(2,1)}), bf16[32,2,1280]{2,1,0:T(2,128)(2,1)S(1)}, u32[]{:S(2)}, u32[]{:S(2)}) async-start(bf16[32,2,1280]{2,1,0:T(2,128)(2,1)} %reshape.85), calls=%async_computation | async-start | bytes 327680 | tf_op jit(solution)/shard_map/all_to_all | solution.py:288
  21.1 12.0 %collective-permute-start.1 = (bf16[80,1280]{1,0:T(8,128)(2,1)S(1)}, bf16[80,1280]{1,0:T(8,128)(2,1)S(1)}, u32[]{:S(2)}, u32[]{:S(2)}) collective-permute-start(bf16[80,1280]{1,0:T(8,128)(2,1)S(1)} %get-tuple-element.262), channel_id=1, source_target_pairs={{0,8},{1,9},{2,10},{3,11},{4,12},{5,13},{6,14},{7,15},{8,16},{9,17... | collective-permute-start | bytes 614408 | tf_op jit(solution)/shard_map/ppermute | solution.py:281
  25.2 19.1 %collective-permute-start.2 = (bf16[80,1280]{1,0:T(8,128)(2,1)S(1)}, bf16[80,1280]{1,0:T(8,128)(2,1)S(1)}, u32[]{:S(2)}, u32[]{:S(2)}) collective-permute-start(bf16[80,1280]{1,0:T(8,128)(2,1)S(1)} %get-tuple-element.262), channel_id=1, source_target_pairs={{0,24},{1,25},{2,26},{3,27},{4,28},{5,29},{6,30},{7,31},{8,0},{9,1... | collective-permute-start | bytes 614408 | tf_op jit(solution)/shard_map/ppermute | solution.py:281
  33.1 11.1 %collective-permute-start.3 = (bf16[80,1280]{1,0:T(8,128)(2,1)S(1)}, bf16[80,1280]{1,0:T(8,128)(2,1)S(1)}, u32[]{:S(2)}, u32[]{:S(2)}) collective-permute-start(bf16[80,1280]{1,0:T(8,128)(2,1)S(1)} %collective-permute-done.1), channel_id=1, source_target_pairs={{0,8},{1,9},{2,10},{3,11},{4,12},{5,13},{6,14},{7,15},{8,16},{9,17... | collective-permute-start | bytes 614408 | tf_op jit(solution)/shard_map/ppermute | solution.py:281
  36.8 18.7 %collective-permute-start.9 = (bf16[80,1280]{1,0:T(8,128)(2,1)S(1)}, bf16[80,1280]{1,0:T(8,128)(2,1)S(1)}, u32[]{:S(2)}, u32[]{:S(2)}) collective-permute-start(bf16[80,1280]{1,0:T(8,128)(2,1)S(1)} %get-tuple-element.134), channel_id=1, source_target_pairs={{0,24},{1,25},{2,26},{3,27},{4,28},{5,29},{6,30},{7,31},{8,0},{9,1... | collective-permute-start | bytes 614408 | tf_op jit(solution)/shard_map/ppermute | solution.py:281
  42.3 10.2 %collective-permute-start.8 = (bf16[80,1280]{1,0:T(8,128)(2,1)S(1)}, bf16[80,1280]{1,0:T(8,128)(2,1)S(1)}, u32[]{:S(2)}, u32[]{:S(2)}) collective-permute-start(bf16[80,1280]{1,0:T(8,128)(2,1)S(1)} %get-tuple-element.134), channel_id=1, source_target_pairs={{0,8},{1,9},{2,10},{3,11},{4,12},{5,13},{6,14},{7,15},{8,16},{9,17... | collective-permute-start | bytes 614408 | tf_op jit(solution)/shard_map/ppermute | solution.py:281
  44.3 23.7 %collective-permute-start.5 = (bf16[320,1280]{1,0:T(8,128)(2,1)S(1)}, bf16[320,1280]{1,0:T(8,128)(2,1)S(1)}, u32[]{:S(2)}, u32[]{:S(2)}) collective-permute-start(bf16[320,1280]{1,0:T(8,128)(2,1)S(1)} %pad_maximum_fusion.refs_0_), channel_id=1, source_target_pairs={{0,7},{1,0},{2,1},{3,2},{4,3},{5,4},{6,5},{7,6},{8,15},{9,8},{10,9... | collective-permute-start | bytes 2457608 | tf_op jit(solution)/shard_map/ppermute | solution.py:281
  48.1 20.0 %collective-permute-start.4 = (bf16[320,1280]{1,0:T(8,128)(2,1)S(1)}, bf16[320,1280]{1,0:T(8,128)(2,1)S(1)}, u32[]{:S(2)}, u32[]{:S(2)}) collective-permute-start(bf16[320,1280]{1,0:T(8,128)(2,1)S(1)} %pad_maximum_fusion.refs_0_), channel_id=1, source_target_pairs={{0,1},{1,2},{2,3},{3,4},{4,5},{5,6},{6,7},{7,0},{8,9},{9,10},{10,1... | collective-permute-start | bytes 2457608 | tf_op jit(solution)/shard_map/ppermute | solution.py:281
  52.5 9.2 %collective-permute-start.10 = (bf16[80,1280]{1,0:T(8,128)(2,1)S(1)}, bf16[80,1280]{1,0:T(8,128)(2,1)S(1)}, u32[]{:S(2)}, u32[]{:S(2)}) collective-permute-start(bf16[80,1280]{1,0:T(8,128)(2,1)S(1)} %collective-permute-done.8), channel_id=1, source_target_pairs={{0,8},{1,9},{2,10},{3,11},{4,12},{5,13},{6,14},{7,15},{8,16},{9,17... | collective-permute-start | bytes 614408 | tf_op jit(solution)/shard_map/ppermute | solution.py:281
  61.8 13.6 %collective-permute-start.12 = (bf16[320,1280]{1,0:T(8,128)(2,1)S(1)}, bf16[320,1280]{1,0:T(8,128)(2,1)S(1)}, u32[]{:S(2)}, u32[]{:S(2)}) collective-permute-start(bf16[320,1280]{1,0:T(8,128)(2,1)S(1)} %constant_dynamic-update-slice_fusion.refs_5_), channel_id=1, source_target_pairs={{0,7},{1,0},{2,1},{3,2},{4,3},{5,4},{6,5},{7,6},{8,15},{9,8},{10,9... | collective-permute-start | bytes 2457608 | tf_op jit(solution)/shard_map/ppermute | solution.py:281
  66.1 14.3 %collective-permute-start.11 = (bf16[320,1280]{1,0:T(8,128)(2,1)S(1)}, bf16[320,1280]{1,0:T(8,128)(2,1)S(1)}, u32[]{:S(2)}, u32[]{:S(2)}) collective-permute-start(bf16[320,1280]{1,0:T(8,128)(2,1)S(1)} %constant_dynamic-update-slice_fusion.refs_5_), channel_id=1, source_target_pairs={{0,1},{1,2},{2,3},{3,4},{4,5},{5,6},{6,7},{7,0},{8,9},{9,10},{10,1... | collective-permute-start | bytes 2457608 | tf_op jit(solution)/shard_map/ppermute | solution.py:281
  68.1 28.6 %collective-permute-start.6 = (bf16[320,1280]{1,0:T(8,128)(2,1)S(1)}, bf16[320,1280]{1,0:T(8,128)(2,1)S(1)}, u32[]{:S(2)}, u32[]{:S(2)}) collective-permute-start(bf16[320,1280]{1,0:T(8,128)(2,1)S(1)} %collective-permute-done.4.refs_1_), channel_id=1, source_target_pairs={{0,1},{1,2},{2,3},{3,4},{4,5},{5,6},{6,7},{7,0},{8,9},{9,10},{10,1... | collective-permute-start | bytes 2457608 | tf_op jit(solution)/shard_map/ppermute | solution.py:281
  70.1 26.5 %collective-permute-start.7 = (bf16[320,1280]{1,0:T(8,128)(2,1)S(1)}, bf16[320,1280]{1,0:T(8,128)(2,1)S(1)}, u32[]{:S(2)}, u32[]{:S(2)}) collective-permute-start(bf16[320,1280]{1,0:T(8,128)(2,1)S(1)} %collective-permute-done.5.refs_2_), channel_id=1, source_target_pairs={{0,7},{1,0},{2,1},{3,2},{4,3},{5,4},{6,5},{7,6},{8,15},{9,8},{10,9... | collective-permute-start | bytes 2457608 | tf_op jit(solution)/shard_map/ppermute | solution.py:281
  80.4 33.8 %collective-permute-start.13 = (bf16[320,1280]{1,0:T(8,128)(2,1)S(1)}, bf16[320,1280]{1,0:T(8,128)(2,1)S(1)}, u32[]{:S(2)}, u32[]{:S(2)}) collective-permute-start(bf16[320,1280]{1,0:T(8,128)(2,1)S(1)} %collective-permute-done.11.refs_6_), channel_id=1, source_target_pairs={{0,1},{1,2},{2,3},{3,4},{4,5},{5,6},{6,7},{7,0},{8,9},{9,10},{10,1... | collective-permute-start | bytes 2457608 | tf_op jit(solution)/shard_map/ppermute | solution.py:281
  82.3 31.9 %collective-permute-start.14 = (bf16[320,1280]{1,0:T(8,128)(2,1)S(1)}, bf16[320,1280]{1,0:T(8,128)(2,1)S(1)}, u32[]{:S(2)}, u32[]{:S(2)}) collective-permute-start(bf16[320,1280]{1,0:T(8,128)(2,1)S(1)} %collective-permute-done.12.refs_7_), channel_id=1, source_target_pairs={{0,7},{1,0},{2,1},{3,2},{4,3},{5,4},{6,5},{7,6},{8,15},{9,8},{10,9... | collective-permute-start | bytes 2457608 | tf_op jit(solution)/shard_map/ppermute | solution.py:281
  96.7 35.1 %collective-permute-start.15 = (bf16[320,1280]{1,0:T(8,128)(2,1)S(1)}, bf16[320,1280]{1,0:T(8,128)(2,1)S(1)}, u32[]{:S(2)}, u32[]{:S(2)}) collective-permute-start(bf16[320,1280]{1,0:T(8,128)(2,1)S(1)} %collective-permute-done.6.refs_3_), channel_id=1, source_target_pairs={{0,1},{1,2},{2,3},{3,4},{4,5},{5,6},{6,7},{7,0},{8,9},{9,10},{10,1... | collective-permute-start | bytes 2457608 | tf_op jit(solution)/shard_map/ppermute | solution.py:281
  98.6 33.2 %collective-permute-start.16 = (bf16[320,1280]{1,0:T(8,128)(2,1)S(1)}, bf16[320,1280]{1,0:T(8,128)(2,1)S(1)}, u32[]{:S(2)}, u32[]{:S(2)}) collective-permute-start(bf16[320,1280]{1,0:T(8,128)(2,1)S(1)} %collective-permute-done.7.refs_4_), channel_id=1, source_target_pairs={{0,7},{1,0},{2,1},{3,2},{4,3},{5,4},{6,5},{7,6},{8,15},{9,8},{10,9... | collective-permute-start | bytes 2457608 | tf_op jit(solution)/shard_map/ppermute | solution.py:281
  114.2 35.1 %collective-permute-start.17 = (bf16[320,1280]{1,0:T(8,128)(2,1)S(1)}, bf16[320,1280]{1,0:T(8,128)(2,1)S(1)}, u32[]{:S(2)}, u32[]{:S(2)}) collective-permute-start(bf16[320,1280]{1,0:T(8,128)(2,1)S(1)} %collective-permute-done.13.refs_8_), channel_id=1, source_target_pairs={{0,1},{1,2},{2,3},{3,4},{4,5},{5,6},{6,7},{7,0},{8,9},{9,10},{10,1... | collective-permute-start | bytes 2457608 | tf_op jit(solution)/shard_map/ppermute | solution.py:281
  116.2 33.2 %collective-permute-start.18 = (bf16[320,1280]{1,0:T(8,128)(2,1)S(1)}, bf16[320,1280]{1,0:T(8,128)(2,1)S(1)}, u32[]{:S(2)}, u32[]{:S(2)}) collective-permute-start(bf16[320,1280]{1,0:T(8,128)(2,1)S(1)} %collective-permute-done.14.refs_9_), channel_id=1, source_target_pairs={{0,7},{1,0},{2,1},{3,2},{4,3},{5,4},{6,5},{7,6},{8,15},{9,8},{10,9... | collective-permute-start | bytes 2457608 | tf_op jit(solution)/shard_map/ppermute | solution.py:281
  156.6 52.7 %collective-permute-start.22 = (bf16[1600,2560]{1,0:T(8,128)(2,1)}, bf16[1600,2560]{1,0:T(8,128)(2,1)}, u32[]{:S(2)}, u32[]{:S(2)}) collective-permute-start(bf16[1600,2560]{1,0:T(8,128)(2,1)} %assemble.3.rest_0_), channel_id=1, source_target_pairs={{0,32},{32,0},{64,96},{96,64},{128,160},{160,128},{192,224},{224,1... | collective-permute-start | bytes 24576008 | tf_op jit(solution)/shard_map/ppermute | solution.py:269
  169.4 23.0 %collective-permute-start.19 = (bf16[320,1280]{1,0:T(8,128)(2,1)S(1)}, bf16[320,1280]{1,0:T(8,128)(2,1)S(1)}, u32[]{:S(2)}, u32[]{:S(2)}) collective-permute-start(bf16[320,1280]{1,0:T(8,128)(2,1)S(1)} %collective-permute-done.15.refs_0_), channel_id=1, source_target_pairs={{0,1},{1,2},{2,3},{3,4},{4,5},{5,6},{6,7},{7,0},{8,9},{9,10},{10,1... | collective-permute-start | bytes 2457608 | tf_op jit(solution)/shard_map/ppermute | solution.py:281
  171.3 21.9 %collective-permute-start.20 = (bf16[320,1280]{1,0:T(8,128)(2,1)S(1)}, bf16[320,1280]{1,0:T(8,128)(2,1)S(1)}, u32[]{:S(2)}, u32[]{:S(2)}) collective-permute-start(bf16[320,1280]{1,0:T(8,128)(2,1)S(1)} %collective-permute-done.18.refs_4_), channel_id=1, source_target_pairs={{0,7},{1,0},{2,1},{3,2},{4,3},{5,4},{6,5},{7,6},{8,15},{9,8},{10,9... | collective-permute-start | bytes 2457608 | tf_op jit(solution)/shard_map/ppermute | solution.py:281
  198.4 19.0 %collective-permute-start.21 = (bf16[960,2560]{1,0:T(8,128)(2,1)}, bf16[960,2560]{1,0:T(8,128)(2,1)}, u32[]{:S(2)}, u32[]{:S(2)}) collective-permute-start(bf16[960,2560]{1,0:T(8,128)(2,1)} %assemble.2.rest_1_), channel_id=1, source_target_pairs={{0,32},{32,0},{64,96},{96,64},{128,160},{160,128},{192,224},{224,1... | collective-permute-start | bytes 14745608 | tf_op jit(solution)/shard_map/ppermute | solution.py:269
  201.4 7.8 %collective-permute-start = (f32[1,2560]{1,0:T(1,128)S(1)}, f32[1,2560]{1,0:T(1,128)S(1)}, u32[]{:S(2)}, u32[]{:S(2)}) collective-permute-start(f32[1,2560]{1,0:T(1,128)S(1)} %copy-done.18), channel_id=1, source_target_pairs={{0,32},{32,0},{64,96},{96,64},{128,160},{160,128},{192,224},{224,1... | collective-permute-start | bytes 30728 | tf_op jit(solution)/shard_map/ppermute | solution.py:269
  226.7 7.2 %collective-permute-start.23 = (bf16[32,2560]{1,0:T(8,128)(2,1)S(1)}, bf16[32,2560]{1,0:T(8,128)(2,1)S(1)}, u32[]{:S(2)}, u32[]{:S(2)}) collective-permute-start(bf16[32,2560]{1,0:T(8,128)(2,1)S(1)} %get-tuple-element.169), channel_id=1, source_target_pairs={{0,64},{32,96},{1,65},{33,97},{2,66},{34,98},{3,67},{35,99},{4,68}... | collective-permute-start | bytes 491528 | tf_op jit(solution)/shard_map/ppermute | solution.py:326
  242.7 12.9 %collective-permute-start.29 = (bf16[32,2560]{1,0:T(8,128)(2,1)S(1)}, bf16[32,2560]{1,0:T(8,128)(2,1)S(1)}, u32[]{:S(2)}, u32[]{:S(2)}) collective-permute-start(bf16[32,2560]{1,0:T(8,128)(2,1)S(1)} %get-tuple-element.184), channel_id=1, source_target_pairs={{192,256},{224,288},{193,257},{225,289},{194,258},{226,290},{195,2... | collective-permute-start | bytes 491528 | tf_op jit(solution)/shard_map/ppermute | solution.py:326
  266.8 6.8 %collective-permute-start.37 = (bf16[32,2560]{1,0:T(8,128)(2,1)S(1)}, bf16[32,2560]{1,0:T(8,128)(2,1)S(1)}, u32[]{:S(2)}, u32[]{:S(2)}) collective-permute-start(bf16[32,2560]{1,0:T(8,128)(2,1)S(1)} %get-tuple-element.205), channel_id=1, source_target_pairs={{448,384},{480,416},{449,385},{481,417},{450,386},{482,418},{451,3... | collective-permute-start | bytes 491528 | tf_op jit(solution)/shard_map/ppermute | solution.py:326
  276.1 6.7 %collective-permute-start.40 = (bf16[32,2560]{1,0:T(8,128)(2,1)S(1)}, bf16[32,2560]{1,0:T(8,128)(2,1)S(1)}, u32[]{:S(2)}, u32[]{:S(2)}) collective-permute-start(bf16[32,2560]{1,0:T(8,128)(2,1)S(1)} %get-tuple-element.214), channel_id=1, source_target_pairs={{384,320},{416,352},{385,321},{417,353},{386,322},{418,354},{387,3... | collective-permute-start | bytes 491528 | tf_op jit(solution)/shard_map/ppermute | solution.py:326
  291.9 5.7 %collective-permute-start.47 = (bf16[32,2560]{1,0:T(8,128)(2,1)S(1)}, bf16[32,2560]{1,0:T(8,128)(2,1)S(1)}, u32[]{:S(2)}, u32[]{:S(2)}) collective-permute-start(bf16[32,2560]{1,0:T(8,128)(2,1)S(1)} %get-tuple-element.241), channel_id=1, source_target_pairs={{128,64},{160,96},{129,65},{161,97},{130,66},{162,98},{131,67},{16... | collective-permute-start | bytes 491528 | tf_op jit(solution)/shard_map/ppermute | solution.py:326
  298.8 91.9 %collective-permute-start.49 = (bf16[32,2560]{1,0:T(8,128)(2,1)S(1)}, bf16[32,2560]{1,0:T(8,128)(2,1)S(1)}, u32[]{:S(2)}, u32[]{:S(2)}) collective-permute-start(bf16[32,2560]{1,0:T(8,128)(2,1)S(1)} %get-tuple-element.248), channel_id=1, source_target_pairs={{64,0},{96,32},{65,1},{97,33},{66,2},{98,34},{67,3},{99,35},{68,4}... | collective-permute-start | bytes 491528 | tf_op jit(solution)/shard_map/ppermute | solution.py:326
  390.8 7.5 %collective-permute-start.50 = (bf16[32,2560]{1,0:T(8,128)(2,1)S(1)}, bf16[32,2560]{1,0:T(8,128)(2,1)S(1)}, u32[]{:S(2)}, u32[]{:S(2)}) collective-permute-start(bf16[32,2560]{1,0:T(8,128)(2,1)S(1)} %get-tuple-element.249), channel_id=1, source_target_pairs={{64,0},{96,32},{65,1},{97,33},{66,2},{98,34},{67,3},{99,35},{68,4}... | collective-permute-start | bytes 491528 | tf_op jit(solution)/shard_map/ppermute | solution.py:326
  404.8 16.7 %collective-permute-start.51 = (bf16[80,2560]{1,0:T(8,128)(2,1)S(1)}, bf16[80,2560]{1,0:T(8,128)(2,1)S(1)}, u32[]{:S(2)}, u32[]{:S(2)}) collective-permute-start(bf16[80,2560]{1,0:T(8,128)(2,1)S(1)} %pack.1), channel_id=1, source_target_pairs={{0,32},{32,0},{64,96},{96,64},{128,160},{160,128},{192,224},{224,1... | collective-permute-start | bytes 1228808 | tf_op jit(solution)/shard_map/ppermute | solution.py:269
  (40 other events, 949.6 us)

commit v4 on v3

--- a/solution.py
+++ b/solution.py
@@ -291,7 +291,8 @@
 
     half = width // 2
     shards = [weight[0, :, :half], weight[0, :, half:]]
-    shards[1], new_momentum = lax.optimization_barrier((shards[1], new_momentum))
+    gains = ordered(gain, swap(gain))
+    shards[1], new_momentum, gains = lax.optimization_barrier((shards[1], new_momentum, gains))
     blocks = [first_block(shard) for shard in shards]
     rings = [[(block, block)] for block in blocks]
     for step in range(3):
@@ -307,7 +308,6 @@
     outer = assemble(*[[*ring[3], end] for ring, end in zip(rings, ends)])
     outer_other = swap(outer)
 
-    gains = ordered(gain, swap(gain))
     replica = lax.axis_index("dp")
     state = jnp.stack([stage, core, replica // 8, lax.rem(replica, 8)]).astype(jnp.int32)
     fresh = lax.dynamic_slice_in_dim(inputs, core * parts, parts, 0)
@@ -321,33 +321,38 @@
     turned = transpose(False, state, weights, turned)
 
     def hop(array, k, to, after):
-        if after is not None:
-            array, after = lax.optimization_barrier((array, after))
+        array, _ = lax.optimization_barrier((array, after))
         return lax.ppermute(array, "section", [(2 * k + c, 2 * to + c) for c in range(2)])
 
     arrived = fresh
     stash, kept = [], []
-    for k in range(stages - 1):
+    path = [(k, k + 1) for k in range(stages - 1)] + [(k, k - 1) for k in range(stages - 1, -1, -1)]
+    waiting = None
+    for at, (k, to) in enumerate(path):
         landed = []
         for m in range(parts):
-            sent, *stash = forward(k, m, parts, state, arrived[m], gains, weights, turned, stash)
-            landed.append(hop(sent, k, k + 1, landed[-1] if landed else None))
+            if m == parts - 1 and waiting is not None:
+                arrived.append(hop(*waiting, [arrived[m - 1], landed[-1] if landed else leaving]))
+                waiting = None
+            if to > k:
+                leaving, *stash = forward(k, m, parts, state, arrived[m], gains, weights, turned, stash)
+            else:
+                if k == stages - 1:
+                    kernel, scratch = functools.partial(turn_kernel, m, stages), [pltpu.VMEM((rows, width), BF16)] * 2
+                    operands = [state, target[m], arrived[m], gains, held(weights), held(turned)]
+                else:
+                    kernel, scratch = functools.partial(backward_kernel, k, m), []
+                    operands = [state, arrived[m], held(stash[0]), gains, held(turned), held(weights)]
+                leaving, *kept = backward(kernel, parts, operands, kept, scratch, "turn" if scratch else "backward")
+            if to < 0:
+                continue
+            if m < parts - 1 or to == stages - 1:
+                landed.append(hop(leaving, k, to, landed[-1:]))
+            else:
+                waiting = (leaving, k, to)
         arrived = landed
-        if k == 3:
+        if at == 3:
             turned = transpose(True, state, weights, turned)
-    for k in range(stages - 1, -1, -1):
-        landed = []
-        for m in range(parts):
-            if k == stages - 1:
-                kernel, scratch = functools.partial(turn_kernel, m, stages), [pltpu.VMEM((rows, width), BF16)] * 2
-                operands = [state, target[m], arrived[m], gains, held(weights), held(turned)]
-            else:
-                kernel, scratch = functools.partial(backward_kernel, k, m), []
-                operands = [state, arrived[m], held(stash[0]), gains, held(turned), held(weights)]
-            leaving, *kept = backward(kernel, parts, operands, kept, scratch, "turn" if scratch else "backward")
-            if k > 0:
-                landed.append(hop(leaving, k, k - 1, landed[-1] if landed else None))
-        arrived = landed
     collected, totals = kept
 
     other = swap(pack(collected, totals))

time: 431 us -> 446 us (1.035)
  waiting for transfers between devices: 184 us -> 196 us
    ppermute x28, waiting for transfers between devices: 91.5 us -> 100 us  [hop(): lax.ppermute(array, 'section', [(2 * k + c, 2 * to + c) for c in range(2)])]
    ppermute x28, starting transfers between devices: 24.1 us -> 32.7 us  [hop(): lax.ppermute(array, 'section', [(2 * k + c, 2 * to + c) for c in range(2)])]
    all_to_all x1, waiting for transfers between devices: 0.01 us -> 6.78 us  [per_device(): pieces = lax.all_to_all(bucket, 'dp', 0, 0, tiled=True).astype(F32)]
    all_to_all x1, starting transfers between devices: 16.5 us -> 10.3 us  [per_device(): pieces = lax.all_to_all(bucket, 'dp', 0, 0, tiled=True).astype(F32)]
    ppermute x4, waiting for transfers between devices: 7 us -> 1.33 us  [swap(): return lax.ppermute(array, 'section', siblings)]
  transfers between devices with their start and end apart: 53 -> 53, of which waited for: 15 -> 15; matrix products, arithmetic and copies ran while one was open for 1% -> 1% of each run, Pallas kernels for 16% -> 7%
where the time goes in v4:
time: 446 us; the launch traced here: 438 us
  waiting for transfers between devices  196 us (44%)
  starting transfers between devices  142 us (32%)
  Pallas kernels  87.9 us (20%)
  other arithmetic  5.82 us (1%)
    ppermute x28, waiting for transfers between devices, hop(): lax.ppermute(array, 'section', [(2 * k + c, 2 * to + c) for c in range(2)])  100 us
    ppermute x20, waiting for transfers between devices, over(): return lax.ppermute(array, 'dp', pairs)  87.6 us
    ppermute x20, starting transfers between devices, over(): return lax.ppermute(array, 'dp', pairs)  66.7 us
    pallas_call x16, Pallas kernels, backward(): pl.pallas_call(kernel, out_shape=[jax.ShapeDtypeStruct((rows, width), BF1...  33.7 us
    ppermute x28, starting transfers between devices, hop(): lax.ppermute(array, 'section', [(2 * k + c, 2 * to + c) for c in range(2)])  32.7 us
    ppermute x4, starting transfers between devices, swap(): return lax.ppermute(array, 'section', siblings)  32.2 us
    pallas_call x14, Pallas kernels, forward(): pl.pallas_call(functools.partial(forward_kernel, k, part), out_shape=[jax...  23.5 us
    pallas_call x2, Pallas kernels, assemble(): pl.pallas_call(assemble_kernel, out_shape=pltpu.HBM(shape, BF16), in_spec...  11.2 us
  transfers between devices with their start and end apart: 53, of which 15 were waited for; matrix products, arithmetic and copies ran while one was open for 1% of the time, Pallas kernels for 7%

profile of v4, /device:TPU:1, one launch (start us, length us, event | category | flops | bytes accessed | tf_op | source)
XLA Modules:
  0.0 437.7 jit_solution(10878739466222508778)
XLA Ops:
  1.7 6.7 %collective-permute-start.2 = (bf16[80,1280]{1,0:T(8,128)(2,1)S(1)}, bf16[80,1280]{1,0:T(8,128)(2,1)S(1)}, u32[]{:S(2)}, u32[]{:S(2)}) collective-permute-start(bf16[80,1280]{1,0:T(8,128)(2,1)S(1)} %get-tuple-element.263), channel_id=1, source_target_pairs={{0,24},{1,25},{2,26},{3,27},{4,28},{5,29},{6,30},{7,31},{8,0},{9,1... | collective-permute-start | bytes 614408 | tf_op jit(solution)/shard_map/ppermute | solution.py:281
  10.3 6.9 %collective-permute-start = (f32[1,2560]{1,0:T(1,128)}, f32[1,2560]{1,0:T(1,128)S(1)}, u32[]{:S(2)}, u32[]{:S(2)}) collective-permute-start(f32[1,2560]{1,0:T(1,128)} %param.9), channel_id=1, source_target_pairs={{0,32},{32,0},{64,96},{96,64},{128,160},{160,128},{192,224},{224,1... | collective-permute-start | bytes 30728 | tf_op jit(solution)/shard_map/ppermute | solution.py:269
  20.2 10.3 %all-to-all-start = ((bf16[32,2,1280]{2,1,0:T(2,128)(2,1)}), bf16[32,2,1280]{2,1,0:T(2,128)(2,1)S(1)}, u32[]{:S(2)}, u32[]{:S(2)}) async-start(bf16[32,2,1280]{2,1,0:T(2,128)(2,1)} %reshape.85), calls=%async_computation | async-start | bytes 327680 | tf_op jit(solution)/shard_map/all_to_all | solution.py:288
  35.4 6.8 %all-to-all-done = bf16[32,2,1280]{2,1,0:T(2,128)(2,1)S(1)} async-done(((bf16[32,2,1280]{2,1,0:T(2,128)(2,1)}), bf16[32,2,1280]{2,1,0:T(2,128)(2,1)S(1)}, u32[]{:S(2)}, u32[]{:S(2)}) %all-to-all-start) | async-done | bytes 163872 | tf_op jit(solution)/shard_map/all_to_all | solution.py:288
  61.3 6.6 %collective-permute-done.10 = bf16[80,1280]{1,0:T(8,128)(2,1)S(1)} collective-permute-done((bf16[80,1280]{1,0:T(8,128)(2,1)S(1)}, bf16[80,1280]{1,0:T(8,128)(2,1)S(1)}, u32[]{:S(2)}, u32[]{:S(2)}) %collective-permute-start.10) | collective-permute-done | bytes 204832 | tf_op jit(solution)/shard_map/ppermute | solution.py:281
  80.6 5.6 %collective-permute-done.12.refs_7_ = bf16[320,1280]{1,0:T(8,128)(2,1)S(1)} collective-permute-done((bf16[320,1280]{1,0:T(8,128)(2,1)S(1)}, bf16[320,1280]{1,0:T(8,128)(2,1)S(1)}, u32[]{:S(2)}, u32[]{:S(2)}) %collective-permute-start.12) | collective-permute-done | bytes 819232 | tf_op jit(solution)/shard_map/ppermute | solution.py:281
  86.2 5.6 %collective-permute-done.11.refs_6_ = bf16[320,1280]{1,0:T(8,128)(2,1)S(1)} collective-permute-done((bf16[320,1280]{1,0:T(8,128)(2,1)S(1)}, bf16[320,1280]{1,0:T(8,128)(2,1)S(1)}, u32[]{:S(2)}, u32[]{:S(2)}) %collective-permute-start.11) | collective-permute-done | bytes 819232 | tf_op jit(solution)/shard_map/ppermute | solution.py:281
  93.8 4.6 %collective-permute-start.14 = (bf16[320,1280]{1,0:T(8,128)(2,1)S(1)}, bf16[320,1280]{1,0:T(8,128)(2,1)S(1)}, u32[]{:S(2)}, u32[]{:S(2)}) collective-permute-start(bf16[320,1280]{1,0:T(8,128)(2,1)S(1)} %collective-permute-done.12.refs_7_), channel_id=1, source_target_pairs={{0,7},{1,0},{2,1},{3,2},{4,3},{5,4},{6,5},{7,6},{8,15},{9,8},{10,9... | collective-permute-start | bytes 2457608 | tf_op jit(solution)/shard_map/ppermute | solution.py:281
  98.3 11.1 %collective-permute-done.6.refs_3_ = bf16[320,1280]{1,0:T(8,128)(2,1)S(1)} collective-permute-done((bf16[320,1280]{1,0:T(8,128)(2,1)S(1)}, bf16[320,1280]{1,0:T(8,128)(2,1)S(1)}, u32[]{:S(2)}, u32[]{:S(2)}) %collective-permute-start.6) | collective-permute-done | bytes 819232 | tf_op jit(solution)/shard_map/ppermute | solution.py:281
  111.3 4.6 %collective-permute-start.16 = (bf16[320,1280]{1,0:T(8,128)(2,1)S(1)}, bf16[320,1280]{1,0:T(8,128)(2,1)S(1)}, u32[]{:S(2)}, u32[]{:S(2)}) collective-permute-start(bf16[320,1280]{1,0:T(8,128)(2,1)S(1)} %collective-permute-done.7.refs_4_), channel_id=1, source_target_pairs={{0,7},{1,0},{2,1},{3,2},{4,3},{5,4},{6,5},{7,6},{8,15},{9,8},{10,9... | collective-permute-start | bytes 2457608 | tf_op jit(solution)/shard_map/ppermute | solution.py:281
  115.9 11.0 %collective-permute-done.13.refs_8_ = bf16[320,1280]{1,0:T(8,128)(2,1)S(1)} collective-permute-done((bf16[320,1280]{1,0:T(8,128)(2,1)S(1)}, bf16[320,1280]{1,0:T(8,128)(2,1)S(1)}, u32[]{:S(2)}, u32[]{:S(2)}) %collective-permute-start.13) | collective-permute-done | bytes 819232 | tf_op jit(solution)/shard_map/ppermute | solution.py:281
  128.9 4.6 %collective-permute-start.18 = (bf16[320,1280]{1,0:T(8,128)(2,1)S(1)}, bf16[320,1280]{1,0:T(8,128)(2,1)S(1)}, u32[]{:S(2)}, u32[]{:S(2)}) collective-permute-start(bf16[320,1280]{1,0:T(8,128)(2,1)S(1)} %collective-permute-done.14.refs_9_), channel_id=1, source_target_pairs={{0,7},{1,0},{2,1},{3,2},{4,3},{5,4},{6,5},{7,6},{8,15},{9,8},{10,9... | collective-permute-start | bytes 2457608 | tf_op jit(solution)/shard_map/ppermute | solution.py:281
  133.5 11.0 %collective-permute-done.15.refs_0_ = bf16[320,1280]{1,0:T(8,128)(2,1)S(1)} collective-permute-done((bf16[320,1280]{1,0:T(8,128)(2,1)S(1)}, bf16[320,1280]{1,0:T(8,128)(2,1)S(1)}, u32[]{:S(2)}, u32[]{:S(2)}) %collective-permute-start.15) | collective-permute-done | bytes 819232 | tf_op jit(solution)/shard_map/ppermute | solution.py:281
  144.5 17.5 %collective-permute-done.17.refs_3_ = bf16[320,1280]{1,0:T(8,128)(2,1)S(1)} collective-permute-done((bf16[320,1280]{1,0:T(8,128)(2,1)S(1)}, bf16[320,1280]{1,0:T(8,128)(2,1)S(1)}, u32[]{:S(2)}, u32[]{:S(2)}) %collective-permute-start.17) | collective-permute-done | bytes 819232 | tf_op jit(solution)/shard_map/ppermute | solution.py:281
  162.2 7.0 %assemble.3.rest_0_ = bf16[1600,2560]{1,0:T(8,128)(2,1)} custom-call(bf16[320,1280]{1,0:T(8,128)(2,1)} %copy-done, bf16[320,1280]{1,0:T(8,128)(2,1)} %copy-done.9, bf16[320,1280]{1,0:T(8,128)(2,1)} %copy-done.8, bf16[320,1280]{1,0:T(8,128)(2,1)} %copy-done.12, bf16[320,1280]{1,0:T(8,128)(2,1)} %copy-done.13, bf16[320,1280]{1,0:T(8,128)(2,1)} %copy-done.1, ...), custom_call_target="tpu_custom_call" | custom-call | tf_op jit(solution)/shard_map/assemble/pallas_call | solution.py:51
  169.2 6.0 %collective-permute-start.22 = (bf16[1600,2560]{1,0:T(8,128)(2,1)}, bf16[1600,2560]{1,0:T(8,128)(2,1)}, u32[]{:S(2)}, u32[]{:S(2)}) collective-permute-start(bf16[1600,2560]{1,0:T(8,128)(2,1)} %assemble.3.rest_0_), channel_id=1, source_target_pairs={{0,32},{32,0},{64,96},{96,64},{128,160},{160,128},{192,224},{224,1... | collective-permute-start | bytes 24576008 | tf_op jit(solution)/shard_map/ppermute | solution.py:269
  177.2 4.6 %collective-permute-start.20 = (bf16[320,1280]{1,0:T(8,128)(2,1)S(1)}, bf16[320,1280]{1,0:T(8,128)(2,1)S(1)}, u32[]{:S(2)}, u32[]{:S(2)}) collective-permute-start(bf16[320,1280]{1,0:T(8,128)(2,1)S(1)} %collective-permute-done.18.refs_4_), channel_id=1, source_target_pairs={{0,7},{1,0},{2,1},{3,2},{4,3},{5,4},{6,5},{7,6},{8,15},{9,8},{10,9... | collective-permute-start | bytes 2457608 | tf_op jit(solution)/shard_map/ppermute | solution.py:281
  181.8 16.4 %collective-permute-done.19.refs_2_ = bf16[320,1280]{1,0:T(8,128)(2,1)S(1)} collective-permute-done((bf16[320,1280]{1,0:T(8,128)(2,1)S(1)}, bf16[320,1280]{1,0:T(8,128)(2,1)S(1)}, u32[]{:S(2)}, u32[]{:S(2)}) %collective-permute-start.19) | collective-permute-done | bytes 819232 | tf_op jit(solution)/shard_map/ppermute | solution.py:281
  200.0 4.2 assemble.2.rest_1_
  207.4 8.1 %place_weight.2 = (bf16[2,2560,2560]{2,1,0:T(8,128)(2,1)S(1)}, bf16[2,2560,2560]{2,1,0:T(8,128)(2,1)S(1)}) custom-call(s32[4]{0:T(128)S(1)} %pad_add_fusion.state, bf16[1600,2560]{1,0:T(8,128)(2,1)} %assemble.3.rest_0_, bf16[960,2560]{1,0:T(8,128)(2,1)} %assemble.2.rest_1_, bf16[1600,2560]{1,0:T(8,128)(2,1)} %collective-permute-done.22.rest_2_), custom_call_target="tpu_custom_call" | custom-call | tf_op jit(solution)/shard_map/place_weight/pallas_call | solution.py:84
  219.1 5.7 %forward.14 = (bf16[32,2560]{1,0:T(8,128)(2,1)S(1)}, bf16[2,2,32,2560]{3,2,1,0:T(8,128)(2,1)S(1)}) custom-call(s32[4]{0:T(128)S(1)} %pad_add_fusion.state, bf16[32,2560]{1,0:T(8,128)(2,1)S(1)} %get-tuple-element.168.arrived, f32[2,2560]{1,0:T(2,128)S(1)} %maximum_select_fusion.1.gains, bf16[2,2560,2560]{2,1,0:T(8,128)(2,1)S(1)} %get-tuple-element.166.weights.rest_0_, ...), custom_call_target="tpu_custom_call" | custom-call | tf_op jit(solution)/shard_map/forward/pallas_call | solution.py:195
  226.1 6.2 %forward.15 = (bf16[32,2560]{1,0:T(8,128)(2,1)S(1)}, bf16[2,2,32,2560]{3,2,1,0:T(8,128)(2,1)S(1)}) custom-call(s32[4]{0:T(128)S(1)} %pad_add_fusion.state, bf16[32,2560]{1,0:T(8,128)(2,1)S(1)} %get-tuple-element.151.arrived, f32[2,2560]{1,0:T(2,128)S(1)} %maximum_select_fusion.1.gains, ...), custom_call_target="tpu_custom_call", output_to_operand_aliasing={{1}: (5, {})} | custom-call | tf_op jit(solution)/shard_map/forward/pallas_call | solution.py:195
  233.6 10.4 %collective-permute-start.25 = (bf16[32,2560]{1,0:T(8,128)(2,1)S(1)}, bf16[32,2560]{1,0:T(8,128)(2,1)S(1)}, u32[]{:S(2)}, u32[]{:S(2)}) collective-permute-start(bf16[32,2560]{1,0:T(8,128)(2,1)S(1)} %get-tuple-element.174), channel_id=1, source_target_pairs={{0,64},{32,96},{1,65},{33,97},{2,66},{34,98},{3,67},{35,99},{4,68}... | collective-permute-start | bytes 491528 | tf_op jit(solution)/shard_map/ppermute | solution.py:325
  254.8 7.8 %transpose_weight.3.rest_0_.turned = bf16[2,2560,2560]{2,1,0:T(8,128)(2,1)S(1)} custom-call(s32[4]{0:T(128)S(1)} %pad_add_fusion.state, bf16[2,2560,2560]{2,1,0:T(8,128)(2,1)S(1)} %get-tuple-element.166.weights.rest_0_, bf16[2,2560,2560]{2,1,0:T(8,128)(2,1)S(1)} %transpose_weight.2.rest_0_._), custom_call_target="tpu_custom_call", output_to_operand_aliasing={{}: (2, {})} | custom-call | tf_op jit(solution)/shard_map/transpose_weight/pallas_call | solution.py:135
  274.0 5.9 %turn.3 = (bf16[32,2560]{1,0:T(8,128)(2,1)S(1)}, bf16[2,2,32,2560]{3,2,1,0:T(8,128)(2,1)S(1)}, f32[2,1,2560]{2,1,0:T(1,128)S(1)}) custom-call(s32[4]{0:T(128)S(1)} %pad_add_fusion.state, bf16[32,2560]{1,0:T(8,128)(2,1)S(1)} %get-tuple-element.150.fresh, ...), custom_call_target="tpu_custom_call", output_to_operand_aliasing={{1}: (6, {}), {2}: (7, {})} | custom-call | tf_op jit(solution)/shard_map/turn/pallas_call | solution.py:243
  282.4 4.4 %backward.16 = (bf16[32,2560]{1,0:T(8,128)(2,1)S(1)}, bf16[2,2,32,2560]{3,2,1,0:T(8,128)(2,1)S(1)}, f32[2,1,2560]{2,1,0:T(1,128)S(1)}) custom-call(s32[4]{0:T(128)S(1)} %pad_add_fusion.state, bf16[32,2560]{1,0:T(8,128)(2,1)S(1)} %collective-permute-done.38.received, ...), custom_call_target="tpu_custom_call", output_to_operand_aliasing={{1}: (6, {}), {2}: (7, {})} | custom-call | tf_op jit(solution)/shard_map/backward/pallas_call | solution.py:243
  290.7 4.6 %backward.19 = (bf16[32,2560]{1,0:T(8,128)(2,1)S(1)}, bf16[2,2,32,2560]{3,2,1,0:T(8,128)(2,1)S(1)}, f32[2,1,2560]{2,1,0:T(1,128)S(1)}) custom-call(s32[4]{0:T(128)S(1)} %pad_add_fusion.state, bf16[32,2560]{1,0:T(8,128)(2,1)S(1)} %collective-permute-done.43.received, ...), custom_call_target="tpu_custom_call", output_to_operand_aliasing={{1}: (6, {}), {2}: (7, {})} | custom-call | tf_op jit(solution)/shard_map/backward/pallas_call | solution.py:243
  304.5 89.9 %collective-permute-done.48.received = bf16[32,2560]{1,0:T(8,128)(2,1)S(1)} collective-permute-done((bf16[32,2560]{1,0:T(8,128)(2,1)S(1)}, bf16[32,2560]{1,0:T(8,128)(2,1)S(1)}, u32[]{:S(2)}, u32[]{:S(2)}) %collective-permute-start.48) | collective-permute-done | bytes 163872 | tf_op jit(solution)/shard_map/ppermute | solution.py:325
  396.9 6.5 %backward.26 = (bf16[32,2560]{1,0:T(8,128)(2,1)}, bf16[2,2,32,2560]{3,2,1,0:T(8,128)(2,1)S(1)}, f32[2,1,2560]{2,1,0:T(1,128)S(1)}) custom-call(s32[4]{0:T(128)S(1)} %pad_add_fusion.state, bf16[32,2560]{1,0:T(8,128)(2,1)S(1)} %collective-permute-done.48.received, ...), custom_call_target="tpu_custom_call", output_to_operand_aliasing={{1}: (6, {}), {2}: (7, {})} | custom-call | tf_op jit(solution)/shard_map/backward/pallas_call | solution.py:243
  403.4 8.3 %collective-permute-done.50.received = bf16[32,2560]{1,0:T(8,128)(2,1)S(1)} collective-permute-done((bf16[32,2560]{1,0:T(8,128)(2,1)S(1)}, bf16[32,2560]{1,0:T(8,128)(2,1)S(1)}, u32[]{:S(2)}, u32[]{:S(2)}) %collective-permute-start.50) | collective-permute-done | bytes 163872 | tf_op jit(solution)/shard_map/ppermute | solution.py:325
  411.7 6.2 %backward.27 = (bf16[32,2560]{1,0:T(8,128)(2,1)}, bf16[2,2,32,2560]{3,2,1,0:T(8,128)(2,1)S(1)}, f32[2,1,2560]{2,1,0:T(1,128)S(1)}) custom-call(s32[4]{0:T(128)S(1)} %pad_add_fusion.state, bf16[32,2560]{1,0:T(8,128)(2,1)S(1)} %collective-permute-done.50.received, ...), custom_call_target="tpu_custom_call", output_to_operand_aliasing={{1}: (6, {}), {2}: (7, {})} | custom-call | tf_op jit(solution)/shard_map/backward/pallas_call | solution.py:243
  418.0 16.3 %collective-permute-start.51 = (bf16[80,2560]{1,0:T(8,128)(2,1)S(1)}, bf16[80,2560]{1,0:T(8,128)(2,1)S(1)}, u32[]{:S(2)}, u32[]{:S(2)}) collective-permute-start(bf16[80,2560]{1,0:T(8,128)(2,1)S(1)} %pack.1), channel_id=1, source_target_pairs={{0,32},{32,0},{64,96},{96,64},{128,160},{160,128},{192,224},{224,1... | collective-permute-start | bytes 1228808 | tf_op jit(solution)/shard_map/ppermute | solution.py:269
  (168 shorter events, 103.8 us)
Async XLA Ops:
  1.7 48.4 %collective-permute-start.2 = (bf16[80,1280]{1,0:T(8,128)(2,1)S(1)}, bf16[80,1280]{1,0:T(8,128)(2,1)S(1)}, u32[]{:S(2)}, u32[]{:S(2)}) collective-permute-start(bf16[80,1280]{1,0:T(8,128)(2,1)S(1)} %get-tuple-element.263), channel_id=1, source_target_pairs={{0,24},{1,25},{2,26},{3,27},{4,28},{5,29},{6,30},{7,31},{8,0},{9,1... | collective-permute-start | bytes 614408 | tf_op jit(solution)/shard_map/ppermute | solution.py:281
  8.4 22.9 %collective-permute-start.1 = (bf16[80,1280]{1,0:T(8,128)(2,1)S(1)}, bf16[80,1280]{1,0:T(8,128)(2,1)S(1)}, u32[]{:S(2)}, u32[]{:S(2)}) collective-permute-start(bf16[80,1280]{1,0:T(8,128)(2,1)S(1)} %get-tuple-element.263), channel_id=1, source_target_pairs={{0,8},{1,9},{2,10},{3,11},{4,12},{5,13},{6,14},{7,15},{8,16},{9,17... | collective-permute-start | bytes 614408 | tf_op jit(solution)/shard_map/ppermute | solution.py:281
  10.3 20.2 %collective-permute-start = (f32[1,2560]{1,0:T(1,128)}, f32[1,2560]{1,0:T(1,128)S(1)}, u32[]{:S(2)}, u32[]{:S(2)}) collective-permute-start(f32[1,2560]{1,0:T(1,128)} %param.9), channel_id=1, source_target_pairs={{0,32},{32,0},{64,96},{96,64},{128,160},{160,128},{192,224},{224,1... | collective-permute-start | bytes 30728 | tf_op jit(solution)/shard_map/ppermute | solution.py:269
  20.2 22.0 %all-to-all-start = ((bf16[32,2,1280]{2,1,0:T(2,128)(2,1)}), bf16[32,2,1280]{2,1,0:T(2,128)(2,1)S(1)}, u32[]{:S(2)}, u32[]{:S(2)}) async-start(bf16[32,2,1280]{2,1,0:T(2,128)(2,1)} %reshape.85), calls=%async_computation | async-start | bytes 327680 | tf_op jit(solution)/shard_map/all_to_all | solution.py:288
  31.3 18.8 %collective-permute-start.3 = (bf16[80,1280]{1,0:T(8,128)(2,1)S(1)}, bf16[80,1280]{1,0:T(8,128)(2,1)S(1)}, u32[]{:S(2)}, u32[]{:S(2)}) collective-permute-start(bf16[80,1280]{1,0:T(8,128)(2,1)S(1)} %collective-permute-done.1), channel_id=1, source_target_pairs={{0,8},{1,9},{2,10},{3,11},{4,12},{5,13},{6,14},{7,15},{8,16},{9,17... | collective-permute-start | bytes 614408 | tf_op jit(solution)/shard_map/ppermute | solution.py:281
  43.9 17.3 %collective-permute-start.9 = (bf16[80,1280]{1,0:T(8,128)(2,1)S(1)}, bf16[80,1280]{1,0:T(8,128)(2,1)S(1)}, u32[]{:S(2)}, u32[]{:S(2)}) collective-permute-start(bf16[80,1280]{1,0:T(8,128)(2,1)S(1)} %get-tuple-element.136), channel_id=1, source_target_pairs={{0,24},{1,25},{2,26},{3,27},{4,28},{5,29},{6,30},{7,31},{8,0},{9,1... | collective-permute-start | bytes 614408 | tf_op jit(solution)/shard_map/ppermute | solution.py:281
  46.8 10.3 %collective-permute-start.8 = (bf16[80,1280]{1,0:T(8,128)(2,1)S(1)}, bf16[80,1280]{1,0:T(8,128)(2,1)S(1)}, u32[]{:S(2)}, u32[]{:S(2)}) collective-permute-start(bf16[80,1280]{1,0:T(8,128)(2,1)S(1)} %get-tuple-element.136), channel_id=1, source_target_pairs={{0,8},{1,9},{2,10},{3,11},{4,12},{5,13},{6,14},{7,15},{8,16},{9,17... | collective-permute-start | bytes 614408 | tf_op jit(solution)/shard_map/ppermute | solution.py:281
  50.2 23.5 %collective-permute-start.5 = (bf16[320,1280]{1,0:T(8,128)(2,1)S(1)}, bf16[320,1280]{1,0:T(8,128)(2,1)S(1)}, u32[]{:S(2)}, u32[]{:S(2)}) collective-permute-start(bf16[320,1280]{1,0:T(8,128)(2,1)S(1)} %pad_maximum_fusion.refs_0_), channel_id=1, source_target_pairs={{0,7},{1,0},{2,1},{3,2},{4,3},{5,4},{6,5},{7,6},{8,15},{9,8},{10,9... | collective-permute-start | bytes 2457608 | tf_op jit(solution)/shard_map/ppermute | solution.py:281
  52.6 21.2 %collective-permute-start.4 = (bf16[320,1280]{1,0:T(8,128)(2,1)S(1)}, bf16[320,1280]{1,0:T(8,128)(2,1)S(1)}, u32[]{:S(2)}, u32[]{:S(2)}) collective-permute-start(bf16[320,1280]{1,0:T(8,128)(2,1)S(1)} %pad_maximum_fusion.refs_0_), channel_id=1, source_target_pairs={{0,1},{1,2},{2,3},{3,4},{4,5},{5,6},{6,7},{7,0},{8,9},{9,10},{10,1... | collective-permute-start | bytes 2457608 | tf_op jit(solution)/shard_map/ppermute | solution.py:281
  57.1 10.8 %collective-permute-start.10 = (bf16[80,1280]{1,0:T(8,128)(2,1)S(1)}, bf16[80,1280]{1,0:T(8,128)(2,1)S(1)}, u32[]{:S(2)}, u32[]{:S(2)}) collective-permute-start(bf16[80,1280]{1,0:T(8,128)(2,1)S(1)} %collective-permute-done.8), channel_id=1, source_target_pairs={{0,8},{1,9},{2,10},{3,11},{4,12},{5,13},{6,14},{7,15},{8,16},{9,17... | collective-permute-start | bytes 614408 | tf_op jit(solution)/shard_map/ppermute | solution.py:281
  67.9 18.3 %collective-permute-start.12 = (bf16[320,1280]{1,0:T(8,128)(2,1)S(1)}, bf16[320,1280]{1,0:T(8,128)(2,1)S(1)}, u32[]{:S(2)}, u32[]{:S(2)}) collective-permute-start(bf16[320,1280]{1,0:T(8,128)(2,1)S(1)} %constant_dynamic-update-slice_fusion.refs_5_), channel_id=1, source_target_pairs={{0,7},{1,0},{2,1},{3,2},{4,3},{5,4},{6,5},{7,6},{8,15},{9,8},{10,9... | collective-permute-start | bytes 2457608 | tf_op jit(solution)/shard_map/ppermute | solution.py:281
  71.8 20.1 %collective-permute-start.11 = (bf16[320,1280]{1,0:T(8,128)(2,1)S(1)}, bf16[320,1280]{1,0:T(8,128)(2,1)S(1)}, u32[]{:S(2)}, u32[]{:S(2)}) collective-permute-start(bf16[320,1280]{1,0:T(8,128)(2,1)S(1)} %constant_dynamic-update-slice_fusion.refs_5_), channel_id=1, source_target_pairs={{0,1},{1,2},{2,3},{3,4},{4,5},{5,6},{6,7},{7,0},{8,9},{9,10},{10,1... | collective-permute-start | bytes 2457608 | tf_op jit(solution)/shard_map/ppermute | solution.py:281
  73.8 35.6 %collective-permute-start.6 = (bf16[320,1280]{1,0:T(8,128)(2,1)S(1)}, bf16[320,1280]{1,0:T(8,128)(2,1)S(1)}, u32[]{:S(2)}, u32[]{:S(2)}) collective-permute-start(bf16[320,1280]{1,0:T(8,128)(2,1)S(1)} %collective-permute-done.4.refs_1_), channel_id=1, source_target_pairs={{0,1},{1,2},{2,3},{3,4},{4,5},{5,6},{6,7},{7,0},{8,9},{9,10},{10,1... | collective-permute-start | bytes 2457608 | tf_op jit(solution)/shard_map/ppermute | solution.py:281
  77.1 32.3 %collective-permute-start.7 = (bf16[320,1280]{1,0:T(8,128)(2,1)S(1)}, bf16[320,1280]{1,0:T(8,128)(2,1)S(1)}, u32[]{:S(2)}, u32[]{:S(2)}) collective-permute-start(bf16[320,1280]{1,0:T(8,128)(2,1)S(1)} %collective-permute-done.5.refs_2_), channel_id=1, source_target_pairs={{0,7},{1,0},{2,1},{3,2},{4,3},{5,4},{6,5},{7,6},{8,15},{9,8},{10,9... | collective-permute-start | bytes 2457608 | tf_op jit(solution)/shard_map/ppermute | solution.py:281
  91.8 35.1 %collective-permute-start.13 = (bf16[320,1280]{1,0:T(8,128)(2,1)S(1)}, bf16[320,1280]{1,0:T(8,128)(2,1)S(1)}, u32[]{:S(2)}, u32[]{:S(2)}) collective-permute-start(bf16[320,1280]{1,0:T(8,128)(2,1)S(1)} %collective-permute-done.11.refs_6_), channel_id=1, source_target_pairs={{0,1},{1,2},{2,3},{3,4},{4,5},{5,6},{6,7},{7,0},{8,9},{9,10},{10,1... | collective-permute-start | bytes 2457608 | tf_op jit(solution)/shard_map/ppermute | solution.py:281
  93.8 33.2 %collective-permute-start.14 = (bf16[320,1280]{1,0:T(8,128)(2,1)S(1)}, bf16[320,1280]{1,0:T(8,128)(2,1)S(1)}, u32[]{:S(2)}, u32[]{:S(2)}) collective-permute-start(bf16[320,1280]{1,0:T(8,128)(2,1)S(1)} %collective-permute-done.12.refs_7_), channel_id=1, source_target_pairs={{0,7},{1,0},{2,1},{3,2},{4,3},{5,4},{6,5},{7,6},{8,15},{9,8},{10,9... | collective-permute-start | bytes 2457608 | tf_op jit(solution)/shard_map/ppermute | solution.py:281
  109.4 35.1 %collective-permute-start.15 = (bf16[320,1280]{1,0:T(8,128)(2,1)S(1)}, bf16[320,1280]{1,0:T(8,128)(2,1)S(1)}, u32[]{:S(2)}, u32[]{:S(2)}) collective-permute-start(bf16[320,1280]{1,0:T(8,128)(2,1)S(1)} %collective-permute-done.6.refs_3_), channel_id=1, source_target_pairs={{0,1},{1,2},{2,3},{3,4},{4,5},{5,6},{6,7},{7,0},{8,9},{9,10},{10,1... | collective-permute-start | bytes 2457608 | tf_op jit(solution)/shard_map/ppermute | solution.py:281
  111.3 33.2 %collective-permute-start.16 = (bf16[320,1280]{1,0:T(8,128)(2,1)S(1)}, bf16[320,1280]{1,0:T(8,128)(2,1)S(1)}, u32[]{:S(2)}, u32[]{:S(2)}) collective-permute-start(bf16[320,1280]{1,0:T(8,128)(2,1)S(1)} %collective-permute-done.7.refs_4_), channel_id=1, source_target_pairs={{0,7},{1,0},{2,1},{3,2},{4,3},{5,4},{6,5},{7,6},{8,15},{9,8},{10,9... | collective-permute-start | bytes 2457608 | tf_op jit(solution)/shard_map/ppermute | solution.py:281
  127.0 35.1 %collective-permute-start.17 = (bf16[320,1280]{1,0:T(8,128)(2,1)S(1)}, bf16[320,1280]{1,0:T(8,128)(2,1)S(1)}, u32[]{:S(2)}, u32[]{:S(2)}) collective-permute-start(bf16[320,1280]{1,0:T(8,128)(2,1)S(1)} %collective-permute-done.13.refs_8_), channel_id=1, source_target_pairs={{0,1},{1,2},{2,3},{3,4},{4,5},{5,6},{6,7},{7,0},{8,9},{9,10},{10,1... | collective-permute-start | bytes 2457608 | tf_op jit(solution)/shard_map/ppermute | solution.py:281
  128.9 33.2 %collective-permute-start.18 = (bf16[320,1280]{1,0:T(8,128)(2,1)S(1)}, bf16[320,1280]{1,0:T(8,128)(2,1)S(1)}, u32[]{:S(2)}, u32[]{:S(2)}) collective-permute-start(bf16[320,1280]{1,0:T(8,128)(2,1)S(1)} %collective-permute-done.14.refs_9_), channel_id=1, source_target_pairs={{0,7},{1,0},{2,1},{3,2},{4,3},{5,4},{6,5},{7,6},{8,15},{9,8},{10,9... | collective-permute-start | bytes 2457608 | tf_op jit(solution)/shard_map/ppermute | solution.py:281
  169.2 38.2 %collective-permute-start.22 = (bf16[1600,2560]{1,0:T(8,128)(2,1)}, bf16[1600,2560]{1,0:T(8,128)(2,1)}, u32[]{:S(2)}, u32[]{:S(2)}) collective-permute-start(bf16[1600,2560]{1,0:T(8,128)(2,1)} %assemble.3.rest_0_), channel_id=1, source_target_pairs={{0,32},{32,0},{64,96},{96,64},{128,160},{160,128},{192,224},{224,1... | collective-permute-start | bytes 24576008 | tf_op jit(solution)/shard_map/ppermute | solution.py:269
  175.3 23.0 %collective-permute-start.19 = (bf16[320,1280]{1,0:T(8,128)(2,1)S(1)}, bf16[320,1280]{1,0:T(8,128)(2,1)S(1)}, u32[]{:S(2)}, u32[]{:S(2)}) collective-permute-start(bf16[320,1280]{1,0:T(8,128)(2,1)S(1)} %collective-permute-done.15.refs_0_), channel_id=1, source_target_pairs={{0,1},{1,2},{2,3},{3,4},{4,5},{5,6},{6,7},{7,0},{8,9},{9,10},{10,1... | collective-permute-start | bytes 2457608 | tf_op jit(solution)/shard_map/ppermute | solution.py:281
  177.2 21.9 %collective-permute-start.20 = (bf16[320,1280]{1,0:T(8,128)(2,1)S(1)}, bf16[320,1280]{1,0:T(8,128)(2,1)S(1)}, u32[]{:S(2)}, u32[]{:S(2)}) collective-permute-start(bf16[320,1280]{1,0:T(8,128)(2,1)S(1)} %collective-permute-done.18.refs_4_), channel_id=1, source_target_pairs={{0,7},{1,0},{2,1},{3,2},{4,3},{5,4},{6,5},{7,6},{8,15},{9,8},{10,9... | collective-permute-start | bytes 2457608 | tf_op jit(solution)/shard_map/ppermute | solution.py:281
  204.3 11.3 %collective-permute-start.21 = (bf16[960,2560]{1,0:T(8,128)(2,1)}, bf16[960,2560]{1,0:T(8,128)(2,1)}, u32[]{:S(2)}, u32[]{:S(2)}) collective-permute-start(bf16[960,2560]{1,0:T(8,128)(2,1)} %assemble.2.rest_1_), channel_id=1, source_target_pairs={{0,32},{32,0},{64,96},{96,64},{128,160},{160,128},{192,224},{224,1... | collective-permute-start | bytes 14745608 | tf_op jit(solution)/shard_map/ppermute | solution.py:269
  224.8 7.5 %collective-permute-start.23 = (bf16[32,2560]{1,0:T(8,128)(2,1)S(1)}, bf16[32,2560]{1,0:T(8,128)(2,1)S(1)}, u32[]{:S(2)}, u32[]{:S(2)}) collective-permute-start(bf16[32,2560]{1,0:T(8,128)(2,1)S(1)} %get-tuple-element.171), channel_id=1, source_target_pairs={{0,64},{32,96},{1,65},{33,97},{2,66},{34,98},{3,67},{35,99},{4,68}... | collective-permute-start | bytes 491528 | tf_op jit(solution)/shard_map/ppermute | solution.py:325
  233.6 12.6 %collective-permute-start.25 = (bf16[32,2560]{1,0:T(8,128)(2,1)S(1)}, bf16[32,2560]{1,0:T(8,128)(2,1)S(1)}, u32[]{:S(2)}, u32[]{:S(2)}) collective-permute-start(bf16[32,2560]{1,0:T(8,128)(2,1)S(1)} %get-tuple-element.174), channel_id=1, source_target_pairs={{0,64},{32,96},{1,65},{33,97},{2,66},{34,98},{3,67},{35,99},{4,68}... | collective-permute-start | bytes 491528 | tf_op jit(solution)/shard_map/ppermute | solution.py:325
  272.1 1.9 collective-permute-start.36
  273.3 6.6 %collective-permute-start.37 = (bf16[32,2560]{1,0:T(8,128)(2,1)S(1)}, bf16[32,2560]{1,0:T(8,128)(2,1)S(1)}, u32[]{:S(2)}, u32[]{:S(2)}) collective-permute-start(bf16[32,2560]{1,0:T(8,128)(2,1)S(1)} %get-tuple-element.207), channel_id=1, source_target_pairs={{448,384},{480,416},{449,385},{481,417},{450,386},{482,418},{451,3... | collective-permute-start | bytes 491528 | tf_op jit(solution)/shard_map/ppermute | solution.py:325
  299.1 3.0 collective-permute-start.47
  303.2 91.2 %collective-permute-start.48 = (bf16[32,2560]{1,0:T(8,128)(2,1)S(1)}, bf16[32,2560]{1,0:T(8,128)(2,1)S(1)}, u32[]{:S(2)}, u32[]{:S(2)}) collective-permute-start(bf16[32,2560]{1,0:T(8,128)(2,1)S(1)} %get-tuple-element.246), channel_id=1, source_target_pairs={{64,0},{96,32},{65,1},{97,33},{66,2},{98,34},{67,3},{99,35},{68,4}... | collective-permute-start | bytes 491528 | tf_op jit(solution)/shard_map/ppermute | solution.py:325
  395.6 16.1 %collective-permute-start.50 = (bf16[32,2560]{1,0:T(8,128)(2,1)S(1)}, bf16[32,2560]{1,0:T(8,128)(2,1)S(1)}, u32[]{:S(2)}, u32[]{:S(2)}) collective-permute-start(bf16[32,2560]{1,0:T(8,128)(2,1)S(1)} %get-tuple-element.251), channel_id=1, source_target_pairs={{64,0},{96,32},{65,1},{97,33},{66,2},{98,34},{67,3},{99,35},{68,4}... | collective-permute-start | bytes 491528 | tf_op jit(solution)/shard_map/ppermute | solution.py:325
  418.0 17.6 %collective-permute-start.51 = (bf16[80,2560]{1,0:T(8,128)(2,1)S(1)}, bf16[80,2560]{1,0:T(8,128)(2,1)S(1)}, u32[]{:S(2)}, u32[]{:S(2)}) collective-permute-start(bf16[80,2560]{1,0:T(8,128)(2,1)S(1)} %pack.1), channel_id=1, source_target_pairs={{0,32},{32,0},{64,96},{96,64},{128,160},{160,128},{192,224},{224,1... | collective-permute-start | bytes 1228808 | tf_op jit(solution)/shard_map/ppermute | solution.py:269
  (39 other events, 874.8 us)

commit v5 on v3

--- a/solution.py
+++ b/solution.py
@@ -282,17 +282,13 @@
 
     def first_block(shard):
         above, below = over(shard, 1, 0), over(shard, -1, 0)
-        return jnp.concatenate([shard, above, below, over(above, 1, 0)], 0)
-
-    bucket = prev_grads[0, 0].astype(BF16)
-    pieces = lax.all_to_all(bucket, "dp", 0, 0, tiled=True).astype(F32)
-    summed = jnp.sum(pieces, axis=0, keepdims=True)
-    new_momentum = 0.9 * momentum + (summed / lax.axis_size("dp"))[None]
+        return above, jnp.concatenate([shard, above, below, over(above, 1, 0)], 0)
 
     half = width // 2
     shards = [weight[0, :, :half], weight[0, :, half:]]
-    shards[1], new_momentum = lax.optimization_barrier((shards[1], new_momentum))
-    blocks = [first_block(shard) for shard in shards]
+    above, block = first_block(shards[0])
+    shards[1], _ = lax.optimization_barrier((shards[1], above))
+    blocks = [block, first_block(shards[1])[1]]
     rings = [[(block, block)] for block in blocks]
     for step in range(3):
         for ring in rings:
@@ -303,18 +299,29 @@
     inner, rings[0][3], rings[1][3] = lax.optimization_barrier((inner, rings[0][3], rings[1][3]))
     inner = assemble(*inner)
     inner_other = swap(inner)
-
+    own_gain, inner = lax.optimization_barrier((gain, inner))
+    gains = ordered(gain, swap(own_gain))
+    ends, gains = lax.optimization_barrier((ends, gains))
+
+    bucket, inner_other = lax.optimization_barrier((prev_grads[0, 0].astype(BF16), inner_other))
+    pieces = lax.all_to_all(bucket, "dp", 0, 0, tiled=True).astype(F32)
+    summed = jnp.sum(pieces, axis=0, keepdims=True)
+    new_momentum = 0.9 * momentum + (summed / lax.axis_size("dp"))[None]
+
+
+    ends, new_momentum = lax.optimization_barrier((ends, new_momentum))
     outer = assemble(*[[*ring[3], end] for ring, end in zip(rings, ends)])
     outer_other = swap(outer)
 
-    gains = ordered(gain, swap(gain))
     replica = lax.axis_index("dp")
     state = jnp.stack([stage, core, replica // 8, lax.rem(replica, 8)]).astype(jnp.int32)
     fresh = lax.dynamic_slice_in_dim(inputs, core * parts, parts, 0)
     target = lax.dynamic_slice_in_dim(cotangent, core * parts, parts, 0)
     fresh = [fresh[m] for m in range(parts)]
     target = [target[m] for m in range(parts)]
-    gains, state, fresh, target, outer = lax.optimization_barrier((gains, state, fresh, target, outer))
+    gains, state, fresh, target, outer, new_momentum = lax.optimization_barrier(
+        (gains, state, fresh, target, outer, new_momentum)
+    )
     near, far = (0, -1, 1, -2, 2), (-3, 3, 4)
     buffers = place(state, ((0, near), (0, far), (1, near)), [inner, outer, inner_other], [])
     weights, turned = place(state, ((1, far),), [outer_other], buffers)

time: 431 us -> 442 us (1.026)
  waiting for transfers between devices: 184 us -> 203 us
  starting transfers between devices: 138 us -> 132 us
    ppermute x20, waiting for transfers between devices: 85.8 us -> 102 us  [over(): return lax.ppermute(array, 'dp', pairs)]
    ppermute x20, starting transfers between devices: 64 us -> 79.1 us  [over(): return lax.ppermute(array, 'dp', pairs)]
    all_to_all x1, starting transfers between devices: 16.5 us -> 3.86 us  [per_device(): pieces = lax.all_to_all(bucket, 'dp', 0, 0, tiled=True).astype(F32)]
    ppermute x4, starting transfers between devices: 33.1 us -> 25.6 us  [swap(): return lax.ppermute(array, 'section', siblings)]
  transfers between devices with their start and end apart: 53 -> 53, of which waited for: 15 -> 16; matrix products, arithmetic and copies ran while one was open for 1% -> 1% of each run, Pallas kernels for 16% -> 15%
where the time goes in v5:
time: 442 us; the launch traced here: 434 us
  waiting for transfers between devices  203 us (46%)
  starting transfers between devices  132 us (30%)
  Pallas kernels  90.5 us (20%)
    ppermute x20, waiting for transfers between devices, over(): return lax.ppermute(array, 'dp', pairs)  102 us
    ppermute x28, waiting for transfers between devices, hop(): lax.ppermute(array, 'section', [(2 * k + c, 2 * to + c) for c in range(2)])  92.4 us
    ppermute x20, starting transfers between devices, over(): return lax.ppermute(array, 'dp', pairs)  79.1 us
    pallas_call x16, Pallas kernels, backward(): pl.pallas_call(kernel, out_shape=[jax.ShapeDtypeStruct((rows, width), BF1...  35 us
    ppermute x4, starting transfers between devices, swap(): return lax.ppermute(array, 'section', siblings)  25.6 us
    pallas_call x14, Pallas kernels, forward(): pl.pallas_call(functools.partial(forward_kernel, k, part), out_shape=[jax...  24.9 us
    ppermute x28, starting transfers between devices, hop(): lax.ppermute(array, 'section', [(2 * k + c, 2 * to + c) for c in range(2)])  23.8 us
    pallas_call x2, Pallas kernels, place(): pl.pallas_call(functools.partial(place_kernel, layouts), out_shape=[pltpu...  11.1 us
  transfers between devices with their start and end apart: 53, of which 16 were waited for; matrix products, arithmetic and copies ran while one was open for 1% of the time, Pallas kernels for 15%

profile of v5, /device:TPU:1, one launch (start us, length us, event | category | flops | bytes accessed | tf_op | source)
XLA Modules:
  0.0 434.0 jit_solution(17042354257213926354)
XLA Ops:
  1.7 5.0 %collective-permute-start = (bf16[80,1280]{1,0:T(8,128)(2,1)S(1)}, bf16[80,1280]{1,0:T(8,128)(2,1)S(1)}, u32[]{:S(2)}, u32[]{:S(2)}) collective-permute-start(bf16[80,1280]{1,0:T(8,128)(2,1)S(1)} %get-tuple-element.282), channel_id=1, source_target_pairs={{0,8},{1,9},{2,10},{3,11},{4,12},{5,13},{6,14},{7,15},{8,16},{9,17... | collective-permute-start | bytes 614408 | tf_op jit(solution)/shard_map/ppermute | solution.py:281
  12.5 7.2 %collective-permute-start.11 = (bf16[80,1280]{1,0:T(8,128)(2,1)S(1)}, bf16[80,1280]{1,0:T(8,128)(2,1)S(1)}, u32[]{:S(2)}, u32[]{:S(2)}) collective-permute-start(bf16[80,1280]{1,0:T(8,128)(2,1)S(1)} %get-tuple-element.145), channel_id=1, source_target_pairs={{0,24},{1,25},{2,26},{3,27},{4,28},{5,29},{6,30},{7,31},{8,0},{9,1... | collective-permute-start | bytes 614408 | tf_op jit(solution)/shard_map/ppermute | solution.py:281
  22.1 6.2 %collective-permute-start.2 = (bf16[80,1280]{1,0:T(8,128)(2,1)S(1)}, bf16[80,1280]{1,0:T(8,128)(2,1)S(1)}, u32[]{:S(2)}, u32[]{:S(2)}) collective-permute-start(bf16[80,1280]{1,0:T(8,128)(2,1)S(1)} %collective-permute-done), channel_id=1, source_target_pairs={{0,8},{1,9},{2,10},{3,11},{4,12},{5,13},{6,14},{7,15},{8,16},{9,17... | collective-permute-start | bytes 614408 | tf_op jit(solution)/shard_map/ppermute | solution.py:281
  28.4 15.5 %collective-permute-done.2 = bf16[80,1280]{1,0:T(8,128)(2,1)S(1)} collective-permute-done((bf16[80,1280]{1,0:T(8,128)(2,1)S(1)}, bf16[80,1280]{1,0:T(8,128)(2,1)S(1)}, u32[]{:S(2)}, u32[]{:S(2)}) %collective-permute-start.2) | collective-permute-done | bytes 204832 | tf_op jit(solution)/shard_map/ppermute | solution.py:281
  44.0 11.6 %collective-permute-start.4 = (bf16[320,1280]{1,0:T(8,128)(2,1)S(1)}, bf16[320,1280]{1,0:T(8,128)(2,1)S(1)}, u32[]{:S(2)}, u32[]{:S(2)}) collective-permute-start(bf16[320,1280]{1,0:T(8,128)(2,1)S(1)} %pad_maximum_fusion.refs_0_), channel_id=1, source_target_pairs={{0,7},{1,0},{2,1},{3,2},{4,3},{5,4},{6,5},{7,6},{8,15},{9,8},{10,9... | collective-permute-start | bytes 2457608 | tf_op jit(solution)/shard_map/ppermute | solution.py:281
  59.6 12.4 %collective-permute-done.12 = bf16[80,1280]{1,0:T(8,128)(2,1)S(1)} collective-permute-done((bf16[80,1280]{1,0:T(8,128)(2,1)S(1)}, bf16[80,1280]{1,0:T(8,128)(2,1)S(1)}, u32[]{:S(2)}, u32[]{:S(2)}) %collective-permute-start.12) | collective-permute-done | bytes 204832 | tf_op jit(solution)/shard_map/ppermute | solution.py:281
  72.0 4.7 %collective-permute-start.14 = (bf16[320,1280]{1,0:T(8,128)(2,1)S(1)}, bf16[320,1280]{1,0:T(8,128)(2,1)S(1)}, u32[]{:S(2)}, u32[]{:S(2)}) collective-permute-start(bf16[320,1280]{1,0:T(8,128)(2,1)S(1)} %constant_dynamic-update-slice_fusion.refs_5_), channel_id=1, source_target_pairs={{0,7},{1,0},{2,1},{3,2},{4,3},{5,4},{6,5},{7,6},{8,15},{9,8},{10,9... | collective-permute-start | bytes 2457608 | tf_op jit(solution)/shard_map/ppermute | solution.py:281
  80.6 4.6 %collective-permute-start.6 = (bf16[320,1280]{1,0:T(8,128)(2,1)S(1)}, bf16[320,1280]{1,0:T(8,128)(2,1)S(1)}, u32[]{:S(2)}, u32[]{:S(2)}) collective-permute-start(bf16[320,1280]{1,0:T(8,128)(2,1)S(1)} %collective-permute-done.4.refs_2_), channel_id=1, source_target_pairs={{0,7},{1,0},{2,1},{3,2},{4,3},{5,4},{6,5},{7,6},{8,15},{9,8},{10,9... | collective-permute-start | bytes 2457608 | tf_op jit(solution)/shard_map/ppermute | solution.py:281
  85.2 8.1 %collective-permute-done.14.refs_7_ = bf16[320,1280]{1,0:T(8,128)(2,1)S(1)} collective-permute-done((bf16[320,1280]{1,0:T(8,128)(2,1)S(1)}, bf16[320,1280]{1,0:T(8,128)(2,1)S(1)}, u32[]{:S(2)}, u32[]{:S(2)}) %collective-permute-start.14) | collective-permute-done | bytes 819232 | tf_op jit(solution)/shard_map/ppermute | solution.py:281
  93.3 5.0 %collective-permute-done.13.refs_6_ = bf16[320,1280]{1,0:T(8,128)(2,1)S(1)} collective-permute-done((bf16[320,1280]{1,0:T(8,128)(2,1)S(1)}, bf16[320,1280]{1,0:T(8,128)(2,1)S(1)}, u32[]{:S(2)}, u32[]{:S(2)}) %collective-permute-start.13) | collective-permute-done | bytes 819232 | tf_op jit(solution)/shard_map/ppermute | solution.py:281
  100.2 4.6 %collective-permute-start.16 = (bf16[320,1280]{1,0:T(8,128)(2,1)S(1)}, bf16[320,1280]{1,0:T(8,128)(2,1)S(1)}, u32[]{:S(2)}, u32[]{:S(2)}) collective-permute-start(bf16[320,1280]{1,0:T(8,128)(2,1)S(1)} %collective-permute-done.14.refs_7_), channel_id=1, source_target_pairs={{0,7},{1,0},{2,1},{3,2},{4,3},{5,4},{6,5},{7,6},{8,15},{9,8},{10,9... | collective-permute-start | bytes 2457608 | tf_op jit(solution)/shard_map/ppermute | solution.py:281
  104.8 11.1 %collective-permute-done.5.refs_3_ = bf16[320,1280]{1,0:T(8,128)(2,1)S(1)} collective-permute-done((bf16[320,1280]{1,0:T(8,128)(2,1)S(1)}, bf16[320,1280]{1,0:T(8,128)(2,1)S(1)}, u32[]{:S(2)}, u32[]{:S(2)}) %collective-permute-start.5) | collective-permute-done | bytes 819232 | tf_op jit(solution)/shard_map/ppermute | solution.py:281
  117.8 4.6 %collective-permute-start.8 = (bf16[320,1280]{1,0:T(8,128)(2,1)S(1)}, bf16[320,1280]{1,0:T(8,128)(2,1)S(1)}, u32[]{:S(2)}, u32[]{:S(2)}) collective-permute-start(bf16[320,1280]{1,0:T(8,128)(2,1)S(1)} %collective-permute-done.6.refs_4_), channel_id=1, source_target_pairs={{0,7},{1,0},{2,1},{3,2},{4,3},{5,4},{6,5},{7,6},{8,15},{9,8},{10,9... | collective-permute-start | bytes 2457608 | tf_op jit(solution)/shard_map/ppermute | solution.py:281
  122.4 11.0 %collective-permute-done.15.refs_8_ = bf16[320,1280]{1,0:T(8,128)(2,1)S(1)} collective-permute-done((bf16[320,1280]{1,0:T(8,128)(2,1)S(1)}, bf16[320,1280]{1,0:T(8,128)(2,1)S(1)}, u32[]{:S(2)}, u32[]{:S(2)}) %collective-permute-start.15) | collective-permute-done | bytes 819232 | tf_op jit(solution)/shard_map/ppermute | solution.py:281
  135.3 4.6 %collective-permute-start.18 = (bf16[320,1280]{1,0:T(8,128)(2,1)S(1)}, bf16[320,1280]{1,0:T(8,128)(2,1)}, u32[]{:S(2)}, u32[]{:S(2)}) collective-permute-start(bf16[320,1280]{1,0:T(8,128)(2,1)S(1)} %collective-permute-done.16.refs_9_), channel_id=1, source_target_pairs={{0,7},{1,0},{2,1},{3,2},{4,3},{5,4},{6,5},{7,6},{8,15},{9,8},{10,9... | collective-permute-start | bytes 2457608 | tf_op jit(solution)/shard_map/ppermute | solution.py:281
  139.9 11.0 %collective-permute-done.7.refs_0_ = bf16[320,1280]{1,0:T(8,128)(2,1)S(1)} collective-permute-done((bf16[320,1280]{1,0:T(8,128)(2,1)S(1)}, bf16[320,1280]{1,0:T(8,128)(2,1)S(1)}, u32[]{:S(2)}, u32[]{:S(2)}) %collective-permute-start.7) | collective-permute-done | bytes 819232 | tf_op jit(solution)/shard_map/ppermute | solution.py:281
  151.0 17.5 %collective-permute-done.17.refs_3_ = bf16[320,1280]{1,0:T(8,128)(2,1)S(1)} collective-permute-done((bf16[320,1280]{1,0:T(8,128)(2,1)S(1)}, bf16[320,1280]{1,0:T(8,128)(2,1)S(1)}, u32[]{:S(2)}, u32[]{:S(2)}) %collective-permute-start.17) | collective-permute-done | bytes 819232 | tf_op jit(solution)/shard_map/ppermute | solution.py:281
  168.6 6.7 %assemble.2.rest_0_ = bf16[1600,2560]{1,0:T(8,128)(2,1)} custom-call(bf16[320,1280]{1,0:T(8,128)(2,1)} %copy-done, bf16[320,1280]{1,0:T(8,128)(2,1)} %copy-done.8, bf16[320,1280]{1,0:T(8,128)(2,1)} %copy-done.7, bf16[320,1280]{1,0:T(8,128)(2,1)} %copy-done.11, bf16[320,1280]{1,0:T(8,128)(2,1)} %copy-done.12, bf16[320,1280]{1,0:T(8,128)(2,1)} %copy-done.1, ...), custom_call_target="tpu_custom_call" | custom-call | tf_op jit(solution)/shard_map/assemble/pallas_call | solution.py:51
  181.4 4.6 %collective-permute-start.19 = (bf16[320,1280]{1,0:T(8,128)(2,1)}, bf16[320,1280]{1,0:T(8,128)(2,1)S(1)}, u32[]{:S(2)}, u32[]{:S(2)}) collective-permute-start(bf16[320,1280]{1,0:T(8,128)(2,1)} %collective-permute-done.18.refs_4_), channel_id=1, source_target_pairs={{0,7},{1,0},{2,1},{3,2},{4,3},{5,4},{6,5},{7,6},{8,15},{9,8},{10,9... | collective-permute-start | bytes 2457608 | tf_op jit(solution)/shard_map/ppermute | solution.py:281
  198.1 4.3 collective-permute-done.9.refs_2_
  210.8 4.3 assemble.3.rest_1_
  219.0 8.1 %place_weight.2 = (bf16[2,2560,2560]{2,1,0:T(8,128)(2,1)S(1)}, bf16[2,2560,2560]{2,1,0:T(8,128)(2,1)S(1)}) custom-call(s32[4]{0:T(128)S(1)} %pad_add_fusion.state, bf16[1600,2560]{1,0:T(8,128)(2,1)} %assemble.2.rest_0_, bf16[960,2560]{1,0:T(8,128)(2,1)} %assemble.3.rest_1_, bf16[1600,2560]{1,0:T(8,128)(2,1)} %collective-permute-done.21.rest_2_), custom_call_target="tpu_custom_call" | custom-call | tf_op jit(solution)/shard_map/place_weight/pallas_call | solution.py:84
  230.7 5.7 %forward.14 = (bf16[32,2560]{1,0:T(8,128)(2,1)S(1)}, bf16[2,2,32,2560]{3,2,1,0:T(8,128)(2,1)S(1)}) custom-call(s32[4]{0:T(128)S(1)} %pad_add_fusion.state, bf16[32,2560]{1,0:T(8,128)(2,1)S(1)} %get-tuple-element.186.arrived, f32[2,2560]{1,0:T(2,128)S(1)} %maximum_select_fusion.1.gains, bf16[2,2560,2560]{2,1,0:T(8,128)(2,1)S(1)} %get-tuple-element.184.weights.rest_0_, ...), custom_call_target="tpu_custom_call" | custom-call | tf_op jit(solution)/shard_map/forward/pallas_call | solution.py:195
  237.7 6.2 %forward.15 = (bf16[32,2560]{1,0:T(8,128)(2,1)S(1)}, bf16[2,2,32,2560]{3,2,1,0:T(8,128)(2,1)S(1)}) custom-call(s32[4]{0:T(128)S(1)} %pad_add_fusion.state, bf16[32,2560]{1,0:T(8,128)(2,1)S(1)} %get-tuple-element.177.arrived, f32[2,2560]{1,0:T(2,128)S(1)} %maximum_select_fusion.1.gains, ...), custom_call_target="tpu_custom_call", output_to_operand_aliasing={{1}: (5, {})} | custom-call | tf_op jit(solution)/shard_map/forward/pallas_call | solution.py:195
  257.5 7.8 %transpose_weight.3.rest_0_.turned = bf16[2,2560,2560]{2,1,0:T(8,128)(2,1)S(1)} custom-call(s32[4]{0:T(128)S(1)} %pad_add_fusion.state, bf16[2,2560,2560]{2,1,0:T(8,128)(2,1)S(1)} %get-tuple-element.184.weights.rest_0_, bf16[2,2560,2560]{2,1,0:T(8,128)(2,1)S(1)} %transpose_weight.2.rest_0_._), custom_call_target="tpu_custom_call", output_to_operand_aliasing={{}: (2, {})} | custom-call | tf_op jit(solution)/shard_map/transpose_weight/pallas_call | solution.py:135
  277.5 5.9 %turn.3 = (bf16[32,2560]{1,0:T(8,128)(2,1)S(1)}, bf16[2,2,32,2560]{3,2,1,0:T(8,128)(2,1)S(1)}, f32[2,1,2560]{2,1,0:T(1,128)S(1)}) custom-call(s32[4]{0:T(128)S(1)} %pad_add_fusion.state, bf16[32,2560]{1,0:T(8,128)(2,1)S(1)} %get-tuple-element.176.fresh, ...), custom_call_target="tpu_custom_call", output_to_operand_aliasing={{1}: (6, {}), {2}: (7, {})} | custom-call | tf_op jit(solution)/shard_map/turn/pallas_call | solution.py:243
  286.6 5.6 %backward.16 = (bf16[32,2560]{1,0:T(8,128)(2,1)S(1)}, bf16[2,2,32,2560]{3,2,1,0:T(8,128)(2,1)S(1)}, f32[2,1,2560]{2,1,0:T(1,128)S(1)}) custom-call(s32[4]{0:T(128)S(1)} %pad_add_fusion.state, bf16[32,2560]{1,0:T(8,128)(2,1)S(1)} %collective-permute-done.39.received, ...), custom_call_target="tpu_custom_call", output_to_operand_aliasing={{1}: (6, {}), {2}: (7, {})} | custom-call | tf_op jit(solution)/shard_map/backward/pallas_call | solution.py:243
  302.6 4.8 %backward.23 = (bf16[32,2560]{1,0:T(8,128)(2,1)S(1)}, bf16[2,2,32,2560]{3,2,1,0:T(8,128)(2,1)S(1)}, f32[2,1,2560]{2,1,0:T(1,128)S(1)}) custom-call(s32[4]{0:T(128)S(1)} %pad_add_fusion.state, bf16[32,2560]{1,0:T(8,128)(2,1)S(1)} %collective-permute-done.46.received, ...), custom_call_target="tpu_custom_call", output_to_operand_aliasing={{1}: (6, {}), {2}: (7, {})} | custom-call | tf_op jit(solution)/shard_map/backward/pallas_call | solution.py:243
  310.5 90.8 %collective-permute-done.49.received = bf16[32,2560]{1,0:T(8,128)(2,1)S(1)} collective-permute-done((bf16[32,2560]{1,0:T(8,128)(2,1)S(1)}, bf16[32,2560]{1,0:T(8,128)(2,1)S(1)}, u32[]{:S(2)}, u32[]{:S(2)}) %collective-permute-start.49) | collective-permute-done | bytes 163872 | tf_op jit(solution)/shard_map/ppermute | solution.py:333
  402.6 6.2 %backward.26 = (bf16[32,2560]{1,0:T(8,128)(2,1)}, bf16[2,2,32,2560]{3,2,1,0:T(8,128)(2,1)S(1)}, f32[2,1,2560]{2,1,0:T(1,128)S(1)}) custom-call(s32[4]{0:T(128)S(1)} %pad_add_fusion.state, bf16[32,2560]{1,0:T(8,128)(2,1)S(1)} %collective-permute-done.49.received, ...), custom_call_target="tpu_custom_call", output_to_operand_aliasing={{1}: (6, {}), {2}: (7, {})} | custom-call | tf_op jit(solution)/shard_map/backward/pallas_call | solution.py:243
  408.9 6.5 %backward.27 = (bf16[32,2560]{1,0:T(8,128)(2,1)}, bf16[2,2,32,2560]{3,2,1,0:T(8,128)(2,1)S(1)}, f32[2,1,2560]{2,1,0:T(1,128)S(1)}) custom-call(s32[4]{0:T(128)S(1)} %pad_add_fusion.state, bf16[32,2560]{1,0:T(8,128)(2,1)S(1)} %collective-permute-done.50.received, ...), custom_call_target="tpu_custom_call", output_to_operand_aliasing={{1}: (6, {}), {2}: (7, {})} | custom-call | tf_op jit(solution)/shard_map/backward/pallas_call | solution.py:243
  415.4 15.3 %collective-permute-start.51 = (bf16[80,2560]{1,0:T(8,128)(2,1)S(1)}, bf16[80,2560]{1,0:T(8,128)(2,1)S(1)}, u32[]{:S(2)}, u32[]{:S(2)}) collective-permute-start(bf16[80,2560]{1,0:T(8,128)(2,1)S(1)} %pack.1), channel_id=1, source_target_pairs={{0,32},{32,0},{64,96},{96,64},{128,160},{160,128},{192,224},{224,1... | collective-permute-start | bytes 1228808 | tf_op jit(solution)/shard_map/ppermute | solution.py:269
  (172 shorter events, 104.2 us)
Async XLA Ops:
  1.7 10.8 %collective-permute-start = (bf16[80,1280]{1,0:T(8,128)(2,1)S(1)}, bf16[80,1280]{1,0:T(8,128)(2,1)S(1)}, u32[]{:S(2)}, u32[]{:S(2)}) collective-permute-start(bf16[80,1280]{1,0:T(8,128)(2,1)S(1)} %get-tuple-element.282), channel_id=1, source_target_pairs={{0,8},{1,9},{2,10},{3,11},{4,12},{5,13},{6,14},{7,15},{8,16},{9,17... | collective-permute-start | bytes 614408 | tf_op jit(solution)/shard_map/ppermute | solution.py:281
  6.7 21.7 %collective-permute-start.1 = (bf16[80,1280]{1,0:T(8,128)(2,1)S(1)}, bf16[80,1280]{1,0:T(8,128)(2,1)S(1)}, u32[]{:S(2)}, u32[]{:S(2)}) collective-permute-start(bf16[80,1280]{1,0:T(8,128)(2,1)S(1)} %get-tuple-element.282), channel_id=1, source_target_pairs={{0,24},{1,25},{2,26},{3,27},{4,28},{5,29},{6,30},{7,31},{8,0},{9,1... | collective-permute-start | bytes 614408 | tf_op jit(solution)/shard_map/ppermute | solution.py:281
  12.5 47.0 %collective-permute-start.11 = (bf16[80,1280]{1,0:T(8,128)(2,1)S(1)}, bf16[80,1280]{1,0:T(8,128)(2,1)S(1)}, u32[]{:S(2)}, u32[]{:S(2)}) collective-permute-start(bf16[80,1280]{1,0:T(8,128)(2,1)S(1)} %get-tuple-element.145), channel_id=1, source_target_pairs={{0,24},{1,25},{2,26},{3,27},{4,28},{5,29},{6,30},{7,31},{8,0},{9,1... | collective-permute-start | bytes 614408 | tf_op jit(solution)/shard_map/ppermute | solution.py:281
  19.7 37.9 %collective-permute-start.10 = (bf16[80,1280]{1,0:T(8,128)(2,1)S(1)}, bf16[80,1280]{1,0:T(8,128)(2,1)S(1)}, u32[]{:S(2)}, u32[]{:S(2)}) collective-permute-start(bf16[80,1280]{1,0:T(8,128)(2,1)S(1)} %get-tuple-element.145), channel_id=1, source_target_pairs={{0,8},{1,9},{2,10},{3,11},{4,12},{5,13},{6,14},{7,15},{8,16},{9,17... | collective-permute-start | bytes 614408 | tf_op jit(solution)/shard_map/ppermute | solution.py:281
  22.1 21.8 %collective-permute-start.2 = (bf16[80,1280]{1,0:T(8,128)(2,1)S(1)}, bf16[80,1280]{1,0:T(8,128)(2,1)S(1)}, u32[]{:S(2)}, u32[]{:S(2)}) collective-permute-start(bf16[80,1280]{1,0:T(8,128)(2,1)S(1)} %collective-permute-done), channel_id=1, source_target_pairs={{0,8},{1,9},{2,10},{3,11},{4,12},{5,13},{6,14},{7,15},{8,16},{9,17... | collective-permute-start | bytes 614408 | tf_op jit(solution)/shard_map/ppermute | solution.py:281
  44.0 34.6 %collective-permute-start.4 = (bf16[320,1280]{1,0:T(8,128)(2,1)S(1)}, bf16[320,1280]{1,0:T(8,128)(2,1)S(1)}, u32[]{:S(2)}, u32[]{:S(2)}) collective-permute-start(bf16[320,1280]{1,0:T(8,128)(2,1)S(1)} %pad_maximum_fusion.refs_0_), channel_id=1, source_target_pairs={{0,7},{1,0},{2,1},{3,2},{4,3},{5,4},{6,5},{7,6},{8,15},{9,8},{10,9... | collective-permute-start | bytes 2457608 | tf_op jit(solution)/shard_map/ppermute | solution.py:281
  55.6 23.0 %collective-permute-start.3 = (bf16[320,1280]{1,0:T(8,128)(2,1)S(1)}, bf16[320,1280]{1,0:T(8,128)(2,1)S(1)}, u32[]{:S(2)}, u32[]{:S(2)}) collective-permute-start(bf16[320,1280]{1,0:T(8,128)(2,1)S(1)} %pad_maximum_fusion.refs_0_), channel_id=1, source_target_pairs={{0,1},{1,2},{2,3},{3,4},{4,5},{5,6},{6,7},{7,0},{8,9},{9,10},{10,1... | collective-permute-start | bytes 2457608 | tf_op jit(solution)/shard_map/ppermute | solution.py:281
  57.6 14.3 %collective-permute-start.12 = (bf16[80,1280]{1,0:T(8,128)(2,1)S(1)}, bf16[80,1280]{1,0:T(8,128)(2,1)S(1)}, u32[]{:S(2)}, u32[]{:S(2)}) collective-permute-start(bf16[80,1280]{1,0:T(8,128)(2,1)S(1)} %collective-permute-done.10), channel_id=1, source_target_pairs={{0,8},{1,9},{2,10},{3,11},{4,12},{5,13},{6,14},{7,15},{8,16},{9,17... | collective-permute-start | bytes 614408 | tf_op jit(solution)/shard_map/ppermute | solution.py:281
  72.0 21.3 %collective-permute-start.14 = (bf16[320,1280]{1,0:T(8,128)(2,1)S(1)}, bf16[320,1280]{1,0:T(8,128)(2,1)S(1)}, u32[]{:S(2)}, u32[]{:S(2)}) collective-permute-start(bf16[320,1280]{1,0:T(8,128)(2,1)S(1)} %constant_dynamic-update-slice_fusion.refs_5_), channel_id=1, source_target_pairs={{0,7},{1,0},{2,1},{3,2},{4,3},{5,4},{6,5},{7,6},{8,15},{9,8},{10,9... | collective-permute-start | bytes 2457608 | tf_op jit(solution)/shard_map/ppermute | solution.py:281
  76.7 21.6 %collective-permute-start.13 = (bf16[320,1280]{1,0:T(8,128)(2,1)S(1)}, bf16[320,1280]{1,0:T(8,128)(2,1)S(1)}, u32[]{:S(2)}, u32[]{:S(2)}) collective-permute-start(bf16[320,1280]{1,0:T(8,128)(2,1)S(1)} %constant_dynamic-update-slice_fusion.refs_5_), channel_id=1, source_target_pairs={{0,1},{1,2},{2,3},{3,4},{4,5},{5,6},{6,7},{7,0},{8,9},{9,10},{10,1... | collective-permute-start | bytes 2457608 | tf_op jit(solution)/shard_map/ppermute | solution.py:281
  78.7 37.2 %collective-permute-start.5 = (bf16[320,1280]{1,0:T(8,128)(2,1)S(1)}, bf16[320,1280]{1,0:T(8,128)(2,1)S(1)}, u32[]{:S(2)}, u32[]{:S(2)}) collective-permute-start(bf16[320,1280]{1,0:T(8,128)(2,1)S(1)} %collective-permute-done.3.refs_1_), channel_id=1, source_target_pairs={{0,1},{1,2},{2,3},{3,4},{4,5},{5,6},{6,7},{7,0},{8,9},{9,10},{10,1... | collective-permute-start | bytes 2457608 | tf_op jit(solution)/shard_map/ppermute | solution.py:281
  80.6 35.3 %collective-permute-start.6 = (bf16[320,1280]{1,0:T(8,128)(2,1)S(1)}, bf16[320,1280]{1,0:T(8,128)(2,1)S(1)}, u32[]{:S(2)}, u32[]{:S(2)}) collective-permute-start(bf16[320,1280]{1,0:T(8,128)(2,1)S(1)} %collective-permute-done.4.refs_2_), channel_id=1, source_target_pairs={{0,7},{1,0},{2,1},{3,2},{4,3},{5,4},{6,5},{7,6},{8,15},{9,8},{10,9... | collective-permute-start | bytes 2457608 | tf_op jit(solution)/shard_map/ppermute | solution.py:281
  98.3 35.1 %collective-permute-start.15 = (bf16[320,1280]{1,0:T(8,128)(2,1)S(1)}, bf16[320,1280]{1,0:T(8,128)(2,1)S(1)}, u32[]{:S(2)}, u32[]{:S(2)}) collective-permute-start(bf16[320,1280]{1,0:T(8,128)(2,1)S(1)} %collective-permute-done.13.refs_6_), channel_id=1, source_target_pairs={{0,1},{1,2},{2,3},{3,4},{4,5},{5,6},{6,7},{7,0},{8,9},{9,10},{10,1... | collective-permute-start | bytes 2457608 | tf_op jit(solution)/shard_map/ppermute | solution.py:281
  100.2 33.2 %collective-permute-start.16 = (bf16[320,1280]{1,0:T(8,128)(2,1)S(1)}, bf16[320,1280]{1,0:T(8,128)(2,1)S(1)}, u32[]{:S(2)}, u32[]{:S(2)}) collective-permute-start(bf16[320,1280]{1,0:T(8,128)(2,1)S(1)} %collective-permute-done.14.refs_7_), channel_id=1, source_target_pairs={{0,7},{1,0},{2,1},{3,2},{4,3},{5,4},{6,5},{7,6},{8,15},{9,8},{10,9... | collective-permute-start | bytes 2457608 | tf_op jit(solution)/shard_map/ppermute | solution.py:281
  115.9 35.1 %collective-permute-start.7 = (bf16[320,1280]{1,0:T(8,128)(2,1)S(1)}, bf16[320,1280]{1,0:T(8,128)(2,1)S(1)}, u32[]{:S(2)}, u32[]{:S(2)}) collective-permute-start(bf16[320,1280]{1,0:T(8,128)(2,1)S(1)} %collective-permute-done.5.refs_3_), channel_id=1, source_target_pairs={{0,1},{1,2},{2,3},{3,4},{4,5},{5,6},{6,7},{7,0},{8,9},{9,10},{10,1... | collective-permute-start | bytes 2457608 | tf_op jit(solution)/shard_map/ppermute | solution.py:281
  117.8 33.2 %collective-permute-start.8 = (bf16[320,1280]{1,0:T(8,128)(2,1)S(1)}, bf16[320,1280]{1,0:T(8,128)(2,1)S(1)}, u32[]{:S(2)}, u32[]{:S(2)}) collective-permute-start(bf16[320,1280]{1,0:T(8,128)(2,1)S(1)} %collective-permute-done.6.refs_4_), channel_id=1, source_target_pairs={{0,7},{1,0},{2,1},{3,2},{4,3},{5,4},{6,5},{7,6},{8,15},{9,8},{10,9... | collective-permute-start | bytes 2457608 | tf_op jit(solution)/shard_map/ppermute | solution.py:281
  133.4 35.1 %collective-permute-start.17 = (bf16[320,1280]{1,0:T(8,128)(2,1)S(1)}, bf16[320,1280]{1,0:T(8,128)(2,1)S(1)}, u32[]{:S(2)}, u32[]{:S(2)}) collective-permute-start(bf16[320,1280]{1,0:T(8,128)(2,1)S(1)} %collective-permute-done.15.refs_8_), channel_id=1, source_target_pairs={{0,1},{1,2},{2,3},{3,4},{4,5},{5,6},{6,7},{7,0},{8,9},{9,10},{10,1... | collective-permute-start | bytes 2457608 | tf_op jit(solution)/shard_map/ppermute | solution.py:281
  135.3 33.2 %collective-permute-start.18 = (bf16[320,1280]{1,0:T(8,128)(2,1)S(1)}, bf16[320,1280]{1,0:T(8,128)(2,1)}, u32[]{:S(2)}, u32[]{:S(2)}) collective-permute-start(bf16[320,1280]{1,0:T(8,128)(2,1)S(1)} %collective-permute-done.16.refs_9_), channel_id=1, source_target_pairs={{0,7},{1,0},{2,1},{3,2},{4,3},{5,4},{6,5},{7,6},{8,15},{9,8},{10,9... | collective-permute-start | bytes 2457608 | tf_op jit(solution)/shard_map/ppermute | solution.py:281
  175.4 16.9 %collective-permute-start.21 = (bf16[1600,2560]{1,0:T(8,128)(2,1)}, bf16[1600,2560]{1,0:T(8,128)(2,1)}, u32[]{:S(2)}, u32[]{:S(2)}) collective-permute-start(bf16[1600,2560]{1,0:T(8,128)(2,1)} %assemble.2.rest_0_), channel_id=1, source_target_pairs={{0,32},{32,0},{64,96},{96,64},{128,160},{160,128},{192,224},{224,1... | collective-permute-start | bytes 24576008 | tf_op jit(solution)/shard_map/ppermute | solution.py:269
  179.5 23.0 %collective-permute-start.9 = (bf16[320,1280]{1,0:T(8,128)(2,1)S(1)}, bf16[320,1280]{1,0:T(8,128)(2,1)S(1)}, u32[]{:S(2)}, u32[]{:S(2)}) collective-permute-start(bf16[320,1280]{1,0:T(8,128)(2,1)S(1)} %collective-permute-done.7.refs_0_), channel_id=1, source_target_pairs={{0,1},{1,2},{2,3},{3,4},{4,5},{5,6},{6,7},{7,0},{8,9},{9,10},{10,1... | collective-permute-start | bytes 2457608 | tf_op jit(solution)/shard_map/ppermute | solution.py:281
  181.4 24.9 %collective-permute-start.19 = (bf16[320,1280]{1,0:T(8,128)(2,1)}, bf16[320,1280]{1,0:T(8,128)(2,1)S(1)}, u32[]{:S(2)}, u32[]{:S(2)}) collective-permute-start(bf16[320,1280]{1,0:T(8,128)(2,1)} %collective-permute-done.18.refs_4_), channel_id=1, source_target_pairs={{0,7},{1,0},{2,1},{3,2},{4,3},{5,4},{6,5},{7,6},{8,15},{9,8},{10,9... | collective-permute-start | bytes 2457608 | tf_op jit(solution)/shard_map/ppermute | solution.py:281
  186.0 12.1 %collective-permute-start.20 = (f32[1,2560]{1,0:T(1,128)S(1)}, f32[1,2560]{1,0:T(1,128)S(1)}, u32[]{:S(2)}, u32[]{:S(2)}) collective-permute-start(f32[1,2560]{1,0:T(1,128)S(1)} %copy-done.19), channel_id=1, source_target_pairs={{0,32},{32,0},{64,96},{96,64},{128,160},{160,128},{192,224},{224,1... | collective-permute-start | bytes 30728 | tf_op jit(solution)/shard_map/ppermute | solution.py:269
  194.2 15.5 %all-to-all-start = ((bf16[32,2,1280]{2,1,0:T(2,128)(2,1)}), bf16[32,2,1280]{2,1,0:T(2,128)(2,1)S(1)}, u32[]{:S(2)}, u32[]{:S(2)}) async-start(bf16[32,2,1280]{2,1,0:T(2,128)(2,1)} %reshape.75), calls=%async_computation | async-start | bytes 327680 | tf_op jit(solution)/shard_map/all_to_all | solution.py:307
  215.1 12.0 %collective-permute-start.22 = (bf16[960,2560]{1,0:T(8,128)(2,1)}, bf16[960,2560]{1,0:T(8,128)(2,1)}, u32[]{:S(2)}, u32[]{:S(2)}) collective-permute-start(bf16[960,2560]{1,0:T(8,128)(2,1)} %assemble.3.rest_1_), channel_id=1, source_target_pairs={{0,32},{32,0},{64,96},{96,64},{128,160},{160,128},{192,224},{224,1... | collective-permute-start | bytes 14745608 | tf_op jit(solution)/shard_map/ppermute | solution.py:269
  236.4 7.5 %collective-permute-start.23 = (bf16[32,2560]{1,0:T(8,128)(2,1)S(1)}, bf16[32,2560]{1,0:T(8,128)(2,1)S(1)}, u32[]{:S(2)}, u32[]{:S(2)}) collective-permute-start(bf16[32,2560]{1,0:T(8,128)(2,1)S(1)} %get-tuple-element.189), channel_id=1, source_target_pairs={{0,64},{32,96},{1,65},{33,97},{2,66},{34,98},{3,67},{35,99},{4,68}... | collective-permute-start | bytes 491528 | tf_op jit(solution)/shard_map/ppermute | solution.py:333
  252.7 12.7 %collective-permute-start.29 = (bf16[32,2560]{1,0:T(8,128)(2,1)S(1)}, bf16[32,2560]{1,0:T(8,128)(2,1)S(1)}, u32[]{:S(2)}, u32[]{:S(2)}) collective-permute-start(bf16[32,2560]{1,0:T(8,128)(2,1)S(1)} %get-tuple-element.204), channel_id=1, source_target_pairs={{192,256},{224,288},{193,257},{225,289},{194,258},{226,290},{195,2... | collective-permute-start | bytes 491528 | tf_op jit(solution)/shard_map/ppermute | solution.py:333
  276.8 6.6 %collective-permute-start.37 = (bf16[32,2560]{1,0:T(8,128)(2,1)S(1)}, bf16[32,2560]{1,0:T(8,128)(2,1)S(1)}, u32[]{:S(2)}, u32[]{:S(2)}) collective-permute-start(bf16[32,2560]{1,0:T(8,128)(2,1)S(1)} %get-tuple-element.225), channel_id=1, source_target_pairs={{448,384},{480,416},{449,385},{481,417},{450,386},{482,418},{451,3... | collective-permute-start | bytes 491528 | tf_op jit(solution)/shard_map/ppermute | solution.py:333
  285.9 6.9 %collective-permute-start.40 = (bf16[32,2560]{1,0:T(8,128)(2,1)S(1)}, bf16[32,2560]{1,0:T(8,128)(2,1)S(1)}, u32[]{:S(2)}, u32[]{:S(2)}) collective-permute-start(bf16[32,2560]{1,0:T(8,128)(2,1)S(1)} %get-tuple-element.234), channel_id=1, source_target_pairs={{384,320},{416,352},{385,321},{417,353},{386,322},{418,354},{387,3... | collective-permute-start | bytes 491528 | tf_op jit(solution)/shard_map/ppermute | solution.py:333
  301.9 5.5 %collective-permute-start.47 = (bf16[32,2560]{1,0:T(8,128)(2,1)S(1)}, bf16[32,2560]{1,0:T(8,128)(2,1)S(1)}, u32[]{:S(2)}, u32[]{:S(2)}) collective-permute-start(bf16[32,2560]{1,0:T(8,128)(2,1)S(1)} %get-tuple-element.261), channel_id=1, source_target_pairs={{128,64},{160,96},{129,65},{161,97},{130,66},{162,98},{131,67},{16... | collective-permute-start | bytes 491528 | tf_op jit(solution)/shard_map/ppermute | solution.py:333
  308.6 92.7 %collective-permute-start.49 = (bf16[32,2560]{1,0:T(8,128)(2,1)S(1)}, bf16[32,2560]{1,0:T(8,128)(2,1)S(1)}, u32[]{:S(2)}, u32[]{:S(2)}) collective-permute-start(bf16[32,2560]{1,0:T(8,128)(2,1)S(1)} %get-tuple-element.268), channel_id=1, source_target_pairs={{64,0},{96,32},{65,1},{97,33},{66,2},{98,34},{67,3},{99,35},{68,4}... | collective-permute-start | bytes 491528 | tf_op jit(solution)/shard_map/ppermute | solution.py:333
  401.4 7.5 %collective-permute-start.50 = (bf16[32,2560]{1,0:T(8,128)(2,1)S(1)}, bf16[32,2560]{1,0:T(8,128)(2,1)S(1)}, u32[]{:S(2)}, u32[]{:S(2)}) collective-permute-start(bf16[32,2560]{1,0:T(8,128)(2,1)S(1)} %get-tuple-element.269), channel_id=1, source_target_pairs={{64,0},{96,32},{65,1},{97,33},{66,2},{98,34},{67,3},{99,35},{68,4}... | collective-permute-start | bytes 491528 | tf_op jit(solution)/shard_map/ppermute | solution.py:333
  415.4 16.7 %collective-permute-start.51 = (bf16[80,2560]{1,0:T(8,128)(2,1)S(1)}, bf16[80,2560]{1,0:T(8,128)(2,1)S(1)}, u32[]{:S(2)}, u32[]{:S(2)}) collective-permute-start(bf16[80,2560]{1,0:T(8,128)(2,1)S(1)} %pack.1), channel_id=1, source_target_pairs={{0,32},{32,0},{64,96},{96,64},{128,160},{160,128},{192,224},{224,1... | collective-permute-start | bytes 1228808 | tf_op jit(solution)/shard_map/ppermute | solution.py:269
  (41 other events, 1224.0 us)

commit v6 on v5

--- a/solution.py
+++ b/solution.py
@@ -282,13 +282,13 @@
 
     def first_block(shard):
         above, below = over(shard, 1, 0), over(shard, -1, 0)
-        return above, jnp.concatenate([shard, above, below, over(above, 1, 0)], 0)
+        return jnp.concatenate([shard, above, below, over(above, 1, 0)], 0)
 
     half = width // 2
     shards = [weight[0, :, :half], weight[0, :, half:]]
-    above, block = first_block(shards[0])
-    shards[1], _ = lax.optimization_barrier((shards[1], above))
-    blocks = [block, first_block(shards[1])[1]]
+    block = first_block(shards[0])
+    shards[1], block = lax.optimization_barrier((shards[1], block))
+    blocks = [block, first_block(shards[1])]
     rings = [[(block, block)] for block in blocks]
     for step in range(3):
         for ring in rings:

time: 442 us -> 437 us (0.989)
  waiting for transfers between devices: 203 us -> 187 us
  starting transfers between devices: 132 us -> 144 us
    ppermute x20, waiting for transfers between devices: 102 us -> 81.8 us  [over(): return lax.ppermute(array, 'dp', pairs)]
    ppermute x20, starting transfers between devices: 79.1 us -> 87.4 us  [over(): return lax.ppermute(array, 'dp', pairs)]
    all_to_all x1, waiting for transfers between devices: 3.41 us -> 8.25 us  [per_device(): pieces = lax.all_to_all(bucket, 'dp', 0, 0, tiled=True).astype(F32)]
  transfers between devices with their start and end apart: 53 -> 53, of which waited for: 16 -> 17; matrix products, arithmetic and copies ran while one was open for 1% -> 1% of each run, Pallas kernels for 15% -> 15%
where the time goes in v6:
time: 437 us; the launch traced here: 429 us
  waiting for transfers between devices  187 us (43%)
  starting transfers between devices  144 us (33%)
  Pallas kernels  90.2 us (21%)
    ppermute x28, waiting for transfers between devices, hop(): lax.ppermute(array, 'section', [(2 * k + c, 2 * to + c) for c in range(2)])  91.8 us
    ppermute x20, starting transfers between devices, over(): return lax.ppermute(array, 'dp', pairs)  87.4 us
    ppermute x20, waiting for transfers between devices, over(): return lax.ppermute(array, 'dp', pairs)  81.8 us
    pallas_call x16, Pallas kernels, backward(): pl.pallas_call(kernel, out_shape=[jax.ShapeDtypeStruct((rows, width), BF1...  35.1 us
    ppermute x4, starting transfers between devices, swap(): return lax.ppermute(array, 'section', siblings)  25.8 us
    pallas_call x14, Pallas kernels, forward(): pl.pallas_call(functools.partial(forward_kernel, k, part), out_shape=[jax...  24.6 us
    ppermute x28, starting transfers between devices, hop(): lax.ppermute(array, 'section', [(2 * k + c, 2 * to + c) for c in range(2)])  24.2 us
    pallas_call x2, Pallas kernels, place(): pl.pallas_call(functools.partial(place_kernel, layouts), out_shape=[pltpu...  11.1 us
  transfers between devices with their start and end apart: 53, of which 17 were waited for; matrix products, arithmetic and copies ran while one was open for 1% of the time, Pallas kernels for 15%

profile of v6, /device:TPU:1, one launch (start us, length us, event | category | flops | bytes accessed | tf_op | source)
XLA Modules:
  0.0 429.1 jit_solution(17298868934740104719)
XLA Ops:
  1.7 5.0 %collective-permute-start = (bf16[80,1280]{1,0:T(8,128)(2,1)S(1)}, bf16[80,1280]{1,0:T(8,128)(2,1)S(1)}, u32[]{:S(2)}, u32[]{:S(2)}) collective-permute-start(bf16[80,1280]{1,0:T(8,128)(2,1)S(1)} %get-tuple-element.283), channel_id=1, source_target_pairs={{0,8},{1,9},{2,10},{3,11},{4,12},{5,13},{6,14},{7,15},{8,16},{9,17... | collective-permute-start | bytes 614408 | tf_op jit(solution)/shard_map/ppermute | solution.py:281
  12.5 7.7 %collective-permute-start.2 = (bf16[80,1280]{1,0:T(8,128)(2,1)S(1)}, bf16[80,1280]{1,0:T(8,128)(2,1)S(1)}, u32[]{:S(2)}, u32[]{:S(2)}) collective-permute-start(bf16[80,1280]{1,0:T(8,128)(2,1)S(1)} %collective-permute-done), channel_id=1, source_target_pairs={{0,8},{1,9},{2,10},{3,11},{4,12},{5,13},{6,14},{7,15},{8,16},{9,17... | collective-permute-start | bytes 614408 | tf_op jit(solution)/shard_map/ppermute | solution.py:281
  22.0 5.9 %collective-permute-done.2 = bf16[80,1280]{1,0:T(8,128)(2,1)S(1)} collective-permute-done((bf16[80,1280]{1,0:T(8,128)(2,1)S(1)}, bf16[80,1280]{1,0:T(8,128)(2,1)S(1)}, u32[]{:S(2)}, u32[]{:S(2)}) %collective-permute-start.2) | collective-permute-done | bytes 204832 | tf_op jit(solution)/shard_map/ppermute | solution.py:281
  28.0 8.4 %collective-permute-start.11 = (bf16[80,1280]{1,0:T(8,128)(2,1)S(1)}, bf16[80,1280]{1,0:T(8,128)(2,1)S(1)}, u32[]{:S(2)}, u32[]{:S(2)}) collective-permute-start(bf16[80,1280]{1,0:T(8,128)(2,1)S(1)} %get-tuple-element.147), channel_id=1, source_target_pairs={{0,24},{1,25},{2,26},{3,27},{4,28},{5,29},{6,30},{7,31},{8,0},{9,1... | collective-permute-start | bytes 614408 | tf_op jit(solution)/shard_map/ppermute | solution.py:281
  38.3 8.1 %collective-permute-start.4 = (bf16[320,1280]{1,0:T(8,128)(2,1)S(1)}, bf16[320,1280]{1,0:T(8,128)(2,1)S(1)}, u32[]{:S(2)}, u32[]{:S(2)}) collective-permute-start(bf16[320,1280]{1,0:T(8,128)(2,1)S(1)} %pad_maximum_fusion.refs_0_), channel_id=1, source_target_pairs={{0,7},{1,0},{2,1},{3,2},{4,3},{5,4},{6,5},{7,6},{8,15},{9,8},{10,9... | collective-permute-start | bytes 2457608 | tf_op jit(solution)/shard_map/ppermute | solution.py:281
  48.4 6.2 %collective-permute-start.12 = (bf16[80,1280]{1,0:T(8,128)(2,1)S(1)}, bf16[80,1280]{1,0:T(8,128)(2,1)S(1)}, u32[]{:S(2)}, u32[]{:S(2)}) collective-permute-start(bf16[80,1280]{1,0:T(8,128)(2,1)S(1)} %collective-permute-done.10), channel_id=1, source_target_pairs={{0,8},{1,9},{2,10},{3,11},{4,12},{5,13},{6,14},{7,15},{8,16},{9,17... | collective-permute-start | bytes 614408 | tf_op jit(solution)/shard_map/ppermute | solution.py:281
  54.6 4.8 %collective-permute-done.12 = bf16[80,1280]{1,0:T(8,128)(2,1)S(1)} collective-permute-done((bf16[80,1280]{1,0:T(8,128)(2,1)S(1)}, bf16[80,1280]{1,0:T(8,128)(2,1)S(1)}, u32[]{:S(2)}, u32[]{:S(2)}) %collective-permute-start.12) | collective-permute-done | bytes 204832 | tf_op jit(solution)/shard_map/ppermute | solution.py:281
  59.5 10.2 %collective-permute-start.14 = (bf16[320,1280]{1,0:T(8,128)(2,1)S(1)}, bf16[320,1280]{1,0:T(8,128)(2,1)S(1)}, u32[]{:S(2)}, u32[]{:S(2)}) collective-permute-start(bf16[320,1280]{1,0:T(8,128)(2,1)S(1)} %constant_dynamic-update-slice_fusion.refs_5_), channel_id=1, source_target_pairs={{0,7},{1,0},{2,1},{3,2},{4,3},{5,4},{6,5},{7,6},{8,15},{9,8},{10,9... | collective-permute-start | bytes 2457608 | tf_op jit(solution)/shard_map/ppermute | solution.py:281
  73.6 4.6 %collective-permute-start.6 = (bf16[320,1280]{1,0:T(8,128)(2,1)S(1)}, bf16[320,1280]{1,0:T(8,128)(2,1)S(1)}, u32[]{:S(2)}, u32[]{:S(2)}) collective-permute-start(bf16[320,1280]{1,0:T(8,128)(2,1)S(1)} %collective-permute-done.4.refs_2_), channel_id=1, source_target_pairs={{0,7},{1,0},{2,1},{3,2},{4,3},{5,4},{6,5},{7,6},{8,15},{9,8},{10,9... | collective-permute-start | bytes 2457608 | tf_op jit(solution)/shard_map/ppermute | solution.py:281
  78.2 8.1 %collective-permute-done.14.refs_7_ = bf16[320,1280]{1,0:T(8,128)(2,1)S(1)} collective-permute-done((bf16[320,1280]{1,0:T(8,128)(2,1)S(1)}, bf16[320,1280]{1,0:T(8,128)(2,1)S(1)}, u32[]{:S(2)}, u32[]{:S(2)}) %collective-permute-start.14) | collective-permute-done | bytes 819232 | tf_op jit(solution)/shard_map/ppermute | solution.py:281
  86.3 5.0 %collective-permute-done.13.refs_6_ = bf16[320,1280]{1,0:T(8,128)(2,1)S(1)} collective-permute-done((bf16[320,1280]{1,0:T(8,128)(2,1)S(1)}, bf16[320,1280]{1,0:T(8,128)(2,1)S(1)}, u32[]{:S(2)}, u32[]{:S(2)}) %collective-permute-start.13) | collective-permute-done | bytes 819232 | tf_op jit(solution)/shard_map/ppermute | solution.py:281
  93.2 4.6 %collective-permute-start.16 = (bf16[320,1280]{1,0:T(8,128)(2,1)S(1)}, bf16[320,1280]{1,0:T(8,128)(2,1)S(1)}, u32[]{:S(2)}, u32[]{:S(2)}) collective-permute-start(bf16[320,1280]{1,0:T(8,128)(2,1)S(1)} %collective-permute-done.14.refs_7_), channel_id=1, source_target_pairs={{0,7},{1,0},{2,1},{3,2},{4,3},{5,4},{6,5},{7,6},{8,15},{9,8},{10,9... | collective-permute-start | bytes 2457608 | tf_op jit(solution)/shard_map/ppermute | solution.py:281
  97.8 11.1 %collective-permute-done.5.refs_3_ = bf16[320,1280]{1,0:T(8,128)(2,1)S(1)} collective-permute-done((bf16[320,1280]{1,0:T(8,128)(2,1)S(1)}, bf16[320,1280]{1,0:T(8,128)(2,1)S(1)}, u32[]{:S(2)}, u32[]{:S(2)}) %collective-permute-start.5) | collective-permute-done | bytes 819232 | tf_op jit(solution)/shard_map/ppermute | solution.py:281
  110.8 4.6 %collective-permute-start.8 = (bf16[320,1280]{1,0:T(8,128)(2,1)S(1)}, bf16[320,1280]{1,0:T(8,128)(2,1)S(1)}, u32[]{:S(2)}, u32[]{:S(2)}) collective-permute-start(bf16[320,1280]{1,0:T(8,128)(2,1)S(1)} %collective-permute-done.6.refs_4_), channel_id=1, source_target_pairs={{0,7},{1,0},{2,1},{3,2},{4,3},{5,4},{6,5},{7,6},{8,15},{9,8},{10,9... | collective-permute-start | bytes 2457608 | tf_op jit(solution)/shard_map/ppermute | solution.py:281
  115.4 11.0 %collective-permute-done.15.refs_8_ = bf16[320,1280]{1,0:T(8,128)(2,1)S(1)} collective-permute-done((bf16[320,1280]{1,0:T(8,128)(2,1)S(1)}, bf16[320,1280]{1,0:T(8,128)(2,1)S(1)}, u32[]{:S(2)}, u32[]{:S(2)}) %collective-permute-start.15) | collective-permute-done | bytes 819232 | tf_op jit(solution)/shard_map/ppermute | solution.py:281
  128.4 4.6 %collective-permute-start.18 = (bf16[320,1280]{1,0:T(8,128)(2,1)S(1)}, bf16[320,1280]{1,0:T(8,128)(2,1)}, u32[]{:S(2)}, u32[]{:S(2)}) collective-permute-start(bf16[320,1280]{1,0:T(8,128)(2,1)S(1)} %collective-permute-done.16.refs_9_), channel_id=1, source_target_pairs={{0,7},{1,0},{2,1},{3,2},{4,3},{5,4},{6,5},{7,6},{8,15},{9,8},{10,9... | collective-permute-start | bytes 2457608 | tf_op jit(solution)/shard_map/ppermute | solution.py:281
  132.9 11.0 %collective-permute-done.7.refs_0_ = bf16[320,1280]{1,0:T(8,128)(2,1)S(1)} collective-permute-done((bf16[320,1280]{1,0:T(8,128)(2,1)S(1)}, bf16[320,1280]{1,0:T(8,128)(2,1)S(1)}, u32[]{:S(2)}, u32[]{:S(2)}) %collective-permute-start.7) | collective-permute-done | bytes 819232 | tf_op jit(solution)/shard_map/ppermute | solution.py:281
  144.0 17.5 %collective-permute-done.17.refs_3_ = bf16[320,1280]{1,0:T(8,128)(2,1)S(1)} collective-permute-done((bf16[320,1280]{1,0:T(8,128)(2,1)S(1)}, bf16[320,1280]{1,0:T(8,128)(2,1)S(1)}, u32[]{:S(2)}, u32[]{:S(2)}) %collective-permute-start.17) | collective-permute-done | bytes 819232 | tf_op jit(solution)/shard_map/ppermute | solution.py:281
  161.6 6.7 %assemble.2.rest_0_ = bf16[1600,2560]{1,0:T(8,128)(2,1)} custom-call(bf16[320,1280]{1,0:T(8,128)(2,1)} %copy-done, bf16[320,1280]{1,0:T(8,128)(2,1)} %copy-done.8, bf16[320,1280]{1,0:T(8,128)(2,1)} %copy-done.7, bf16[320,1280]{1,0:T(8,128)(2,1)} %copy-done.11, bf16[320,1280]{1,0:T(8,128)(2,1)} %copy-done.12, bf16[320,1280]{1,0:T(8,128)(2,1)} %copy-done.1, ...), custom_call_target="tpu_custom_call" | custom-call | tf_op jit(solution)/shard_map/assemble/pallas_call | solution.py:51
  187.2 6.5 %all-to-all-start = ((bf16[32,2,1280]{2,1,0:T(2,128)(2,1)}), bf16[32,2,1280]{2,1,0:T(2,128)(2,1)S(1)}, u32[]{:S(2)}, u32[]{:S(2)}) async-start(bf16[32,2,1280]{2,1,0:T(2,128)(2,1)} %reshape.75), calls=%async_computation | async-start | bytes 327680 | tf_op jit(solution)/shard_map/all_to_all | solution.py:307
  197.0 8.2 %all-to-all-done = bf16[32,2,1280]{2,1,0:T(2,128)(2,1)S(1)} async-done(((bf16[32,2,1280]{2,1,0:T(2,128)(2,1)}), bf16[32,2,1280]{2,1,0:T(2,128)(2,1)S(1)}, u32[]{:S(2)}, u32[]{:S(2)}) %all-to-all-start) | async-done | bytes 163872 | tf_op jit(solution)/shard_map/all_to_all | solution.py:307
  214.7 8.1 %place_weight.2 = (bf16[2,2560,2560]{2,1,0:T(8,128)(2,1)S(1)}, bf16[2,2560,2560]{2,1,0:T(8,128)(2,1)S(1)}) custom-call(s32[4]{0:T(128)S(1)} %pad_add_fusion.state, bf16[1600,2560]{1,0:T(8,128)(2,1)} %assemble.2.rest_0_, bf16[960,2560]{1,0:T(8,128)(2,1)} %assemble.3.rest_1_, bf16[1600,2560]{1,0:T(8,128)(2,1)} %collective-permute-done.21.rest_2_), custom_call_target="tpu_custom_call" | custom-call | tf_op jit(solution)/shard_map/place_weight/pallas_call | solution.py:84
  226.4 5.7 %forward.14 = (bf16[32,2560]{1,0:T(8,128)(2,1)S(1)}, bf16[2,2,32,2560]{3,2,1,0:T(8,128)(2,1)S(1)}) custom-call(s32[4]{0:T(128)S(1)} %pad_add_fusion.state, bf16[32,2560]{1,0:T(8,128)(2,1)S(1)} %get-tuple-element.188.arrived, f32[2,2560]{1,0:T(2,128)S(1)} %maximum_select_fusion.1.gains, bf16[2,2560,2560]{2,1,0:T(8,128)(2,1)S(1)} %get-tuple-element.186.weights.rest_0_, ...), custom_call_target="tpu_custom_call" | custom-call | tf_op jit(solution)/shard_map/forward/pallas_call | solution.py:195
  233.3 5.8 %forward.15 = (bf16[32,2560]{1,0:T(8,128)(2,1)S(1)}, bf16[2,2,32,2560]{3,2,1,0:T(8,128)(2,1)S(1)}) custom-call(s32[4]{0:T(128)S(1)} %pad_add_fusion.state, bf16[32,2560]{1,0:T(8,128)(2,1)S(1)} %get-tuple-element.179.arrived, f32[2,2560]{1,0:T(2,128)S(1)} %maximum_select_fusion.1.gains, ...), custom_call_target="tpu_custom_call", output_to_operand_aliasing={{1}: (5, {})} | custom-call | tf_op jit(solution)/shard_map/forward/pallas_call | solution.py:195
  253.4 7.8 %transpose_weight.3.rest_0_.turned = bf16[2,2560,2560]{2,1,0:T(8,128)(2,1)S(1)} custom-call(s32[4]{0:T(128)S(1)} %pad_add_fusion.state, bf16[2,2560,2560]{2,1,0:T(8,128)(2,1)S(1)} %get-tuple-element.186.weights.rest_0_, bf16[2,2560,2560]{2,1,0:T(8,128)(2,1)S(1)} %transpose_weight.2.rest_0_._), custom_call_target="tpu_custom_call", output_to_operand_aliasing={{}: (2, {})} | custom-call | tf_op jit(solution)/shard_map/transpose_weight/pallas_call | solution.py:135
  273.2 6.1 %turn.3 = (bf16[32,2560]{1,0:T(8,128)(2,1)S(1)}, bf16[2,2,32,2560]{3,2,1,0:T(8,128)(2,1)S(1)}, f32[2,1,2560]{2,1,0:T(1,128)S(1)}) custom-call(s32[4]{0:T(128)S(1)} %pad_add_fusion.state, bf16[32,2560]{1,0:T(8,128)(2,1)S(1)} %get-tuple-element.178.fresh, ...), custom_call_target="tpu_custom_call", output_to_operand_aliasing={{1}: (6, {}), {2}: (7, {})} | custom-call | tf_op jit(solution)/shard_map/turn/pallas_call | solution.py:243
  282.4 5.3 %backward.16 = (bf16[32,2560]{1,0:T(8,128)(2,1)S(1)}, bf16[2,2,32,2560]{3,2,1,0:T(8,128)(2,1)S(1)}, f32[2,1,2560]{2,1,0:T(1,128)S(1)}) custom-call(s32[4]{0:T(128)S(1)} %pad_add_fusion.state, bf16[32,2560]{1,0:T(8,128)(2,1)S(1)} %collective-permute-done.39.received, ...), custom_call_target="tpu_custom_call", output_to_operand_aliasing={{1}: (6, {}), {2}: (7, {})} | custom-call | tf_op jit(solution)/shard_map/backward/pallas_call | solution.py:243
  298.3 5.0 %backward.23 = (bf16[32,2560]{1,0:T(8,128)(2,1)S(1)}, bf16[2,2,32,2560]{3,2,1,0:T(8,128)(2,1)S(1)}, f32[2,1,2560]{2,1,0:T(1,128)S(1)}) custom-call(s32[4]{0:T(128)S(1)} %pad_add_fusion.state, bf16[32,2560]{1,0:T(8,128)(2,1)S(1)} %collective-permute-done.46.received, ...), custom_call_target="tpu_custom_call", output_to_operand_aliasing={{1}: (6, {}), {2}: (7, {})} | custom-call | tf_op jit(solution)/shard_map/backward/pallas_call | solution.py:243
  306.4 90.2 %collective-permute-done.49.received = bf16[32,2560]{1,0:T(8,128)(2,1)S(1)} collective-permute-done((bf16[32,2560]{1,0:T(8,128)(2,1)S(1)}, bf16[32,2560]{1,0:T(8,128)(2,1)S(1)}, u32[]{:S(2)}, u32[]{:S(2)}) %collective-permute-start.49) | collective-permute-done | bytes 163872 | tf_op jit(solution)/shard_map/ppermute | solution.py:333
  397.9 6.2 %backward.26 = (bf16[32,2560]{1,0:T(8,128)(2,1)}, bf16[2,2,32,2560]{3,2,1,0:T(8,128)(2,1)S(1)}, f32[2,1,2560]{2,1,0:T(1,128)S(1)}) custom-call(s32[4]{0:T(128)S(1)} %pad_add_fusion.state, bf16[32,2560]{1,0:T(8,128)(2,1)S(1)} %collective-permute-done.49.received, ...), custom_call_target="tpu_custom_call", output_to_operand_aliasing={{1}: (6, {}), {2}: (7, {})} | custom-call | tf_op jit(solution)/shard_map/backward/pallas_call | solution.py:243
  404.1 6.4 %backward.27 = (bf16[32,2560]{1,0:T(8,128)(2,1)}, bf16[2,2,32,2560]{3,2,1,0:T(8,128)(2,1)S(1)}, f32[2,1,2560]{2,1,0:T(1,128)S(1)}) custom-call(s32[4]{0:T(128)S(1)} %pad_add_fusion.state, bf16[32,2560]{1,0:T(8,128)(2,1)S(1)} %collective-permute-done.50.received, ...), custom_call_target="tpu_custom_call", output_to_operand_aliasing={{1}: (6, {}), {2}: (7, {})} | custom-call | tf_op jit(solution)/shard_map/backward/pallas_call | solution.py:243
  410.6 15.4 %collective-permute-start.51 = (bf16[80,2560]{1,0:T(8,128)(2,1)S(1)}, bf16[80,2560]{1,0:T(8,128)(2,1)S(1)}, u32[]{:S(2)}, u32[]{:S(2)}) collective-permute-start(bf16[80,2560]{1,0:T(8,128)(2,1)S(1)} %pack.1), channel_id=1, source_target_pairs={{0,32},{32,0},{64,96},{96,64},{128,160},{160,128},{192,224},{224,1... | collective-permute-start | bytes 1228808 | tf_op jit(solution)/shard_map/ppermute | solution.py:269
  (172 shorter events, 105.0 us)
Async XLA Ops:
  1.7 10.8 %collective-permute-start = (bf16[80,1280]{1,0:T(8,128)(2,1)S(1)}, bf16[80,1280]{1,0:T(8,128)(2,1)S(1)}, u32[]{:S(2)}, u32[]{:S(2)}) collective-permute-start(bf16[80,1280]{1,0:T(8,128)(2,1)S(1)} %get-tuple-element.283), channel_id=1, source_target_pairs={{0,8},{1,9},{2,10},{3,11},{4,12},{5,13},{6,14},{7,15},{8,16},{9,17... | collective-permute-start | bytes 614408 | tf_op jit(solution)/shard_map/ppermute | solution.py:281
  6.7 15.2 %collective-permute-start.1 = (bf16[80,1280]{1,0:T(8,128)(2,1)S(1)}, bf16[80,1280]{1,0:T(8,128)(2,1)S(1)}, u32[]{:S(2)}, u32[]{:S(2)}) collective-permute-start(bf16[80,1280]{1,0:T(8,128)(2,1)S(1)} %get-tuple-element.283), channel_id=1, source_target_pairs={{0,24},{1,25},{2,26},{3,27},{4,28},{5,29},{6,30},{7,31},{8,0},{9,1... | collective-permute-start | bytes 614408 | tf_op jit(solution)/shard_map/ppermute | solution.py:281
  12.5 15.4 %collective-permute-start.2 = (bf16[80,1280]{1,0:T(8,128)(2,1)S(1)}, bf16[80,1280]{1,0:T(8,128)(2,1)S(1)}, u32[]{:S(2)}, u32[]{:S(2)}) collective-permute-start(bf16[80,1280]{1,0:T(8,128)(2,1)S(1)} %collective-permute-done), channel_id=1, source_target_pairs={{0,8},{1,9},{2,10},{3,11},{4,12},{5,13},{6,14},{7,15},{8,16},{9,17... | collective-permute-start | bytes 614408 | tf_op jit(solution)/shard_map/ppermute | solution.py:281
  28.0 26.6 %collective-permute-start.11 = (bf16[80,1280]{1,0:T(8,128)(2,1)S(1)}, bf16[80,1280]{1,0:T(8,128)(2,1)S(1)}, u32[]{:S(2)}, u32[]{:S(2)}) collective-permute-start(bf16[80,1280]{1,0:T(8,128)(2,1)S(1)} %get-tuple-element.147), channel_id=1, source_target_pairs={{0,24},{1,25},{2,26},{3,27},{4,28},{5,29},{6,30},{7,31},{8,0},{9,1... | collective-permute-start | bytes 614408 | tf_op jit(solution)/shard_map/ppermute | solution.py:281
  36.4 12.0 %collective-permute-start.10 = (bf16[80,1280]{1,0:T(8,128)(2,1)S(1)}, bf16[80,1280]{1,0:T(8,128)(2,1)S(1)}, u32[]{:S(2)}, u32[]{:S(2)}) collective-permute-start(bf16[80,1280]{1,0:T(8,128)(2,1)S(1)} %get-tuple-element.147), channel_id=1, source_target_pairs={{0,8},{1,9},{2,10},{3,11},{4,12},{5,13},{6,14},{7,15},{8,16},{9,17... | collective-permute-start | bytes 614408 | tf_op jit(solution)/shard_map/ppermute | solution.py:281
  38.3 33.3 %collective-permute-start.4 = (bf16[320,1280]{1,0:T(8,128)(2,1)S(1)}, bf16[320,1280]{1,0:T(8,128)(2,1)S(1)}, u32[]{:S(2)}, u32[]{:S(2)}) collective-permute-start(bf16[320,1280]{1,0:T(8,128)(2,1)S(1)} %pad_maximum_fusion.refs_0_), channel_id=1, source_target_pairs={{0,7},{1,0},{2,1},{3,2},{4,3},{5,4},{6,5},{7,6},{8,15},{9,8},{10,9... | collective-permute-start | bytes 2457608 | tf_op jit(solution)/shard_map/ppermute | solution.py:281
  46.4 25.2 %collective-permute-start.3 = (bf16[320,1280]{1,0:T(8,128)(2,1)S(1)}, bf16[320,1280]{1,0:T(8,128)(2,1)S(1)}, u32[]{:S(2)}, u32[]{:S(2)}) collective-permute-start(bf16[320,1280]{1,0:T(8,128)(2,1)S(1)} %pad_maximum_fusion.refs_0_), channel_id=1, source_target_pairs={{0,1},{1,2},{2,3},{3,4},{4,5},{5,6},{6,7},{7,0},{8,9},{9,10},{10,1... | collective-permute-start | bytes 2457608 | tf_op jit(solution)/shard_map/ppermute | solution.py:281
  48.4 11.1 %collective-permute-start.12 = (bf16[80,1280]{1,0:T(8,128)(2,1)S(1)}, bf16[80,1280]{1,0:T(8,128)(2,1)S(1)}, u32[]{:S(2)}, u32[]{:S(2)}) collective-permute-start(bf16[80,1280]{1,0:T(8,128)(2,1)S(1)} %collective-permute-done.10), channel_id=1, source_target_pairs={{0,8},{1,9},{2,10},{3,11},{4,12},{5,13},{6,14},{7,15},{8,16},{9,17... | collective-permute-start | bytes 614408 | tf_op jit(solution)/shard_map/ppermute | solution.py:281
  59.5 26.8 %collective-permute-start.14 = (bf16[320,1280]{1,0:T(8,128)(2,1)S(1)}, bf16[320,1280]{1,0:T(8,128)(2,1)S(1)}, u32[]{:S(2)}, u32[]{:S(2)}) collective-permute-start(bf16[320,1280]{1,0:T(8,128)(2,1)S(1)} %constant_dynamic-update-slice_fusion.refs_5_), channel_id=1, source_target_pairs={{0,7},{1,0},{2,1},{3,2},{4,3},{5,4},{6,5},{7,6},{8,15},{9,8},{10,9... | collective-permute-start | bytes 2457608 | tf_op jit(solution)/shard_map/ppermute | solution.py:281
  69.7 21.6 %collective-permute-start.13 = (bf16[320,1280]{1,0:T(8,128)(2,1)S(1)}, bf16[320,1280]{1,0:T(8,128)(2,1)S(1)}, u32[]{:S(2)}, u32[]{:S(2)}) collective-permute-start(bf16[320,1280]{1,0:T(8,128)(2,1)S(1)} %constant_dynamic-update-slice_fusion.refs_5_), channel_id=1, source_target_pairs={{0,1},{1,2},{2,3},{3,4},{4,5},{5,6},{6,7},{7,0},{8,9},{9,10},{10,1... | collective-permute-start | bytes 2457608 | tf_op jit(solution)/shard_map/ppermute | solution.py:281
  71.7 37.2 %collective-permute-start.5 = (bf16[320,1280]{1,0:T(8,128)(2,1)S(1)}, bf16[320,1280]{1,0:T(8,128)(2,1)S(1)}, u32[]{:S(2)}, u32[]{:S(2)}) collective-permute-start(bf16[320,1280]{1,0:T(8,128)(2,1)S(1)} %collective-permute-done.3.refs_1_), channel_id=1, source_target_pairs={{0,1},{1,2},{2,3},{3,4},{4,5},{5,6},{6,7},{7,0},{8,9},{9,10},{10,1... | collective-permute-start | bytes 2457608 | tf_op jit(solution)/shard_map/ppermute | solution.py:281
  73.6 35.3 %collective-permute-start.6 = (bf16[320,1280]{1,0:T(8,128)(2,1)S(1)}, bf16[320,1280]{1,0:T(8,128)(2,1)S(1)}, u32[]{:S(2)}, u32[]{:S(2)}) collective-permute-start(bf16[320,1280]{1,0:T(8,128)(2,1)S(1)} %collective-permute-done.4.refs_2_), channel_id=1, source_target_pairs={{0,7},{1,0},{2,1},{3,2},{4,3},{5,4},{6,5},{7,6},{8,15},{9,8},{10,9... | collective-permute-start | bytes 2457608 | tf_op jit(solution)/shard_map/ppermute | solution.py:281
  91.3 35.1 %collective-permute-start.15 = (bf16[320,1280]{1,0:T(8,128)(2,1)S(1)}, bf16[320,1280]{1,0:T(8,128)(2,1)S(1)}, u32[]{:S(2)}, u32[]{:S(2)}) collective-permute-start(bf16[320,1280]{1,0:T(8,128)(2,1)S(1)} %collective-permute-done.13.refs_6_), channel_id=1, source_target_pairs={{0,1},{1,2},{2,3},{3,4},{4,5},{5,6},{6,7},{7,0},{8,9},{9,10},{10,1... | collective-permute-start | bytes 2457608 | tf_op jit(solution)/shard_map/ppermute | solution.py:281
  93.2 33.2 %collective-permute-start.16 = (bf16[320,1280]{1,0:T(8,128)(2,1)S(1)}, bf16[320,1280]{1,0:T(8,128)(2,1)S(1)}, u32[]{:S(2)}, u32[]{:S(2)}) collective-permute-start(bf16[320,1280]{1,0:T(8,128)(2,1)S(1)} %collective-permute-done.14.refs_7_), channel_id=1, source_target_pairs={{0,7},{1,0},{2,1},{3,2},{4,3},{5,4},{6,5},{7,6},{8,15},{9,8},{10,9... | collective-permute-start | bytes 2457608 | tf_op jit(solution)/shard_map/ppermute | solution.py:281
  108.9 35.1 %collective-permute-start.7 = (bf16[320,1280]{1,0:T(8,128)(2,1)S(1)}, bf16[320,1280]{1,0:T(8,128)(2,1)S(1)}, u32[]{:S(2)}, u32[]{:S(2)}) collective-permute-start(bf16[320,1280]{1,0:T(8,128)(2,1)S(1)} %collective-permute-done.5.refs_3_), channel_id=1, source_target_pairs={{0,1},{1,2},{2,3},{3,4},{4,5},{5,6},{6,7},{7,0},{8,9},{9,10},{10,1... | collective-permute-start | bytes 2457608 | tf_op jit(solution)/shard_map/ppermute | solution.py:281
  110.8 33.2 %collective-permute-start.8 = (bf16[320,1280]{1,0:T(8,128)(2,1)S(1)}, bf16[320,1280]{1,0:T(8,128)(2,1)S(1)}, u32[]{:S(2)}, u32[]{:S(2)}) collective-permute-start(bf16[320,1280]{1,0:T(8,128)(2,1)S(1)} %collective-permute-done.6.refs_4_), channel_id=1, source_target_pairs={{0,7},{1,0},{2,1},{3,2},{4,3},{5,4},{6,5},{7,6},{8,15},{9,8},{10,9... | collective-permute-start | bytes 2457608 | tf_op jit(solution)/shard_map/ppermute | solution.py:281
  126.4 35.1 %collective-permute-start.17 = (bf16[320,1280]{1,0:T(8,128)(2,1)S(1)}, bf16[320,1280]{1,0:T(8,128)(2,1)S(1)}, u32[]{:S(2)}, u32[]{:S(2)}) collective-permute-start(bf16[320,1280]{1,0:T(8,128)(2,1)S(1)} %collective-permute-done.15.refs_8_), channel_id=1, source_target_pairs={{0,1},{1,2},{2,3},{3,4},{4,5},{5,6},{6,7},{7,0},{8,9},{9,10},{10,1... | collective-permute-start | bytes 2457608 | tf_op jit(solution)/shard_map/ppermute | solution.py:281
  128.4 33.2 %collective-permute-start.18 = (bf16[320,1280]{1,0:T(8,128)(2,1)S(1)}, bf16[320,1280]{1,0:T(8,128)(2,1)}, u32[]{:S(2)}, u32[]{:S(2)}) collective-permute-start(bf16[320,1280]{1,0:T(8,128)(2,1)S(1)} %collective-permute-done.16.refs_9_), channel_id=1, source_target_pairs={{0,7},{1,0},{2,1},{3,2},{4,3},{5,4},{6,5},{7,6},{8,15},{9,8},{10,9... | collective-permute-start | bytes 2457608 | tf_op jit(solution)/shard_map/ppermute | solution.py:281
  168.4 16.9 %collective-permute-start.21 = (bf16[1600,2560]{1,0:T(8,128)(2,1)}, bf16[1600,2560]{1,0:T(8,128)(2,1)}, u32[]{:S(2)}, u32[]{:S(2)}) collective-permute-start(bf16[1600,2560]{1,0:T(8,128)(2,1)} %assemble.2.rest_0_), channel_id=1, source_target_pairs={{0,32},{32,0},{64,96},{96,64},{128,160},{160,128},{192,224},{224,1... | collective-permute-start | bytes 24576008 | tf_op jit(solution)/shard_map/ppermute | solution.py:269
  172.5 23.0 %collective-permute-start.9 = (bf16[320,1280]{1,0:T(8,128)(2,1)S(1)}, bf16[320,1280]{1,0:T(8,128)(2,1)S(1)}, u32[]{:S(2)}, u32[]{:S(2)}) collective-permute-start(bf16[320,1280]{1,0:T(8,128)(2,1)S(1)} %collective-permute-done.7.refs_0_), channel_id=1, source_target_pairs={{0,1},{1,2},{2,3},{3,4},{4,5},{5,6},{6,7},{7,0},{8,9},{9,10},{10,1... | collective-permute-start | bytes 2457608 | tf_op jit(solution)/shard_map/ppermute | solution.py:281
  174.4 22.6 %collective-permute-start.19 = (bf16[320,1280]{1,0:T(8,128)(2,1)}, bf16[320,1280]{1,0:T(8,128)(2,1)S(1)}, u32[]{:S(2)}, u32[]{:S(2)}) collective-permute-start(bf16[320,1280]{1,0:T(8,128)(2,1)} %collective-permute-done.18.refs_4_), channel_id=1, source_target_pairs={{0,7},{1,0},{2,1},{3,2},{4,3},{5,4},{6,5},{7,6},{8,15},{9,8},{10,9... | collective-permute-start | bytes 2457608 | tf_op jit(solution)/shard_map/ppermute | solution.py:281
  179.0 14.7 %collective-permute-start.20 = (f32[1,2560]{1,0:T(1,128)S(1)}, f32[1,2560]{1,0:T(1,128)S(1)}, u32[]{:S(2)}, u32[]{:S(2)}) collective-permute-start(f32[1,2560]{1,0:T(1,128)S(1)} %copy-done.19), channel_id=1, source_target_pairs={{0,32},{32,0},{64,96},{96,64},{128,160},{160,128},{192,224},{224,1... | collective-permute-start | bytes 30728 | tf_op jit(solution)/shard_map/ppermute | solution.py:269
  187.2 18.1 %all-to-all-start = ((bf16[32,2,1280]{2,1,0:T(2,128)(2,1)}), bf16[32,2,1280]{2,1,0:T(2,128)(2,1)S(1)}, u32[]{:S(2)}, u32[]{:S(2)}) async-start(bf16[32,2,1280]{2,1,0:T(2,128)(2,1)} %reshape.75), calls=%async_computation | async-start | bytes 327680 | tf_op jit(solution)/shard_map/all_to_all | solution.py:307
  210.6 12.1 %collective-permute-start.22 = (bf16[960,2560]{1,0:T(8,128)(2,1)}, bf16[960,2560]{1,0:T(8,128)(2,1)}, u32[]{:S(2)}, u32[]{:S(2)}) collective-permute-start(bf16[960,2560]{1,0:T(8,128)(2,1)} %assemble.3.rest_1_), channel_id=1, source_target_pairs={{0,32},{32,0},{64,96},{96,64},{128,160},{160,128},{192,224},{224,1... | collective-permute-start | bytes 14745608 | tf_op jit(solution)/shard_map/ppermute | solution.py:269
  232.0 7.2 %collective-permute-start.23 = (bf16[32,2560]{1,0:T(8,128)(2,1)S(1)}, bf16[32,2560]{1,0:T(8,128)(2,1)S(1)}, u32[]{:S(2)}, u32[]{:S(2)}) collective-permute-start(bf16[32,2560]{1,0:T(8,128)(2,1)S(1)} %get-tuple-element.191), channel_id=1, source_target_pairs={{0,64},{32,96},{1,65},{33,97},{2,66},{34,98},{3,67},{35,99},{4,68}... | collective-permute-start | bytes 491528 | tf_op jit(solution)/shard_map/ppermute | solution.py:333
  248.4 12.9 %collective-permute-start.29 = (bf16[32,2560]{1,0:T(8,128)(2,1)S(1)}, bf16[32,2560]{1,0:T(8,128)(2,1)S(1)}, u32[]{:S(2)}, u32[]{:S(2)}) collective-permute-start(bf16[32,2560]{1,0:T(8,128)(2,1)S(1)} %get-tuple-element.206), channel_id=1, source_target_pairs={{192,256},{224,288},{193,257},{225,289},{194,258},{226,290},{195,2... | collective-permute-start | bytes 491528 | tf_op jit(solution)/shard_map/ppermute | solution.py:333
  272.5 6.8 %collective-permute-start.37 = (bf16[32,2560]{1,0:T(8,128)(2,1)S(1)}, bf16[32,2560]{1,0:T(8,128)(2,1)S(1)}, u32[]{:S(2)}, u32[]{:S(2)}) collective-permute-start(bf16[32,2560]{1,0:T(8,128)(2,1)S(1)} %get-tuple-element.227), channel_id=1, source_target_pairs={{448,384},{480,416},{449,385},{481,417},{450,386},{482,418},{451,3... | collective-permute-start | bytes 491528 | tf_op jit(solution)/shard_map/ppermute | solution.py:333
  281.8 6.7 %collective-permute-start.40 = (bf16[32,2560]{1,0:T(8,128)(2,1)S(1)}, bf16[32,2560]{1,0:T(8,128)(2,1)S(1)}, u32[]{:S(2)}, u32[]{:S(2)}) collective-permute-start(bf16[32,2560]{1,0:T(8,128)(2,1)S(1)} %get-tuple-element.236), channel_id=1, source_target_pairs={{384,320},{416,352},{385,321},{417,353},{386,322},{418,354},{387,3... | collective-permute-start | bytes 491528 | tf_op jit(solution)/shard_map/ppermute | solution.py:333
  297.6 5.7 %collective-permute-start.47 = (bf16[32,2560]{1,0:T(8,128)(2,1)S(1)}, bf16[32,2560]{1,0:T(8,128)(2,1)S(1)}, u32[]{:S(2)}, u32[]{:S(2)}) collective-permute-start(bf16[32,2560]{1,0:T(8,128)(2,1)S(1)} %get-tuple-element.263), channel_id=1, source_target_pairs={{128,64},{160,96},{129,65},{161,97},{130,66},{162,98},{131,67},{16... | collective-permute-start | bytes 491528 | tf_op jit(solution)/shard_map/ppermute | solution.py:333
  304.5 92.1 %collective-permute-start.49 = (bf16[32,2560]{1,0:T(8,128)(2,1)S(1)}, bf16[32,2560]{1,0:T(8,128)(2,1)S(1)}, u32[]{:S(2)}, u32[]{:S(2)}) collective-permute-start(bf16[32,2560]{1,0:T(8,128)(2,1)S(1)} %get-tuple-element.270), channel_id=1, source_target_pairs={{64,0},{96,32},{65,1},{97,33},{66,2},{98,34},{67,3},{99,35},{68,4}... | collective-permute-start | bytes 491528 | tf_op jit(solution)/shard_map/ppermute | solution.py:333
  396.6 7.5 %collective-permute-start.50 = (bf16[32,2560]{1,0:T(8,128)(2,1)S(1)}, bf16[32,2560]{1,0:T(8,128)(2,1)S(1)}, u32[]{:S(2)}, u32[]{:S(2)}) collective-permute-start(bf16[32,2560]{1,0:T(8,128)(2,1)S(1)} %get-tuple-element.271), channel_id=1, source_target_pairs={{64,0},{96,32},{65,1},{97,33},{66,2},{98,34},{67,3},{99,35},{68,4}... | collective-permute-start | bytes 491528 | tf_op jit(solution)/shard_map/ppermute | solution.py:333
  410.6 16.7 %collective-permute-start.51 = (bf16[80,2560]{1,0:T(8,128)(2,1)S(1)}, bf16[80,2560]{1,0:T(8,128)(2,1)S(1)}, u32[]{:S(2)}, u32[]{:S(2)}) collective-permute-start(bf16[80,2560]{1,0:T(8,128)(2,1)S(1)} %pack.1), channel_id=1, source_target_pairs={{0,32},{32,0},{64,96},{96,64},{128,160},{160,128},{192,224},{224,1... | collective-permute-start | bytes 1228808 | tf_op jit(solution)/shard_map/ppermute | solution.py:269
  (41 other events, 1265.2 us)
